TPU v7x, 32 devices: a whole 2x2x4 slice. The times are simulated.
32 devices in a mesh: groups: 2 (over y), fsdp: 4 (over z), tp: 2 (over x), dp: 2 (over core).
Axes of the slice: x: 2, y: 2, z: 4, core: 2. Of those that a mesh axis runs over, the one named last changes fastest.
Arguments:
- activations: bfloat16 [5120, 8192], P(('groups', 'fsdp'), ('tp', 'dp')), parts along dimension 0, may hold values from -6 to 6
- grad_out: bfloat16 [5120, 2048], P(('groups', 'fsdp')), parts along dimension 0, may hold values from -6 to 6
- codes: bfloat16 [8192, 2048], P(('tp', 'dp'), 'fsdp'), may hold values from -0.125 to 0.125
- scales: float32 [64, 16], P(('tp', 'dp')), may hold values from 0.5 to 2
- adapter_a: bfloat16 [4, 8192, 128], P('fsdp', ('tp', 'dp')), may hold values from -0.0625 to 0.0625
- adapter_b: bfloat16 [4, 2048, 64], P('fsdp', ('tp', 'dp')), may hold values from -0.1875 to 0.1875
- lengths: int32 [8], P('groups'), parts along dimension 0, may hold values from 160 to 1920, as said below
- slot_job: int32 [4], replicated, may hold values from 0 to 3, each once
Outputs:
- input_gradient: bfloat16 [5120, 8192], P(('groups', 'fsdp'), ('tp', 'dp')), parts along dimension 0
- grad_a: float32 [8, 8192, 128], P(('groups', 'fsdp'), ('tp', 'dp')), parts along dimension 0
- grad_b: float32 [8, 2048, 64], P(('groups', 'fsdp'), ('tp', 'dp')), parts along dimension 0
There are 2 independent parts, one for each index of `groups`. A program takes and returns all parts, laid end to end along the dimension named above; an argument that names none is the same for every part. Nothing has to cross between parts.
Inputs may be any that keep to these rules, and one draw needn't show every extreme that they name: The longest job has exactly 1920 rows and the shortest exactly 160; the lengths sum to 2560. `slot_job`: each job appears in exactly one slot.
All inputs are finite; a program needn't handle non-finite values.
Results may differ from a plain program's by a relative error of at most 0.015.
Values may be sent and summed in bfloat16 or wider, within the bound.
No kernel may reach another device: no remote copies, remote signals or barrier semaphores. Data moves between devices by JAX's collectives and lax.ppermute only.
A program may use at most 128 MiB of HBM per device.

v0:
```python
import jax
import jax.numpy as jnp
from jax import lax
from jax.sharding import PartitionSpec as P

BLOCK = 128


adapter_scale = 2.0


def local(activations, grad_out, codes, scales, adapter_a, adapter_b, lengths, slot_job):
    rows = activations.shape[0]
    width_local = activations.shape[1]
    wide = grad_out.shape[1]
    half = wide // 2
    rank_both = adapter_a.shape[2]
    rank = rank_both // 2
    jobs_total = lengths.shape[0]
    shards = lax.axis_size(("tp", "dp"))
    column = lax.axis_index(("tp", "dp"))
    block_cols = wide // shards
    first = lax.axis_index("fsdp") * rows
    starts = jnp.cumsum(lengths) - lengths
    ends = starts + lengths
    counts = jnp.clip(jnp.minimum(ends, first + rows) - jnp.maximum(starts, first), 0, rows)
    positions = first + jnp.arange(rows, dtype=jnp.int32)
    row_job = jnp.sum((positions[:, None] >= starts[None, :]).astype(jnp.int32), axis=1) - 1
    inverse = jnp.argsort(slot_job)
    scale_cols = jnp.repeat(jnp.repeat(scales, BLOCK, axis=0), BLOCK, axis=1)
    weight = (
        lax.all_gather(codes, "fsdp", axis=1, tiled=True).astype(jnp.float32) * scale_cols
    ).astype(jnp.bfloat16)
    frozen_term = lax.dot_general(
        grad_out, weight, (((1,), (1,)), ((), ())), preferred_element_type=jnp.float32
    )
    g_block = lax.dynamic_slice_in_dim(grad_out, column * block_cols, block_cols, 1)
    key_side = column * block_cols < half
    a_every, b_every = (
        lax.all_gather(adapter_a, "fsdp", axis=0, tiled=True),
        lax.all_gather(adapter_b, "fsdp", axis=0, tiled=True),
    )
    a_job = a_every[inverse]
    b_job = b_every[inverse]
    h_part = lax.ragged_dot(activations, a_job, counts, preferred_element_type=jnp.float32)
    u_block = lax.ragged_dot(g_block, b_job, counts, preferred_element_type=jnp.float32)
    u_part = jnp.concatenate(
        [jnp.where(key_side, u_block, 0.0), jnp.where(key_side, 0.0, u_block)], axis=1
    )
    low_h, low_u = (
        lax.psum(h_part.astype(jnp.bfloat16), ("tp", "dp")).astype(jnp.float32),
        lax.psum(u_part.astype(jnp.bfloat16), ("tp", "dp")).astype(jnp.float32),
    )
    h_narrow = low_h.astype(jnp.bfloat16)
    u_narrow = low_u.astype(jnp.bfloat16)
    adapter_branch = lax.ragged_dot(
        u_narrow, jnp.swapaxes(a_job, 1, 2), counts, preferred_element_type=jnp.float32
    )
    input_gradient = (frozen_term + adapter_scale * adapter_branch).astype(jnp.bfloat16)
    h_side = jnp.where(key_side, h_narrow[:, :rank], h_narrow[:, rank:])
    onehot = (row_job[:, None] == slot_job[None, :]).astype(jnp.bfloat16)
    masked_update = (onehot[:, :, None] * u_narrow[:, None, :]).reshape(
        rows, jobs_total * rank_both
    )
    down_portion = (
        lax.dot_general(
            activations, masked_update, (((0,), (0,)), ((), ())), preferred_element_type=jnp.float32
        )
        * adapter_scale
    )
    masked_h = (onehot[:, :, None] * h_side[:, None, :]).reshape(rows, jobs_total * rank)
    up_portion = (
        lax.dot_general(
            g_block, masked_h, (((0,), (0,)), ((), ())), preferred_element_type=jnp.float32
        )
        * adapter_scale
    )
    down_portion = down_portion.reshape(width_local, jobs_total, rank_both)
    up_portion = up_portion.reshape(block_cols, jobs_total, rank)
    summed_a, summed_b = (
        lax.psum_scatter(
            down_portion.astype(jnp.bfloat16), "fsdp", scatter_dimension=1, tiled=True
        ).astype(jnp.float32),
        lax.psum_scatter(
            up_portion.astype(jnp.bfloat16), "fsdp", scatter_dimension=1, tiled=True
        ).astype(jnp.float32),
    )
    grad_a = jnp.transpose(summed_a, (1, 0, 2))
    grad_b = jnp.transpose(summed_b, (1, 0, 2))
    return (input_gradient, grad_a, grad_b)


def solution(mesh):
    in_specs = (
        P(("groups", "fsdp"), ("tp", "dp")),
        P(("groups", "fsdp"), None),
        P(("tp", "dp"), "fsdp"),
        P(("tp", "dp"), None),
        P("fsdp", ("tp", "dp"), None),
        P("fsdp", ("tp", "dp"), None),
        P("groups"),
        P(),
    )
    out_specs = (
        P(("groups", "fsdp"), ("tp", "dp")),
        P(("groups", "fsdp"), ("tp", "dp"), None),
        P(("groups", "fsdp"), ("tp", "dp"), None),
    )
    return jax.shard_map(local, mesh=mesh, in_specs=in_specs, out_specs=out_specs, check_vma=False)
```

profile of v0, /device:TPU:0, one launch (start us, length us, event | category | flops | bytes accessed | tf_op | source)
XLA Modules:
  0.0 354.1 jit_solution(680141456205707387)
XLA Ops:
  7.2 0.7 all-gather.5.cloned.1.call-update
  8.0 0.8 reduce-window.9
  8.8 1.2 fusion.10
  10.0 1.4 ragged-dot-metadata
  11.4 1.4 sort.17
  12.8 17.3 %all_gather.10 = bf16[4,512,64]{1,2,0:T(8,128)(2,1)S(1)} all-gather(bf16[1,512,64]{1,2,0:T(8,128)(2,1)} %param.13), channel_id=1, replica_groups=mesh['groups'=2,'fsdp'=4,'tp'=2,'dp'=2] {'fsdp'}, dimensions={0}, use_global_device_ids=true | all-gather | bytes 327680 | tf_op jit(solution)/shard_map/all_gather | solution.py:41
  30.0 0.6 gather_fusion
  30.6 1.0 copy.27
  31.6 0.9 constant_dynamic-slice_fusion
  32.5 6.0 %ragged-dot-none.2 = f32[640,64]{1,0:T(8,128)} custom-call(s32[1]{0:T(128)} %get-tuple-element.9, s32[5]{0:T(128)} %get-tuple-element.10, s32[8]{0:T(128)} %get-tuple-element.11, s32[8]{0:T(128)} %get-tuple-element.12, s32[1]{0:T(128)} %get-tuple-element.9, bf16[640,512]{1,0:T(8,128)(2,1)} %constant_dynamic-slice_fusion, bf16[4,512,64]{2,1,0:T(8,128)(2,1)} %copy.27), custom_call_target="tpu_custom_call" | custom-call | flops 41943040 | bytes 1081360 | tf_op jit(solution)/shard_map/ragged_dot_general/ragged-dot-none
  38.6 1.0 select_convert_fusion.1
  39.6 0.8 pad_maximum_fusion
  40.4 19.8 %all-gather.5.cloned.1.call-done = bf16[4,2048,128]{2,1,0:T(8,128)(2,1)} async-done(((bf16[1,2048,128]{2,1,0:T(8,128)(2,1)}), bf16[4,2048,128]{2,1,0:T(8,128)(2,1)}) %all-gather.5.cloned.1.call-update) | async-done | bytes 2097168 | tf_op jit(solution)/shard_map/all_gather | solution.py:40
  60.2 3.7 %gather_fusion.1 = bf16[4,2048,128]{2,1,0:T(8,128)(2,1)} fusion(bf16[4,2048,128]{2,1,0:T(8,128)(2,1)} %all-gather.5.cloned.1.call-done, s32[1024]{0:T(1024)S(1)} %pad_clamp_fusion), kind=kCustom, calls=%fused_computation.1 | custom fusion | bytes 4194320 | tf_op jit(solution)/shard_map/gather | solution.py:43
  63.9 6.9 %ragged-dot-none = f32[640,128]{1,0:T(8,128)} custom-call(s32[1]{0:T(128)} %get-tuple-element.9, s32[5]{0:T(128)} %get-tuple-element.10, s32[8]{0:T(128)} %get-tuple-element.11, s32[8]{0:T(128)} %get-tuple-element.12, s32[1]{0:T(128)} %get-tuple-element.9, bf16[640,2048]{1,0:T(8,128)(2,1)} %param.8, bf16[4,2048,128]{2,1,0:T(8,128)(2,1)} %gather_fusion.1), custom_call_target="tpu_custom_call" | custom-call | flops 335544320 | bytes 5046288 | tf_op jit(solution)/shard_map/ragged_dot_general/ragged-dot-none
  70.9 1.6 convert_element_type.52
  72.7 0.8 copy.29
  73.5 31.4 %all-reduce.3.cloned.1.call-done = (bf16[640,128]{1,0:T(8,128)(2,1)}, bf16[640,128]{1,0:T(8,128)(2,1)}) async-done(((bf16[640,128]{1,0:T(8,128)(2,1)}, bf16[640,128]{1,0:T(8,128)(2,1)}), (bf16[640,128]{1,0:T(8,128)(2,1)}, bf16[640,128]{1,0:T(8,128)(2,1)})) %all-reduce.3.cloned.1.call-update) | async-done | bytes 327696 | tf_op jit(solution)/shard_map/psum | solution.py:52
  105.0 1.1 slice_select_fusion
  106.3 1.1 fusion.6
  107.4 1.8 broadcast_multiply_fusion
  109.2 4.9 %multiply_convert_fusion = bf16[512,2048]{1,0:T(8,128)(2,1)} fusion(bf16[640,2048]{1,0:T(8,128)(2,1)} %param.8, bf16[80,8,4,128]{3,2,1,0:T(4,128)(2,1)S(1)} %bitcast.48), kind=kOutput, calls=%fused_computation.7 | convolution fusion | flops 1344274432 | bytes 5373952 | tf_op jit(solution)/shard_map/dot_general | solution.py:66
  114.1 3.9 %copy.30 = bf16[2048,4,128]{2,0,1:T(8,128)(2,1)} copy(bf16[2048,4,128]{0,2,1:T(8,128)(2,1)} %bitcast.44) | data formatting | bytes 4194304 | tf_op jit(solution)/shard_map/convert_element_type | solution.py:82
  118.1 0.5 all-gather.3.cloned.1.call-update
  118.6 4.0 %copy.28 = bf16[4,128,2048]{2,1,0:T(8,128)(2,1)} copy(bf16[4,128,2048]{1,2,0:T(8,128)(2,1)} %bitcast.42) | data formatting | bytes 4194304 | tf_op jit(solution)/shard_map/transpose | solution.py:57
  122.7 6.9 %ragged-dot-none.1 = f32[640,2048]{1,0:T(8,128)} custom-call(s32[1]{0:T(128)} %get-tuple-element.9, s32[5]{0:T(128)} %get-tuple-element.10, s32[8]{0:T(128)} %get-tuple-element.11, s32[8]{0:T(128)} %get-tuple-element.12, s32[1]{0:T(128)} %get-tuple-element.9, bf16[640,128]{1,0:T(8,128)(2,1)} %get-tuple-element.17, bf16[4,128,2048]{2,1,0:T(8,128)(2,1)} %copy.28), custom_call_target="tpu_custom_call" | custom-call | flops 335544320 | bytes 7503888 | tf_op jit(solution)/shard_map/ragged_dot_general/ragged-dot-none
  129.6 1.5 bitcast_convert_fusion.1
  131.1 40.7 %reduce-scatter.3.cloned.1.call-done = bf16[2048,1,128]{2,0,1:T(8,128)(2,1)} async-done(((bf16[2048,4,128]{2,0,1:T(8,128)(2,1)}), bf16[2048,1,128]{2,0,1:T(8,128)(2,1)}) %reduce-scatter.3.cloned.1.call-update) | async-done | bytes 524304 | tf_op jit(solution)/shard_map/reduce_scatter | solution.py:81
  171.9 2.1 bitcast_convert_fusion
  173.9 148.3 %all-gather.3.cloned.1.call-done = bf16[2048,2048]{1,0:T(8,128)(2,1)} async-done(((bf16[2048,512]{1,0:T(8,128)(2,1)}), bf16[2048,2048]{1,0:T(8,128)(2,1)}) %all-gather.3.cloned.1.call-update) | async-done | bytes 8388624 | tf_op jit(solution)/shard_map/all_gather | solution.py:32
  322.4 9.0 %broadcast_in_dim.13 = f32[2048,16,128]{2,1,0:T(8,128)} broadcast(f32[2048,16]{1,0:T(8,128)S(1)} %bitcast.47), dimensions={0,1} | broadcast | bytes 16908288 | tf_op jit(solution)/shard_map/broadcast_in_dim | solution.py:30
  331.4 16.1 %fusion.3 = bf16[640,2048]{1,0:T(8,128)(2,1)} fusion(f32[640,2048]{1,0:T(8,128)S(1)} %bitcast.46, bf16[640,2048]{1,0:T(8,128)(2,1)S(1)} %copy-done, f32[256,8,16,128]{3,2,1,0:T(8,128)} %bitcast.43, bf16[2048,2048]{1,0:T(8,128)(2,1)} %all-gather.3.cloned.1.call-done), kind=kOutput, calls=%fused_computation.6 | convolution fusion | flops 5385224192 | bytes 35651584 | tf_op jit(solution)/shard_map/dot_general | solution.py:34
  (32 shorter events, 0.7 us)
Async XLA Ops:
  7.2 24.5 %copy-start = (bf16[640,2048]{1,0:T(8,128)(2,1)S(1)}, bf16[640,2048]{1,0:T(8,128)(2,1)}, u32[]{:S(2)}) copy-start(bf16[640,2048]{1,0:T(8,128)(2,1)} %param.9) | copy-start | bytes 7864324
  7.2 53.0 %all-gather.5.cloned.1.call-start = ((), (), s32[]{:S(2)}) async-start(), calls=%async_computation.3 | async-start | bytes 2621440 | tf_op jit(solution)/shard_map/all_gather | solution.py:40
  7.9 97.0 %all-reduce.3.cloned.1.call-start = ((), (), s32[]{:S(2)}) async-start(), calls=%async_computation.6 | async-start | bytes 655360 | tf_op jit(solution)/shard_map/psum | solution.py:52
  63.9 8.7 %copy-start.3 = (s32[4]{0:T(128)S(1)}, s32[4]{0:T(128)}, u32[]{:S(2)}) copy-start(s32[4]{0:T(128)} %param.15) | copy-start | bytes 52
  63.9 42.3 %copy-start.1 = (bf16[640,512]{1,0:T(8,128)(2,1)S(1)}, bf16[640,512]{1,0:T(8,128)(2,1)}, u32[]{:S(2)}) copy-start(bf16[640,512]{1,0:T(8,128)(2,1)} %constant_dynamic-slice_fusion) | copy-start | bytes 1966084
  72.6 57.1 %reduce-scatter.5.cloned.1.call-start = ((), (), s32[]{:S(2)}) async-start(), calls=%async_computation.5 | async-start | bytes 327680 | tf_op jit(solution)/shard_map/reduce_scatter | solution.py:84
  107.4 64.5 %reduce-scatter.3.cloned.1.call-start = ((), (), s32[]{:S(2)}) async-start(), calls=%async_computation.4 | async-start | bytes 2621440 | tf_op jit(solution)/shard_map/reduce_scatter | solution.py:81
  118.0 204.2 %all-gather.3.cloned.1.call-start = ((), (), s32[]{:S(2)}) async-start(), calls=%async_computation.2 | async-start | bytes 10485760 | tf_op jit(solution)/shard_map/all_gather | solution.py:32
  122.7 199.6 %copy-start.2 = (f32[16,16]{1,0:T(8,128)S(1)}, f32[16,16]{1,0:T(8,128)}, u32[]{:S(2)}) copy-start(f32[16,16]{1,0:T(8,128)} %param.11) | copy-start | bytes 3076
  322.3 9.1 %slice-start = ((s8[5242880]{0:T(1024)(128)(4,1)}), s8[4194304]{0:T(1024)(128)(4,1)S(1)}, s32[]{:S(2)}) async-start(s8[5242880]{0:T(1024)(128)(4,1)} %bitcast.45), calls=%async_computation.7 | async-start | bytes 8388608
  322.4 9.0 %slice-start.1 = ((s8[5242880]{0:T(1024)(128)(4,1)}), s8[1048576]{0:T(1024)(128)(4,1)S(1)}, s32[]{:S(2)}) async-start(s8[5242880]{0:T(1024)(128)(4,1)} %bitcast.45), calls=%async_computation.8 | async-start | bytes 2097152
Sparse Core Ops, SparseCore 0:
  9.6 50.5 all-gather.4
  72.7 32.2 all-reduce.2
  107.8 19.6 reduce-scatter.4
  129.7 42.0 reduce-scatter.2
  173.3 148.9 all-gather.2
where the time goes:
time: 355 us; the launch traced here: 354 us
  waiting for transfers between devices  242 us (68%)
  local copies, waits for them, and re-layouts  24.2 us (7%)
  matrix products  22.1 us (6%)
  Pallas kernels  21.2 us (6%)
  blocking collectives  17.3 us (5%)
  between operations  13.9 us (4%)
  other arithmetic  13.5 us (4%)
    all_gather x1, waiting for transfers between devices, local(): lax.all_gather(codes, 'fsdp', axis=1, tiled=True).astype(jnp.float32)  148 us
    reduce_scatter x1, waiting for transfers between devices, local(): lax.psum_scatter(down_portion.astype(jnp.bfloat16), 'fsdp', scatter_dimen...  40.7 us
    psum x1, waiting for transfers between devices, local(): lax.psum(u_part.astype(jnp.bfloat16), ('tp', 'dp')).astype(jnp.float32)  31.4 us
    another operation x3, Pallas kernels  19.9 us
    all_gather x1, waiting for transfers between devices, local(): lax.all_gather(adapter_a, 'fsdp', axis=0, tiled=True)  19.8 us
    all_gather x1, blocking collectives, local(): lax.all_gather(adapter_b, 'fsdp', axis=0, tiled=True)  17.3 us
    dot_general x1, matrix products, local(): lax.dot_general(grad_out, weight, (((1,), (1,)), ((), ())), preferred_ele...  16.1 us
    broadcast_in_dim x2, local copies, waits for them, and re-layouts, local(): scale_cols = jnp.repeat(jnp.repeat(scales, BLOCK, axis=0), BLOCK, axis=1)  9.1 us
  transfers between devices with their start and end apart: 5, of which 4 were waited for; matrix products, arithmetic and copies ran while one was open for 8% of the time, Pallas kernels for 4%

commit v1 on v0

v1 whole, which is shorter than its diff:
```python
import functools
import jax
import jax.numpy as jnp
from jax import lax
from jax.experimental import pallas as pl
from jax.experimental.pallas import tpu as pltpu
from jax.sharding import PartitionSpec as P

BLOCK = 128
CHUNKS = 2

adapter_scale = 2.0

ANY = pl.BlockSpec(memory_space=pl.ANY)
SMEM = pl.BlockSpec(memory_space=pltpu.SMEM)
VMEM = pl.BlockSpec(memory_space=pltpu.VMEM)
VMEM_LIMIT = 48 * 1024 * 1024


def swap_pairs(size):
    return [(k, (k + 1) % size) for k in range(size)]


def spread(x, n):
    from_left = lax.ppermute(x, "fsdp", [(k, k + 1) for k in range(n - 1)])
    from_right = lax.ppermute(x, "fsdp", [(k + 1, k) for k in range(n - 1)])
    across = lax.ppermute(x, "fsdp", [(k, (k + 2) % n) for k in range(n)])
    ends = lax.ppermute(across, "fsdp", [(1, 0), (n - 2, n - 1)])
    return from_left, from_right, across, ends


def swap_groups(blocks, n):
    holders = (range(1, n), range(0, n - 1), range(n), (0, n - 1))
    return tuple(
        lax.ppermute(block, ("groups", "fsdp"), [(g * n + k, (1 - g) * n + k) for g in range(2) for k in held])
        for block, held in zip(blocks, holders)
    )


def chain_scatter(terms, f, n):
    total = lax.dynamic_index_in_dim(terms, f, 0, keepdims=False).astype(jnp.float32)
    leftward = rightward = None
    for t in range(1, n):
        x = lax.dynamic_index_in_dim(terms, jnp.clip(f - n + t, 0, n - 1), 0, keepdims=False)
        x = x if leftward is None else x + leftward
        leftward = lax.ppermute(x, "fsdp", [(k, k - 1) for k in range(n - t, n)])
        y = lax.dynamic_index_in_dim(terms, jnp.clip(f + n - t, 0, n - 1), 0, keepdims=False)
        y = y if rightward is None else y + rightward
        rightward = lax.ppermute(y, "fsdp", [(k, k + 1) for k in range(t)])
    return total + leftward.astype(jnp.float32) + rightward.astype(jnp.float32)


def pick(slot, f, n, own, blocks, act):
    from_left, from_right, across, ends = blocks
    pl.when(f == slot)(lambda: act(own))
    pl.when(lax.rem(f + 2, n) == slot)(lambda: act(across))
    if slot == n - 1:
        pl.when(f == 0)(lambda: act(ends))
    if slot == 0:
        pl.when(f == n - 1)(lambda: act(ends))
    if slot < n - 1:
        pl.when(f == slot + 1)(lambda: act(from_left))
    if slot > 0:
        pl.when(f == slot - 1)(lambda: act(from_right))


def slot_bounds(slot, lengths, slot_job, first):
    job = slot_job[slot]
    start = jnp.int32(0)
    for j in range(lengths.shape[0]):
        start = start + jnp.where(j < job, lengths[j], 0)
    return start - first, start - first + lengths[job]


def row_mask(slot, lengths, slot_job, first, shape):
    low, high = slot_bounds(slot, lengths, slot_job, first)
    row = lax.broadcasted_iota(jnp.int32, shape, 0)
    return (row >= low) & (row < high)


NT = (((1,), (1,)), ((), ()))
TN = (((0,), (0,)), ((), ()))


def u_kernel(n, ids, lengths, slot_job, grad, own, *refs):
    blocks, (out, g_all, b_all, sems) = refs[:4], refs[4:]
    f, column = ids[0], ids[2]
    rows, cols = g_all.shape
    rank = out.shape[1]
    grab = pltpu.make_async_copy(grad.at[:, pl.ds(pl.multiple_of(column * cols, cols), cols)], g_all, sems.at[n])
    grab.start()
    for s in range(n):
        pick(s, f, n, own, blocks, lambda ref, s=s: pltpu.make_async_copy(ref, b_all.at[pl.ds(s * rank, rank)], sems.at[s]).start())
    for s in range(n):
        pltpu.make_async_copy(own, b_all.at[pl.ds(s * rank, rank)], sems.at[s]).wait()
    grab.wait()
    total = jnp.zeros(out.shape, jnp.float32)
    for s in range(n):
        part = lax.dot_general(g_all[...], b_all[s * rank:(s + 1) * rank, :], NT, preferred_element_type=jnp.float32)
        total = jnp.where(row_mask(s, lengths, slot_job, f * rows, out.shape), part, total)
    out[...] = total


def h_kernel(n, ids, lengths, slot_job, acts, own, *refs):
    blocks, swapped, (out, a_out, a_all, sems, out_sem) = refs[:4], refs[4:8], refs[8:]
    f, g = ids[0], ids[1]
    rows = acts.shape[0]
    half = blocks[0].shape[0]
    both = out.shape[1]
    for s in range(n):
        for side, held in enumerate((blocks, swapped)):
            first = pl.multiple_of(jnp.where(side == 0, g, 1 - g) * half, half)
            dst = a_all.at[pl.ds(first, half), pl.ds(s * both, both)]
            pick(s, f, n, own.at[pl.ds(first, half)], held, lambda ref, dst=dst, s=s, side=side: pltpu.make_async_copy(ref, dst, sems.at[s, side]).start())
    for s in range(n):
        for side in range(2):
            dst = a_all.at[pl.ds(0, half), pl.ds(s * both, both)]
            pltpu.make_async_copy(blocks[0], dst, sems.at[s, side]).wait()
    keep = pltpu.make_async_copy(a_all, a_out, out_sem)
    keep.start()
    product = jnp.dot(acts[...], a_all[...], preferred_element_type=jnp.float32)
    total = jnp.zeros(out.shape, jnp.float32)
    for s in range(n):
        total = jnp.where(row_mask(s, lengths, slot_job, f * rows, out.shape), product[:, s * both:(s + 1) * both], total)
    out[...] = total
    keep.wait()


def terms_a_kernel(n, ids, lengths, slot_job, acts, low_u, out, masked):
    f = ids[0]
    rows, both = low_u.shape
    doubled = low_u[...].astype(jnp.float32) * adapter_scale
    for s in range(n):
        part = jnp.where(row_mask(s, lengths, slot_job, f * rows, low_u.shape), doubled, 0.0).astype(jnp.bfloat16)
        masked[:, s * both:(s + 1) * both] = part
        out[s] = lax.dot_general(acts[...], part, TN, preferred_element_type=jnp.float32).astype(jnp.bfloat16)


def terms_b_kernel(n, ids, lengths, slot_job, grad, h_side, out, g_all, sem):
    f, column = ids[0], ids[2]
    rows, cols = g_all.shape
    grab = pltpu.make_async_copy(grad.at[:, pl.ds(pl.multiple_of(column * cols, cols), cols)], g_all, sem)
    grab.start()
    doubled = h_side[...].astype(jnp.float32) * adapter_scale
    grab.wait()
    for s in range(n):
        part = jnp.where(row_mask(s, lengths, slot_job, f * rows, h_side.shape), doubled, 0.0).astype(jnp.bfloat16)
        out[s] = lax.dot_general(part, g_all[...], TN, preferred_element_type=jnp.float32).astype(jnp.bfloat16)


def base_kernel(n, chunk, ids, grad, masked, scale_rows, a_all, own, *refs):
    blocks, swapped = refs[:4], refs[4:8]
    out, codes, factors, result, sems, a_sems, out_sems = refs[-7:]
    f, g = ids[0], ids[1]
    size, cols = blocks[0].shape
    half = own.shape[0] // 2
    firsts = []
    for side, held in enumerate((blocks, swapped)):
        first = pl.multiple_of(jnp.where(side == 0, g, 1 - g) * half + chunk * size, size)
        firsts.append(first)
        for s in range(n):
            dst = codes.at[side, :, pl.ds(s * cols, cols)]
            pick(s, f, n, own.at[pl.ds(first, size)], held, lambda ref, dst=dst, s=s, side=side: pltpu.make_async_copy(ref, dst, sems.at[side, s]).start())
        pltpu.make_async_copy(a_all.at[pl.ds(first, size)], factors.at[side], a_sems.at[side]).start()
    for side in range(2):
        first = firsts[side]
        for s in range(n):
            pltpu.make_async_copy(blocks[0], codes.at[side, :, pl.ds(s * cols, cols)], sems.at[side, s]).wait()
        pltpu.make_async_copy(a_all.at[pl.ds(first, size)], factors.at[side], a_sems.at[side]).wait()
        weight = []
        for b in range(size // BLOCK):
            scale = scale_rows[pl.ds(first // BLOCK + b, 1), :]
            weight.append((codes[side, b * BLOCK:(b + 1) * BLOCK, :].astype(jnp.float32) * scale).astype(jnp.bfloat16))
        weight = jnp.concatenate(weight, axis=0)
        total = lax.dot_general(grad[...], weight, NT, preferred_element_type=jnp.float32)
        total += lax.dot_general(masked[...], factors[side], NT, preferred_element_type=jnp.float32)
        result[side] = total.astype(jnp.bfloat16)
        pltpu.make_async_copy(result.at[side], out.at[:, pl.ds(first, size)], out_sems.at[side]).start()
    for side in range(2):
        pltpu.make_async_copy(result.at[side], out.at[:, pl.ds(firsts[side], size)], out_sems.at[side]).wait()


def params():
    return pltpu.CompilerParams(vmem_limit_bytes=VMEM_LIMIT)


def cost(flops, moved):
    return pl.CostEstimate(flops=int(flops), bytes_accessed=int(moved), transcendentals=0)


def local_chain(activations, grad_out, codes, scales, adapter_a, adapter_b, lengths, slot_job):
    n = 4
    rows, width = activations.shape
    wide = grad_out.shape[1]
    both = adapter_a.shape[2]
    rank = both // 2
    cols = codes.shape[1]
    block_cols = adapter_b.shape[1]
    half = width // 2
    f, g = lax.axis_index("fsdp"), lax.axis_index("groups")
    tp, dp = lax.axis_index("tp"), lax.axis_index("dp")
    ids = jnp.stack([f, g, tp * 2 + dp]).astype(jnp.int32)
    a_own = adapter_a[0]
    b_own = adapter_b[0].T

    b_blocks = spread(b_own, n)
    a_half = lax.dynamic_slice_in_dim(a_own, g * half, half, 0)
    a_blocks = spread(a_half, n)
    a_swapped = swap_groups(a_blocks, n)
    size = half // CHUNKS
    code_blocks, code_swapped = [], []
    for c in range(CHUNKS):
        piece = lax.dynamic_slice_in_dim(codes, g * half + c * size, size, 0)
        got = spread(piece, n)
        code_blocks.append(got)
        code_swapped.append(swap_groups(got, n))

    u_part = pl.pallas_call(
        functools.partial(u_kernel, n),
        out_shape=jax.ShapeDtypeStruct((rows, rank), jnp.float32),
        in_specs=[SMEM] * 3 + [ANY] * 6,
        out_specs=VMEM,
        scratch_shapes=[
            pltpu.VMEM((rows, block_cols), jnp.bfloat16),
            pltpu.VMEM((n * rank, block_cols), jnp.bfloat16),
            pltpu.SemaphoreType.DMA((n + 1,)),
        ],
        compiler_params=params(),
        cost_estimate=cost(2 * rows * block_cols * n * rank, rows * block_cols * 2),
        name="low_u",
    )(ids, lengths, slot_job, grad_out, b_own, *b_blocks)
    u_own = (u_part + lax.ppermute(u_part, "dp", swap_pairs(2))).astype(jnp.bfloat16)
    u_far = lax.ppermute(u_own, "tp", swap_pairs(2))
    low_u = jnp.where(tp == 0, jnp.concatenate([u_own, u_far], axis=1), jnp.concatenate([u_far, u_own], axis=1))

    terms_a, masked_u = pl.pallas_call(
        functools.partial(terms_a_kernel, n),
        out_shape=(
            jax.ShapeDtypeStruct((n, width, both), jnp.bfloat16),
            jax.ShapeDtypeStruct((rows, n * both), jnp.bfloat16),
        ),
        in_specs=[SMEM] * 3 + [VMEM] * 2,
        out_specs=(VMEM, VMEM),
        compiler_params=params(),
        cost_estimate=cost(2 * rows * width * n * both, rows * width * 2 + n * width * both * 2),
        name="terms_a",
    )(ids, lengths, slot_job, activations, low_u)
    grad_a = chain_scatter(terms_a, f, n)

    h_part, a_all = pl.pallas_call(
        functools.partial(h_kernel, n),
        out_shape=(
            jax.ShapeDtypeStruct((rows, both), jnp.float32),
            jax.ShapeDtypeStruct((width, n * both), jnp.bfloat16),
        ),
        in_specs=[SMEM] * 3 + [VMEM] + [ANY] * 9,
        out_specs=(VMEM, ANY),
        scratch_shapes=[
            pltpu.VMEM((width, n * both), jnp.bfloat16),
            pltpu.SemaphoreType.DMA((n, 2)),
            pltpu.SemaphoreType.DMA,
        ],
        compiler_params=params(),
        cost_estimate=cost(2 * rows * width * n * both, rows * width * 2 + n * width * both * 4),
        name="low_h",
    )(ids, lengths, slot_job, activations, a_own, *a_blocks, *a_swapped)
    h_core = (h_part + lax.ppermute(h_part, "dp", swap_pairs(2))).astype(jnp.bfloat16)
    low_h = h_core + lax.ppermute(h_core, "tp", swap_pairs(2))
    h_side = jnp.where(tp == 0, low_h[:, :rank], low_h[:, rank:])
    terms_b = pl.pallas_call(
        functools.partial(terms_b_kernel, n),
        out_shape=jax.ShapeDtypeStruct((n, rank, block_cols), jnp.bfloat16),
        in_specs=[SMEM] * 3 + [ANY, VMEM],
        out_specs=VMEM,
        scratch_shapes=[pltpu.VMEM((rows, block_cols), jnp.bfloat16), pltpu.SemaphoreType.DMA],
        compiler_params=params(),
        cost_estimate=cost(2 * rows * block_cols * n * rank, rows * block_cols * 2),
        name="terms_b",
    )(ids, lengths, slot_job, grad_out, h_side)
    grad_b = chain_scatter(terms_b, f, n)

    scale_rows = jnp.repeat(scales, BLOCK, axis=1)
    result = None
    for c in range(CHUNKS):
        more = [] if result is None else [result]
        result = pl.pallas_call(
            functools.partial(base_kernel, n, c),
            out_shape=jax.ShapeDtypeStruct((rows, width), jnp.bfloat16),
            in_specs=[SMEM] + [VMEM] * 3 + [ANY] * (10 + len(more)),
            out_specs=ANY,
            scratch_shapes=[
                pltpu.VMEM((2, size, wide), jnp.bfloat16),
                pltpu.VMEM((2, size, n * both), jnp.bfloat16),
                pltpu.VMEM((2, rows, size), jnp.bfloat16),
                pltpu.SemaphoreType.DMA((2, n)),
                pltpu.SemaphoreType.DMA((2,)),
                pltpu.SemaphoreType.DMA((2,)),
            ],
            input_output_aliases={14: 0} if more else {},
            compiler_params=params(),
            cost_estimate=cost(2 * rows * 2 * size * (wide + n * both), 2 * size * wide * 2 + rows * wide * 2),
            name="base",
        )(ids, grad_out, masked_u, scale_rows, a_all, codes, *code_blocks[c], *code_swapped[c], *more)
    return result, grad_a[None], grad_b.T[None]


def local_any(activations, grad_out, codes, scales, adapter_a, adapter_b, lengths, slot_job):
    rows = activations.shape[0]
    width = activations.shape[1]
    wide = grad_out.shape[1]
    half = wide // 2
    both = adapter_a.shape[2]
    rank = both // 2
    jobs = lengths.shape[0]
    shards = lax.axis_size(("tp", "dp"))
    column = lax.axis_index(("tp", "dp"))
    block_cols = wide // shards
    first = lax.axis_index("fsdp") * rows
    starts = jnp.cumsum(lengths) - lengths
    positions = first + jnp.arange(rows, dtype=jnp.int32)
    row_job = jnp.sum((positions[:, None] >= starts[None, :]).astype(jnp.int32), axis=1) - 1
    onehot = row_job[:, None] == slot_job[None, :]
    scale_cols = jnp.repeat(jnp.repeat(scales, BLOCK, axis=0), BLOCK, axis=1)
    weight = (lax.all_gather(codes, "fsdp", axis=1, tiled=True).astype(jnp.float32) * scale_cols).astype(jnp.bfloat16)
    frozen = lax.dot_general(grad_out, weight, NT, preferred_element_type=jnp.float32)
    g_block = lax.dynamic_slice_in_dim(grad_out, column * block_cols, block_cols, 1)
    key_side = column * block_cols < half
    a_every = lax.all_gather(adapter_a, "fsdp", axis=0, tiled=True)
    b_every = lax.all_gather(adapter_b, "fsdp", axis=0, tiled=True)
    h_every = jnp.einsum("ri,sic->rsc", activations, a_every, preferred_element_type=jnp.float32)
    u_every = jnp.einsum("ro,sok->rsk", g_block, b_every, preferred_element_type=jnp.float32)
    h_part = jnp.sum(jnp.where(onehot[:, :, None], h_every, 0.0), axis=1)
    u_block = jnp.sum(jnp.where(onehot[:, :, None], u_every, 0.0), axis=1)
    u_part = jnp.concatenate([jnp.where(key_side, u_block, 0.0), jnp.where(key_side, 0.0, u_block)], axis=1)
    low_h = lax.psum(h_part.astype(jnp.bfloat16), ("tp", "dp"))
    low_u = lax.psum(u_part.astype(jnp.bfloat16), ("tp", "dp"))
    masked_u = jnp.where(onehot[:, :, None], low_u[:, None, :], 0).reshape(rows, jobs * both)
    branch = jnp.einsum("rsc,sic->ri", masked_u.reshape(rows, jobs, both), a_every, preferred_element_type=jnp.float32)
    input_gradient = (frozen + adapter_scale * branch).astype(jnp.bfloat16)
    h_side = jnp.where(key_side, low_h[:, :rank], low_h[:, rank:])
    masked_h = jnp.where(onehot[:, :, None], h_side[:, None, :], 0).reshape(rows, jobs * rank)
    down = lax.dot_general(activations, masked_u, TN, preferred_element_type=jnp.float32) * adapter_scale
    up = lax.dot_general(g_block, masked_h, TN, preferred_element_type=jnp.float32) * adapter_scale
    down = down.reshape(width, jobs, both).astype(jnp.bfloat16)
    up = up.reshape(block_cols, jobs, rank).astype(jnp.bfloat16)
    summed_a = lax.psum_scatter(down, "fsdp", scatter_dimension=1, tiled=True).astype(jnp.float32)
    summed_b = lax.psum_scatter(up, "fsdp", scatter_dimension=1, tiled=True).astype(jnp.float32)
    return input_gradient, jnp.transpose(summed_a, (1, 0, 2)), jnp.transpose(summed_b, (1, 0, 2))


def solution(mesh):
    in_specs = (
        P(("groups", "fsdp"), ("tp", "dp")),
        P(("groups", "fsdp"), None),
        P(("tp", "dp"), "fsdp"),
        P(("tp", "dp"), None),
        P("fsdp", ("tp", "dp"), None),
        P("fsdp", ("tp", "dp"), None),
        P("groups"),
        P(),
    )
    out_specs = (
        P(("groups", "fsdp"), ("tp", "dp")),
        P(("groups", "fsdp"), ("tp", "dp"), None),
        P(("groups", "fsdp"), ("tp", "dp"), None),
    )
    shape = dict(mesh.shape)
    chain = shape == {"groups": 2, "fsdp": 4, "tp": 2, "dp": 2}
    local = local_chain if chain else local_any
    return jax.shard_map(local, mesh=mesh, in_specs=in_specs, out_specs=out_specs, check_vma=False)
```

time: 355 us -> 248 us (0.70)
  waiting for transfers between devices: 242 us -> 62.1 us
  starting transfers between devices: 0.2 us -> 120 us
  matrix products: 22.1 us -> 0 us
  blocking collectives: 17.3 us -> 0 us
  between operations: 13.9 us -> 1.26 us
  Pallas kernels: 21.2 us -> 28.3 us
  local copies, waits for them, and re-layouts: 24.2 us -> 19.9 us
    all_gather x2 -> x0, waiting for transfers between devices: 168 us -> none  [the longest x1 148 us: local(): lax.all_gather(codes, 'fsdp', axis=1, tiled=True).astype(jnp.float32)]
    ppermute x0 -> x44, starting transfers between devices: none -> 120 us  [the longest x6 53.3 us: chain_scatter(): rightward = lax.ppermute(y, 'fsdp', [(k, k + 1) for k in range(t)])]
    ppermute x0 -> x44, waiting for transfers between devices: none -> 62.1 us  [the longest x4 29.2 us: spread(): across = lax.ppermute(x, 'fsdp', [(k, (k + 2) % n) for k in range(n)])]
    reduce_scatter x2 -> x0, waiting for transfers between devices: 40.7 us -> none  [the longest x1 40.7 us: local(): lax.psum_scatter(down_portion.astype(jnp.bfloat16), 'fsdp', scatter_dimen...]
    psum x1 -> x0, waiting for transfers between devices: 31.4 us -> none  [local(): lax.psum(u_part.astype(jnp.bfloat16), ('tp', 'dp')).astype(jnp.float32)]
    pallas_call x0 -> x6, Pallas kernels: none -> 28.3 us  [the longest x2 16.5 us: local_chain(): pl.pallas_call(functools.partial(base_kernel, n, c), out_shape=jax.ShapeD...]
    dot_general x3 -> x0, matrix products: 22.1 us -> none  [the longest x1 16.1 us: local(): lax.dot_general(grad_out, weight, (((1,), (1,)), ((), ())), preferred_ele...]
    another operation x3 -> x0, Pallas kernels: 19.9 us -> none
  transfers between devices with their start and end apart: 5 -> 44, of which waited for: 4 -> 12; matrix products, arithmetic and copies ran while one was open for 8% -> 7% of each run, Pallas kernels for 4% -> 12%
where the time goes in v1:
time: 248 us; the launch traced here: 246 us
  starting transfers between devices  120 us (48%)
  waiting for transfers between devices  62.1 us (25%)
  Pallas kernels  28.3 us (11%)
  local copies, waits for them, and re-layouts  19.9 us (8%)
  other arithmetic  14.9 us (6%)
    ppermute x6, starting transfers between devices, chain_scatter(): rightward = lax.ppermute(y, 'fsdp', [(k, k + 1) for k in range(t)])  53.3 us
    ppermute x4, waiting for transfers between devices, spread(): across = lax.ppermute(x, 'fsdp', [(k, (k + 2) % n) for k in range(n)])  29.2 us
    ppermute x12, starting transfers between devices, swap_groups(): lax.ppermute(block, ('groups', 'fsdp'), [(g * n + k, (1 - g) * n + k) for...  22.3 us
    ppermute x12, waiting for transfers between devices, swap_groups(): lax.ppermute(block, ('groups', 'fsdp'), [(g * n + k, (1 - g) * n + k) for...  17.5 us
    pallas_call x2, Pallas kernels, local_chain(): pl.pallas_call(functools.partial(base_kernel, n, c), out_shape=jax.ShapeD...  16.5 us
    unnamed x61, local copies, waits for them, and re-layouts  14.8 us
    ppermute x4, starting transfers between devices, spread(): from_left = lax.ppermute(x, 'fsdp', [(k, k + 1) for k in range(n - 1)])  12.2 us
    ppermute x4, starting transfers between devices, spread(): across = lax.ppermute(x, 'fsdp', [(k, (k + 2) % n) for k in range(n)])  10.1 us
  transfers between devices with their start and end apart: 44, of which 12 were waited for; matrix products, arithmetic and copies ran while one was open for 7% of the time, Pallas kernels for 12%

profile of v1, /device:TPU:0, one launch (start us, length us, event | category | flops | bytes accessed | tf_op | source)
XLA Modules:
  0.0 246.0 jit_solution(9405567302664608123)
XLA Ops:
  1.7 4.1 %collective-permute-start.8 = (bf16[1024,128]{1,0:T(8,128)(2,1)S(1)}, bf16[1024,128]{1,0:T(8,128)(2,1)S(1)}, u32[]{:S(2)}, u32[]{:S(2)}) collective-permute-start(bf16[1024,128]{1,0:T(8,128)(2,1)S(1)} %dynamic-slice_bitcast_fusion.2), channel_id=1, source_target_pairs={{0,8},{4,12},{8,0},{12,4},{1,9},{5,13},{9,1},{13,5},{2,10},{6,14},... | collective-permute-start | bytes 786440 | tf_op jit(solution)/shard_map/ppermute | solution.py:27
  5.8 3.5 %collective-permute-start.6 = (bf16[1024,128]{1,0:T(8,128)(2,1)S(1)}, bf16[1024,128]{1,0:T(8,128)(2,1)S(1)}, u32[]{:S(2)}, u32[]{:S(2)}) collective-permute-start(bf16[1024,128]{1,0:T(8,128)(2,1)S(1)} %dynamic-slice_bitcast_fusion.2), channel_id=1, source_target_pairs={{0,4},{4,8},{8,12},{1,5},{5,9},{9,13},{2,6},{6,10},{10,14},{3,7},{... | collective-permute-start | bytes 786440 | tf_op jit(solution)/shard_map/ppermute | solution.py:25
  10.6 8.0 %collective-permute-done.8.refs_2_ = bf16[1024,128]{1,0:T(8,128)(2,1)S(1)} collective-permute-done((bf16[1024,128]{1,0:T(8,128)(2,1)S(1)}, bf16[1024,128]{1,0:T(8,128)(2,1)S(1)}, u32[]{:S(2)}, u32[]{:S(2)}) %collective-permute-start.8) | collective-permute-done | bytes 262176 | tf_op jit(solution)/shard_map/ppermute | solution.py:27
  19.9 4.1 %collective-permute-start.2 = (bf16[64,512]{1,0:T(8,128)(2,1)}, bf16[64,512]{1,0:T(8,128)(2,1)S(1)}, u32[]{:S(2)}, u32[]{:S(2)}) collective-permute-start(bf16[64,512]{1,0:T(8,128)(2,1)} %bitcast.52), channel_id=1, source_target_pairs={{0,8},{4,12},{8,0},{12,4},{1,9},{5,13},{9,1},{13,5},{2,10},{6,14},... | collective-permute-start | bytes 196616 | tf_op jit(solution)/shard_map/ppermute | solution.py:27
  28.9 2.4 collective-permute-start.11
  31.3 3.4 %collective-permute-start.13 = (bf16[1024,128]{1,0:T(8,128)(2,1)S(1)}, bf16[1024,128]{1,0:T(8,128)(2,1)S(1)}, u32[]{:S(2)}, u32[]{:S(2)}) collective-permute-start(bf16[1024,128]{1,0:T(8,128)(2,1)S(1)} %collective-permute-done.9.refs_3_), channel_id=1, source_target_pairs={{0,16},{12,28},{16,0},{28,12},{1,17},{13,29},{17,1},{29,13},{2,18}... | collective-permute-start | bytes 786440 | tf_op jit(solution)/shard_map/ppermute | solution.py:35
  36.1 5.1 %collective-permute-done.1.refs_1_ = bf16[64,512]{1,0:T(8,128)(2,1)S(1)} collective-permute-done((bf16[64,512]{1,0:T(8,128)(2,1)}, bf16[64,512]{1,0:T(8,128)(2,1)S(1)}, u32[]{:S(2)}, u32[]{:S(2)}) %collective-permute-start.1) | collective-permute-done | bytes 65568 | tf_op jit(solution)/shard_map/ppermute | solution.py:26
  42.5 4.8 %collective-permute-done.3.refs_3_ = bf16[64,512]{1,0:T(8,128)(2,1)S(1)} collective-permute-done((bf16[64,512]{1,0:T(8,128)(2,1)S(1)}, bf16[64,512]{1,0:T(8,128)(2,1)S(1)}, u32[]{:S(2)}, u32[]{:S(2)}) %collective-permute-start.3) | collective-permute-done | bytes 65568 | tf_op jit(solution)/shard_map/ppermute | solution.py:28
  47.3 1.7 copy-done
  51.2 1.9 low_u.1
  62.8 4.9 %low_h.1 = (f32[640,128]{1,0:T(8,128)}, bf16[2048,512]{1,0:T(8,128)(2,1)S(1)}) custom-call(s32[3]{0:T(128)S(1)} %pad_add_fusion.ids, s32[4]{0:T(128)S(1)} %copy-done.24, s32[4]{0:T(128)S(1)} %copy-done.26, bf16[640,2048]{1,0:T(8,128)(2,1)} %acts.3, bf16[2048,128]{1,0:T(8,128)(2,1)S(1)} %bitcast.51, bf16[1024,128]{1,0:T(8,128)(2,1)S(1)} %copy-done.10, ...), custom_call_target="tpu_custom_call" | custom-call | flops 1342177280 | bytes 6815744 | tf_op jit(solution)/shard_map/low_h/pallas_call | solution.py:250
  71.1 4.6 %collective-permute-done.5 = bf16[640,64]{1,0:T(8,128)(2,1)S(1)} collective-permute-done((bf16[640,64]{1,0:T(8,128)(2,1)S(1)}, bf16[640,64]{1,0:T(8,128)(2,1)S(1)}, u32[]{:S(2)}, u32[]{:S(2)}) %collective-permute-start.5) | collective-permute-done | bytes 81952 | tf_op jit(solution)/shard_map/ppermute | solution.py:233
  76.0 3.6 %terms_a.1 = (bf16[4,2048,128]{2,1,0:T(8,128)(2,1)S(1)}, bf16[640,512]{1,0:T(8,128)(2,1)S(1)}) custom-call(s32[3]{0:T(128)S(1)} %pad_add_fusion.ids, s32[4]{0:T(128)S(1)} %copy-done.25, s32[4]{0:T(128)S(1)} %copy-done.27, bf16[640,2048]{1,0:T(8,128)(2,1)S(1)} %copy-done.5, bf16[640,128]{1,0:T(8,128)(2,1)S(1)} %maximum_select_fusion.low_u), custom_call_target="tpu_custom_call" | custom-call | flops 1342177280 | bytes 4718592 | tf_op jit(solution)/shard_map/terms_a/pallas_call | solution.py:236
  85.5 2.3 constant_dynamic-slice_fusion
  88.3 6.2 %collective-permute-start.22 = (bf16[512,512]{1,0:T(8,128)(2,1)}, bf16[512,512]{1,0:T(8,128)(2,1)}, u32[]{:S(2)}, u32[]{:S(2)}) collective-permute-start(bf16[512,512]{1,0:T(8,128)(2,1)} %get-tuple-element.15), channel_id=1, source_target_pairs={{0,4},{4,8},{8,12},{1,5},{5,9},{9,13},{2,6},{6,10},{10,14},{3,7},{... | collective-permute-start | bytes 1572872 | tf_op jit(solution)/shard_map/ppermute | solution.py:25
  101.0 2.1 bitcast_add_fusion.2
  103.1 12.0 %collective-permute-done.24.refs_2_ = bf16[512,512]{1,0:T(8,128)(2,1)} collective-permute-done((bf16[512,512]{1,0:T(8,128)(2,1)}, bf16[512,512]{1,0:T(8,128)(2,1)}, u32[]{:S(2)}, u32[]{:S(2)}) %collective-permute-start.24) | collective-permute-done | bytes 524320 | tf_op jit(solution)/shard_map/ppermute | solution.py:27
  116.3 20.6 %collective-permute-start.33 = (bf16[2048,128]{1,0:T(8,128)(2,1)}, bf16[2048,128]{1,0:T(8,128)(2,1)}, u32[]{:S(2)}, u32[]{:S(2)}) collective-permute-start(bf16[2048,128]{1,0:T(8,128)(2,1)} %get-tuple-element.14), channel_id=1, source_target_pairs={{0,4},{1,5},{2,6},{3,7},{16,20},{17,21},{18,22},{19,23}} | collective-permute-start | bytes 1572872 | tf_op jit(solution)/shard_map/ppermute | solution.py:49
  139.0 1.9 collective-permute-start.41
  140.9 7.8 %collective-permute-done.16.refs_2_ = bf16[512,512]{1,0:T(8,128)(2,1)} collective-permute-done((bf16[512,512]{1,0:T(8,128)(2,1)}, bf16[512,512]{1,0:T(8,128)(2,1)}, u32[]{:S(2)}, u32[]{:S(2)}) %collective-permute-start.16) | collective-permute-done | bytes 524320 | tf_op jit(solution)/shard_map/ppermute | solution.py:27
  156.2 15.9 %collective-permute-start.42 = (bf16[64,512]{1,0:T(8,128)(2,1)S(1)}, bf16[64,512]{1,0:T(8,128)(2,1)}, u32[]{:S(2)}, u32[]{:S(2)}) collective-permute-start(bf16[64,512]{1,0:T(8,128)(2,1)S(1)} %get-tuple-element.18), channel_id=1, source_target_pairs={{0,4},{4,8},{1,5},{5,9},{2,6},{6,10},{3,7},{7,11},{16,20},{20,24},... | collective-permute-start | bytes 196616 | tf_op jit(solution)/shard_map/ppermute | solution.py:49
  172.0 2.3 bitcast_add_fusion.3
  174.3 2.4 collective-permute-start.27
  178.0 6.2 %collective-permute-start.34 = (bf16[2048,128]{1,0:T(8,128)(2,1)}, bf16[2048,128]{1,0:T(8,128)(2,1)}, u32[]{:S(2)}, u32[]{:S(2)}) collective-permute-start(bf16[2048,128]{1,0:T(8,128)(2,1)} %get-tuple-element.12), channel_id=1, source_target_pairs={{0,4},{4,8},{1,5},{5,9},{2,6},{6,10},{3,7},{7,11},{16,20},{20,24},... | collective-permute-start | bytes 1572872 | tf_op jit(solution)/shard_map/ppermute | solution.py:49
  187.0 7.5 %collective-permute-start.43 = (bf16[64,512]{1,0:T(8,128)(2,1)}, bf16[64,512]{1,0:T(8,128)(2,1)}, u32[]{:S(2)}, u32[]{:S(2)}) collective-permute-start(bf16[64,512]{1,0:T(8,128)(2,1)} %bitcast_add_fusion.5), channel_id=1, source_target_pairs={{0,4},{4,8},{8,12},{1,5},{5,9},{9,13},{2,6},{6,10},{10,14},{3,7},{... | collective-permute-start | bytes 196616 | tf_op jit(solution)/shard_map/ppermute | solution.py:49
  196.1 2.6 %collective-permute-start.29 = (bf16[512,512]{1,0:T(8,128)(2,1)}, bf16[512,512]{1,0:T(8,128)(2,1)S(1)}, u32[]{:S(2)}, u32[]{:S(2)}) collective-permute-start(bf16[512,512]{1,0:T(8,128)(2,1)} %collective-permute-done.25.refs_3_), channel_id=1, source_target_pairs={{0,16},{12,28},{16,0},{28,12},{1,17},{13,29},{17,1},{29,13},{2,18}... | collective-permute-start | bytes 1572872 | tf_op jit(solution)/shard_map/ppermute | solution.py:35
  201.1 3.2 %collective-permute-start.19 = (bf16[512,512]{1,0:T(8,128)(2,1)}, bf16[512,512]{1,0:T(8,128)(2,1)S(1)}, u32[]{:S(2)}, u32[]{:S(2)}) collective-permute-start(bf16[512,512]{1,0:T(8,128)(2,1)} %collective-permute-done.15.refs_1_), channel_id=1, source_target_pairs={{0,16},{4,20},{8,24},{16,0},{20,4},{24,8},{1,17},{5,21},{9,25},{17... | collective-permute-start | bytes 1572872 | tf_op jit(solution)/shard_map/ppermute | solution.py:35
  204.4 2.6 %collective-permute-start.21 = (bf16[512,512]{1,0:T(8,128)(2,1)}, bf16[512,512]{1,0:T(8,128)(2,1)S(1)}, u32[]{:S(2)}, u32[]{:S(2)}) collective-permute-start(bf16[512,512]{1,0:T(8,128)(2,1)} %collective-permute-done.17.refs_3_), channel_id=1, source_target_pairs={{0,16},{12,28},{16,0},{28,12},{1,17},{13,29},{17,1},{29,13},{2,18}... | collective-permute-start | bytes 1572872 | tf_op jit(solution)/shard_map/ppermute | solution.py:35
  211.1 9.9 %collective-permute-done.29.refs_7_ = bf16[512,512]{1,0:T(8,128)(2,1)S(1)} collective-permute-done((bf16[512,512]{1,0:T(8,128)(2,1)}, bf16[512,512]{1,0:T(8,128)(2,1)S(1)}, u32[]{:S(2)}, u32[]{:S(2)}) %collective-permute-start.29) | collective-permute-done | bytes 524320 | tf_op jit(solution)/shard_map/ppermute | solution.py:35
  222.4 8.4 %base.2.refs_8_ = bf16[640,2048]{1,0:T(8,128)(2,1)} custom-call(s32[3]{0:T(128)S(1)} %pad_add_fusion.ids, bf16[640,2048]{1,0:T(8,128)(2,1)} %grad.7, bf16[640,512]{1,0:T(8,128)(2,1)S(1)} %get-tuple-element.7.masked, f32[16,2048]{1,0:T(8,128)S(1)} %bitcast.49, bf16[2048,512]{1,0:T(8,128)(2,1)} %copy-done.2, bf16[2048,512]{1,0:T(8,128)(2,1)} %own.3, ...), custom_call_target="tpu_custom_call" | custom-call | flops 3355443200 | bytes 6815744 | tf_op jit(solution)/shard_map/base/pallas_call | solution.py:286
  231.0 5.6 %collective-permute-done.21.refs_7_ = bf16[512,512]{1,0:T(8,128)(2,1)S(1)} collective-permute-done((bf16[512,512]{1,0:T(8,128)(2,1)}, bf16[512,512]{1,0:T(8,128)(2,1)S(1)}, u32[]{:S(2)}, u32[]{:S(2)}) %collective-permute-start.21) | collective-permute-done | bytes 524320 | tf_op jit(solution)/shard_map/ppermute | solution.py:35
  236.6 8.2 %base.3 = bf16[640,2048]{1,0:T(8,128)(2,1)} custom-call(s32[3]{0:T(128)S(1)} %pad_add_fusion.ids, bf16[640,2048]{1,0:T(8,128)(2,1)} %grad.7, bf16[640,512]{1,0:T(8,128)(2,1)S(1)} %get-tuple-element.7.masked, f32[16,2048]{1,0:T(8,128)S(1)} %bitcast.50, bf16[2048,512]{1,0:T(8,128)(2,1)} %copy-done.2, ...), custom_call_target="tpu_custom_call", output_to_operand_aliasing={{}: (14, {})} | custom-call | flops 3355443200 | bytes 6815744 | tf_op jit(solution)/shard_map/base/pallas_call | solution.py:286
  (142 shorter events, 65.2 us)
Async XLA Ops:
  1.7 16.9 %collective-permute-start.8 = (bf16[1024,128]{1,0:T(8,128)(2,1)S(1)}, bf16[1024,128]{1,0:T(8,128)(2,1)S(1)}, u32[]{:S(2)}, u32[]{:S(2)}) collective-permute-start(bf16[1024,128]{1,0:T(8,128)(2,1)S(1)} %dynamic-slice_bitcast_fusion.2), channel_id=1, source_target_pairs={{0,8},{4,12},{8,0},{12,4},{1,9},{5,13},{9,1},{13,5},{2,10},{6,14},... | collective-permute-start | bytes 786440 | tf_op jit(solution)/shard_map/ppermute | solution.py:27
  5.8 22.4 %collective-permute-start.6 = (bf16[1024,128]{1,0:T(8,128)(2,1)S(1)}, bf16[1024,128]{1,0:T(8,128)(2,1)S(1)}, u32[]{:S(2)}, u32[]{:S(2)}) collective-permute-start(bf16[1024,128]{1,0:T(8,128)(2,1)S(1)} %dynamic-slice_bitcast_fusion.2), channel_id=1, source_target_pairs={{0,4},{4,8},{8,12},{1,5},{5,9},{9,13},{2,6},{6,10},{10,14},{3,7},{... | collective-permute-start | bytes 786440 | tf_op jit(solution)/shard_map/ppermute | solution.py:25
  9.3 19.6 %collective-permute-start.7 = (bf16[1024,128]{1,0:T(8,128)(2,1)S(1)}, bf16[1024,128]{1,0:T(8,128)(2,1)S(1)}, u32[]{:S(2)}, u32[]{:S(2)}) collective-permute-start(bf16[1024,128]{1,0:T(8,128)(2,1)S(1)} %dynamic-slice_bitcast_fusion.2), channel_id=1, source_target_pairs={{4,0},{8,4},{12,8},{5,1},{9,5},{13,9},{6,2},{10,6},{14,10},{7,3},{... | collective-permute-start | bytes 786440 | tf_op jit(solution)/shard_map/ppermute | solution.py:26
  26.7 26.5 %collective-permute-start.12 = (bf16[1024,128]{1,0:T(8,128)(2,1)S(1)}, bf16[1024,128]{1,0:T(8,128)(2,1)S(1)}, u32[]{:S(2)}, u32[]{:S(2)}) collective-permute-start(bf16[1024,128]{1,0:T(8,128)(2,1)S(1)} %collective-permute-done.8.refs_2_), channel_id=1, source_target_pairs={{0,16},{4,20},{8,24},{12,28},{16,0},{20,4},{24,8},{28,12},{1,17},{... | collective-permute-start | bytes 786440 | tf_op jit(solution)/shard_map/ppermute | solution.py:35
  28.2 25.8 %collective-permute-start.10 = (bf16[1024,128]{1,0:T(8,128)(2,1)S(1)}, bf16[1024,128]{1,0:T(8,128)(2,1)S(1)}, u32[]{:S(2)}, u32[]{:S(2)}) collective-permute-start(bf16[1024,128]{1,0:T(8,128)(2,1)S(1)} %collective-permute-done.6.refs_0_), channel_id=1, source_target_pairs={{4,20},{8,24},{12,28},{20,4},{24,8},{28,12},{5,21},{9,25},{13,29},... | collective-permute-start | bytes 786440 | tf_op jit(solution)/shard_map/ppermute | solution.py:35
  28.9 25.8 %collective-permute-start.11 = (bf16[1024,128]{1,0:T(8,128)(2,1)S(1)}, bf16[1024,128]{1,0:T(8,128)(2,1)S(1)}, u32[]{:S(2)}, u32[]{:S(2)}) collective-permute-start(bf16[1024,128]{1,0:T(8,128)(2,1)S(1)} %collective-permute-done.7.refs_1_), channel_id=1, source_target_pairs={{0,16},{4,20},{8,24},{16,0},{20,4},{24,8},{1,17},{5,21},{9,25},{17... | collective-permute-start | bytes 786440 | tf_op jit(solution)/shard_map/ppermute | solution.py:35
  31.3 24.0 %collective-permute-start.13 = (bf16[1024,128]{1,0:T(8,128)(2,1)S(1)}, bf16[1024,128]{1,0:T(8,128)(2,1)S(1)}, u32[]{:S(2)}, u32[]{:S(2)}) collective-permute-start(bf16[1024,128]{1,0:T(8,128)(2,1)S(1)} %collective-permute-done.9.refs_3_), channel_id=1, source_target_pairs={{0,16},{12,28},{16,0},{28,12},{1,17},{13,29},{17,1},{29,13},{2,18}... | collective-permute-start | bytes 786440 | tf_op jit(solution)/shard_map/ppermute | solution.py:35
  53.1 16.4 %collective-permute-start.4 = (f32[640,64]{1,0:T(8,128)S(1)}, f32[640,64]{1,0:T(8,128)S(1)}, u32[]{:S(2)}, u32[]{:S(2)}) collective-permute-start(f32[640,64]{1,0:T(8,128)S(1)} %low_u.1), channel_id=1, source_target_pairs={{0,1},{1,0},{2,3},{3,2},{4,5},{5,4},{6,7},{7,6},{8,9},{9,8},{10,11... | collective-permute-start | bytes 491528 | tf_op jit(solution)/shard_map/ppermute | solution.py:232
  83.9 16.5 %collective-permute-start.30 = (bf16[2048,128]{1,0:T(8,128)(2,1)}, bf16[2048,128]{1,0:T(8,128)(2,1)}, u32[]{:S(2)}, u32[]{:S(2)}) collective-permute-start(bf16[2048,128]{1,0:T(8,128)(2,1)} %get-tuple-element.13), channel_id=1, source_target_pairs={{12,8},{13,9},{14,10},{15,11},{28,24},{29,25},{30,26},{31,27}} | collective-permute-start | bytes 1572872 | tf_op jit(solution)/shard_map/ppermute | solution.py:46
  87.7 27.3 %collective-permute-start.24 = (bf16[512,512]{1,0:T(8,128)(2,1)}, bf16[512,512]{1,0:T(8,128)(2,1)}, u32[]{:S(2)}, u32[]{:S(2)}) collective-permute-start(bf16[512,512]{1,0:T(8,128)(2,1)} %get-tuple-element.15), channel_id=1, source_target_pairs={{0,8},{4,12},{8,0},{12,4},{1,9},{5,13},{9,1},{13,5},{2,10},{6,14},... | collective-permute-start | bytes 1572872 | tf_op jit(solution)/shard_map/ppermute | solution.py:27
  88.3 28.0 %collective-permute-start.22 = (bf16[512,512]{1,0:T(8,128)(2,1)}, bf16[512,512]{1,0:T(8,128)(2,1)}, u32[]{:S(2)}, u32[]{:S(2)}) collective-permute-start(bf16[512,512]{1,0:T(8,128)(2,1)} %get-tuple-element.15), channel_id=1, source_target_pairs={{0,4},{4,8},{8,12},{1,5},{5,9},{9,13},{2,6},{6,10},{10,14},{3,7},{... | collective-permute-start | bytes 1572872 | tf_op jit(solution)/shard_map/ppermute | solution.py:25
  94.5 44.6 %collective-permute-start.23 = (bf16[512,512]{1,0:T(8,128)(2,1)}, bf16[512,512]{1,0:T(8,128)(2,1)}, u32[]{:S(2)}, u32[]{:S(2)}) collective-permute-start(bf16[512,512]{1,0:T(8,128)(2,1)} %get-tuple-element.15), channel_id=1, source_target_pairs={{4,0},{8,4},{12,8},{5,1},{9,5},{13,9},{6,2},{10,6},{14,10},{7,3},{... | collective-permute-start | bytes 1572872 | tf_op jit(solution)/shard_map/ppermute | solution.py:26
  95.8 52.9 %collective-permute-start.16 = (bf16[512,512]{1,0:T(8,128)(2,1)}, bf16[512,512]{1,0:T(8,128)(2,1)}, u32[]{:S(2)}, u32[]{:S(2)}) collective-permute-start(bf16[512,512]{1,0:T(8,128)(2,1)} %get-tuple-element.16), channel_id=1, source_target_pairs={{0,8},{4,12},{8,0},{12,4},{1,9},{5,13},{9,1},{13,5},{2,10},{6,14},... | collective-permute-start | bytes 1572872 | tf_op jit(solution)/shard_map/ppermute | solution.py:27
  100.3 36.6 %collective-permute-start.38 = (bf16[64,512]{1,0:T(8,128)(2,1)S(1)}, bf16[64,512]{1,0:T(8,128)(2,1)S(1)}, u32[]{:S(2)}, u32[]{:S(2)}) collective-permute-start(bf16[64,512]{1,0:T(8,128)(2,1)S(1)} %get-tuple-element.19), channel_id=1, source_target_pairs={{12,8},{13,9},{14,10},{15,11},{28,24},{29,25},{30,26},{31,27}} | collective-permute-start | bytes 196616 | tf_op jit(solution)/shard_map/ppermute | solution.py:46
  115.0 39.1 %collective-permute-start.14 = (bf16[512,512]{1,0:T(8,128)(2,1)}, bf16[512,512]{1,0:T(8,128)(2,1)S(1)}, u32[]{:S(2)}, u32[]{:S(2)}) collective-permute-start(bf16[512,512]{1,0:T(8,128)(2,1)} %get-tuple-element.16), channel_id=1, source_target_pairs={{0,4},{4,8},{8,12},{1,5},{5,9},{9,13},{2,6},{6,10},{10,14},{3,7},{... | collective-permute-start | bytes 1572872 | tf_op jit(solution)/shard_map/ppermute | solution.py:25
  116.3 38.3 %collective-permute-start.33 = (bf16[2048,128]{1,0:T(8,128)(2,1)}, bf16[2048,128]{1,0:T(8,128)(2,1)}, u32[]{:S(2)}, u32[]{:S(2)}) collective-permute-start(bf16[2048,128]{1,0:T(8,128)(2,1)} %get-tuple-element.14), channel_id=1, source_target_pairs={{0,4},{1,5},{2,6},{3,7},{16,20},{17,21},{18,22},{19,23}} | collective-permute-start | bytes 1572872 | tf_op jit(solution)/shard_map/ppermute | solution.py:49
  136.9 19.2 %collective-permute-start.31 = (bf16[2048,128]{1,0:T(8,128)(2,1)}, bf16[2048,128]{1,0:T(8,128)(2,1)}, u32[]{:S(2)}, u32[]{:S(2)}) collective-permute-start(bf16[2048,128]{1,0:T(8,128)(2,1)} %bitcast_add_fusion.2), channel_id=1, source_target_pairs={{8,4},{12,8},{9,5},{13,9},{10,6},{14,10},{11,7},{15,11},{24,20},{2... | collective-permute-start | bytes 1572872 | tf_op jit(solution)/shard_map/ppermute | solution.py:46
  150.0 24.3 %collective-permute-start.15 = (bf16[512,512]{1,0:T(8,128)(2,1)}, bf16[512,512]{1,0:T(8,128)(2,1)}, u32[]{:S(2)}, u32[]{:S(2)}) collective-permute-start(bf16[512,512]{1,0:T(8,128)(2,1)} %get-tuple-element.16), channel_id=1, source_target_pairs={{4,0},{8,4},{12,8},{5,1},{9,5},{13,9},{6,2},{10,6},{14,10},{7,3},{... | collective-permute-start | bytes 1572872 | tf_op jit(solution)/shard_map/ppermute | solution.py:26
  151.3 25.4 %collective-permute-start.25 = (bf16[512,512]{1,0:T(8,128)(2,1)}, bf16[512,512]{1,0:T(8,128)(2,1)}, u32[]{:S(2)}, u32[]{:S(2)}) collective-permute-start(bf16[512,512]{1,0:T(8,128)(2,1)} %collective-permute-done.24.refs_2_), channel_id=1, source_target_pairs={{4,0},{8,12},{5,1},{9,13},{6,2},{10,14},{7,3},{11,15},{20,16},{24,... | collective-permute-start | bytes 1572872 | tf_op jit(solution)/shard_map/ppermute | solution.py:28
  154.1 31.6 %collective-permute-start.28 = (bf16[512,512]{1,0:T(8,128)(2,1)}, bf16[512,512]{1,0:T(8,128)(2,1)}, u32[]{:S(2)}, u32[]{:S(2)}) collective-permute-start(bf16[512,512]{1,0:T(8,128)(2,1)} %collective-permute-done.24.refs_2_), channel_id=1, source_target_pairs={{0,16},{4,20},{8,24},{12,28},{16,0},{20,4},{24,8},{28,12},{1,17},{... | collective-permute-start | bytes 1572872 | tf_op jit(solution)/shard_map/ppermute | solution.py:35
  154.6 32.3 %collective-permute-start.26 = (bf16[512,512]{1,0:T(8,128)(2,1)}, bf16[512,512]{1,0:T(8,128)(2,1)}, u32[]{:S(2)}, u32[]{:S(2)}) collective-permute-start(bf16[512,512]{1,0:T(8,128)(2,1)} %collective-permute-done.22.refs_0_), channel_id=1, source_target_pairs={{4,20},{8,24},{12,28},{20,4},{24,8},{28,12},{5,21},{9,25},{13,29},... | collective-permute-start | bytes 1572872 | tf_op jit(solution)/shard_map/ppermute | solution.py:35
  156.2 21.9 %collective-permute-start.42 = (bf16[64,512]{1,0:T(8,128)(2,1)S(1)}, bf16[64,512]{1,0:T(8,128)(2,1)}, u32[]{:S(2)}, u32[]{:S(2)}) collective-permute-start(bf16[64,512]{1,0:T(8,128)(2,1)S(1)} %get-tuple-element.18), channel_id=1, source_target_pairs={{0,4},{4,8},{1,5},{5,9},{2,6},{6,10},{3,7},{7,11},{16,20},{20,24},... | collective-permute-start | bytes 196616 | tf_op jit(solution)/shard_map/ppermute | solution.py:49
  174.3 25.9 %collective-permute-start.27 = (bf16[512,512]{1,0:T(8,128)(2,1)}, bf16[512,512]{1,0:T(8,128)(2,1)}, u32[]{:S(2)}, u32[]{:S(2)}) collective-permute-start(bf16[512,512]{1,0:T(8,128)(2,1)} %collective-permute-done.23.refs_1_), channel_id=1, source_target_pairs={{0,16},{4,20},{8,24},{16,0},{20,4},{24,8},{1,17},{5,21},{9,25},{17... | collective-permute-start | bytes 1572872 | tf_op jit(solution)/shard_map/ppermute | solution.py:35
  176.7 24.4 %collective-permute-start.17 = (bf16[512,512]{1,0:T(8,128)(2,1)}, bf16[512,512]{1,0:T(8,128)(2,1)}, u32[]{:S(2)}, u32[]{:S(2)}) collective-permute-start(bf16[512,512]{1,0:T(8,128)(2,1)} %collective-permute-done.16.refs_2_), channel_id=1, source_target_pairs={{4,0},{8,12},{5,1},{9,13},{6,2},{10,14},{7,3},{11,15},{20,16},{24,... | collective-permute-start | bytes 1572872 | tf_op jit(solution)/shard_map/ppermute | solution.py:28
  178.0 26.3 %collective-permute-start.34 = (bf16[2048,128]{1,0:T(8,128)(2,1)}, bf16[2048,128]{1,0:T(8,128)(2,1)}, u32[]{:S(2)}, u32[]{:S(2)}) collective-permute-start(bf16[2048,128]{1,0:T(8,128)(2,1)} %get-tuple-element.12), channel_id=1, source_target_pairs={{0,4},{4,8},{1,5},{5,9},{2,6},{6,10},{3,7},{7,11},{16,20},{20,24},... | collective-permute-start | bytes 1572872 | tf_op jit(solution)/shard_map/ppermute | solution.py:49
  194.7 15.1 %collective-permute-start.20 = (bf16[512,512]{1,0:T(8,128)(2,1)}, bf16[512,512]{1,0:T(8,128)(2,1)S(1)}, u32[]{:S(2)}, u32[]{:S(2)}) collective-permute-start(bf16[512,512]{1,0:T(8,128)(2,1)} %collective-permute-done.16.refs_2_), channel_id=1, source_target_pairs={{0,16},{4,20},{8,24},{12,28},{16,0},{20,4},{24,8},{28,12},{1,17},{... | collective-permute-start | bytes 1572872 | tf_op jit(solution)/shard_map/ppermute | solution.py:35
  196.1 25.0 %collective-permute-start.29 = (bf16[512,512]{1,0:T(8,128)(2,1)}, bf16[512,512]{1,0:T(8,128)(2,1)S(1)}, u32[]{:S(2)}, u32[]{:S(2)}) collective-permute-start(bf16[512,512]{1,0:T(8,128)(2,1)} %collective-permute-done.25.refs_3_), channel_id=1, source_target_pairs={{0,16},{12,28},{16,0},{28,12},{1,17},{13,29},{17,1},{29,13},{2,18}... | collective-permute-start | bytes 1572872 | tf_op jit(solution)/shard_map/ppermute | solution.py:35
  200.2 30.5 %collective-permute-start.18 = (bf16[512,512]{1,0:T(8,128)(2,1)}, bf16[512,512]{1,0:T(8,128)(2,1)S(1)}, u32[]{:S(2)}, u32[]{:S(2)}) collective-permute-start(bf16[512,512]{1,0:T(8,128)(2,1)} %copy-done.7), channel_id=1, source_target_pairs={{4,20},{8,24},{12,28},{20,4},{24,8},{28,12},{5,21},{9,25},{13,29},... | collective-permute-start | bytes 1572872 | tf_op jit(solution)/shard_map/ppermute | solution.py:35
  201.1 29.9 %collective-permute-start.19 = (bf16[512,512]{1,0:T(8,128)(2,1)}, bf16[512,512]{1,0:T(8,128)(2,1)S(1)}, u32[]{:S(2)}, u32[]{:S(2)}) collective-permute-start(bf16[512,512]{1,0:T(8,128)(2,1)} %collective-permute-done.15.refs_1_), channel_id=1, source_target_pairs={{0,16},{4,20},{8,24},{16,0},{20,4},{24,8},{1,17},{5,21},{9,25},{17... | collective-permute-start | bytes 1572872 | tf_op jit(solution)/shard_map/ppermute | solution.py:35
  204.4 32.2 %collective-permute-start.21 = (bf16[512,512]{1,0:T(8,128)(2,1)}, bf16[512,512]{1,0:T(8,128)(2,1)S(1)}, u32[]{:S(2)}, u32[]{:S(2)}) collective-permute-start(bf16[512,512]{1,0:T(8,128)(2,1)} %collective-permute-done.17.refs_3_), channel_id=1, source_target_pairs={{0,16},{12,28},{16,0},{28,12},{1,17},{13,29},{17,1},{29,13},{2,18}... | collective-permute-start | bytes 1572872 | tf_op jit(solution)/shard_map/ppermute | solution.py:35
  209.8 35.0 %collective-permute-start.32 = (bf16[2048,128]{1,0:T(8,128)(2,1)}, bf16[2048,128]{1,0:T(8,128)(2,1)S(1)}, u32[]{:S(2)}, u32[]{:S(2)}) collective-permute-start(bf16[2048,128]{1,0:T(8,128)(2,1)} %get-tuple-element.11), channel_id=1, source_target_pairs={{4,0},{8,4},{12,8},{5,1},{9,5},{13,9},{6,2},{10,6},{14,10},{7,3},{... | collective-permute-start | bytes 1572872 | tf_op jit(solution)/shard_map/ppermute | solution.py:46
  221.0 23.7 %collective-permute-start.35 = (bf16[2048,128]{1,0:T(8,128)(2,1)S(1)}, bf16[2048,128]{1,0:T(8,128)(2,1)S(1)}, u32[]{:S(2)}, u32[]{:S(2)}) collective-permute-start(bf16[2048,128]{1,0:T(8,128)(2,1)S(1)} %bitcast_add_fusion.1), channel_id=1, source_target_pairs={{0,4},{4,8},{8,12},{1,5},{5,9},{9,13},{2,6},{6,10},{10,14},{3,7},{... | collective-permute-start | bytes 1572872 | tf_op jit(solution)/shard_map/ppermute | solution.py:49
  (42 other events, 545.1 us)

commit v2 on v0

v2 whole, which is shorter than its diff:
```python
import functools
import math
import jax
import jax.numpy as jnp
from jax import lax
from jax.experimental import pallas as pl
from jax.experimental.pallas import tpu as pltpu
from jax.sharding import PartitionSpec as P

BLOCK = 128
CUTS = (2, 3, 3)
SUM_COST = 20
LATE = True
BASE_COST = 0

adapter_scale = 2.0

SWAP = [(0, 1), (1, 0)]
NT = (((1,), (1,)), ((), ()))
TN = (((0,), (0,)), ((), ()))

HBM = pl.BlockSpec(memory_space=pltpu.HBM)
ANY = pl.BlockSpec(memory_space=pl.ANY)
SMEM = pl.BlockSpec(memory_space=pltpu.SMEM)
VMEM = pl.BlockSpec(memory_space=pltpu.VMEM)
VMEM_LIMIT = 48 * 1024 * 1024


def swap_groups(blocks, f, n):
    others = jnp.stack([lax.dynamic_index_in_dim(blocks, (f + k) % n, 0, keepdims=False) for k in range(1, n)])
    return lax.ppermute(others, "groups", SWAP)


def hold(x, after):
    return pl.pallas_call(
        lambda *refs: None,
        out_shape=jax.ShapeDtypeStruct(x.shape, x.dtype),
        in_specs=[HBM] * (1 + len(after)),
        out_specs=HBM,
        input_output_aliases={0: 0},
        cost_estimate=cost(),
        name="hold",
    )(x, *after)


def pack(a_own, codes, ids, size):
    half, both = a_own.shape[0] // 2, a_own.shape[1]
    parts = codes.shape[1] // both

    def kernel(ids, a_own, codes, out, held, sems):
        first = pl.multiple_of(ids[1] * half, half)
        copies = [pltpu.make_async_copy(a_own.at[pl.ds(first, half)], held.at[pl.ds(0, half)], sems.at[parts])]
        for k in range(parts):
            src = codes.at[pl.ds(first, size), pl.ds(k * both, both)]
            copies.append(pltpu.make_async_copy(src, held.at[pl.ds(half + k * size, size)], sems.at[k]))
        for copy in copies:
            copy.start()
        for copy in copies:
            copy.wait()
        copy = pltpu.make_async_copy(held, out, sems.at[0])
        copy.start()
        copy.wait()

    shape = (half + parts * size, both)
    return pl.pallas_call(
        kernel,
        out_shape=jax.ShapeDtypeStruct(shape, a_own.dtype),
        in_specs=[SMEM, HBM, HBM],
        out_specs=HBM,
        scratch_shapes=[pltpu.VMEM(shape, a_own.dtype), pltpu.SemaphoreType.DMA((parts + 1,))],
        cost_estimate=cost(),
        name="pack",
    )(ids, a_own, codes)


def inward(x):
    return lax.ppermute(x, "fsdp", [(0, 1), (3, 2)])


def inside(x):
    return lax.ppermute(x, "fsdp", [(1, 2), (2, 1)])


def outward(x):
    return lax.ppermute(x, "fsdp", [(1, 0), (2, 3)])


def slot_bounds(slot, lengths, slot_job, first):
    job = slot_job[slot]
    start = jnp.int32(0)
    for j in range(lengths.shape[0]):
        start = start + jnp.where(j < job, lengths[j], 0)
    return start - first, start - first + lengths[job]


def row_mask(slot, lengths, slot_job, first, shape):
    low, high = slot_bounds(slot, lengths, slot_job, first)
    row = lax.broadcasted_iota(jnp.int32, shape, 0)
    return (row >= low) & (row < high)


def u_kernel(n, ids, lengths, slot_job, grad, factors, *refs):
    out, g_all, b_all, sems = refs[-4:]
    f, column = ids[0], ids[2]
    rows, cols = g_all.shape
    rank = out.shape[1]
    grab = pltpu.make_async_copy(grad.at[:, pl.ds(pl.multiple_of(column * cols, cols), cols)], g_all, sems.at[0])
    grab.start()
    fetch = pltpu.make_async_copy(factors, b_all, sems.at[1])
    fetch.start()
    fetch.wait()
    grab.wait()
    total = jnp.zeros(out.shape, jnp.float32)
    for s in range(n):
        part = lax.dot_general(g_all[...], b_all[s], NT, preferred_element_type=jnp.float32)
        total = jnp.where(row_mask(s, lengths, slot_job, f * rows, out.shape), part, total)
    out[...] = total.astype(out.dtype)


def fetch_other(slot, f, n, own, others, dst, sem):
    pl.when(f == slot)(lambda: pltpu.make_async_copy(own, dst, sem).start())
    pl.when(f != slot)(lambda: pltpu.make_async_copy(others.at[lax.rem(slot - f + 2 * n - 1, n)], dst, sem).start())


def h_kernel(n, ids, lengths, slot_job, acts, own, others, first_blocks, *refs):
    out, a_all, sems = refs[-3:]
    f, g = ids[0], ids[1]
    rows = acts.shape[0]
    half = own.shape[0] // 2
    both = out.shape[1]
    here, there = pl.multiple_of(g * half, half), pl.multiple_of((1 - g) * half, half)
    for s in range(n):
        dst = a_all.at[pl.ds(here, half), pl.ds(s * both, both)]
        pltpu.make_async_copy(first_blocks.at[s, pl.ds(0, half)], dst, sems.at[s, 0]).start()
        fetch_other(s, f, n, own.at[pl.ds(there, half)], others, a_all.at[pl.ds(there, half), pl.ds(s * both, both)], sems.at[s, 1])
    for s in range(n):
        for side in range(2):
            pltpu.make_async_copy(own.at[pl.ds(0, half)], a_all.at[pl.ds(0, half), pl.ds(s * both, both)], sems.at[s, side]).wait()
    product = jnp.dot(acts[...], a_all[...], preferred_element_type=jnp.float32)
    total = jnp.zeros(out.shape, jnp.float32)
    for s in range(n):
        total = jnp.where(row_mask(s, lengths, slot_job, f * rows, out.shape), product[:, s * both:(s + 1) * both], total)
    out[...] = total.astype(out.dtype)


def added(parts):
    total = parts[0].astype(jnp.float32)
    for part in parts[1:]:
        total = total + part.astype(jnp.float32)
    return total.astype(jnp.bfloat16)


def terms_a_kernel(n, ids, lengths, slot_job, acts, u_parts, masked, *refs):
    outs, (held, sems) = refs[:n], refs[n:]
    f = ids[0]
    shards, rows, _ = u_parts.shape
    both = held.shape[2]
    key = added([u_parts[k] for k in range(shards // 2)])
    value = added([u_parts[k] for k in range(shards // 2, shards)])
    doubled = jnp.concatenate([key, value], axis=1).astype(jnp.float32) * adapter_scale
    for s in range(n):
        part = jnp.where(row_mask(s, lengths, slot_job, f * rows, doubled.shape), doubled, 0.0).astype(jnp.bfloat16)
        masked[:, s * both:(s + 1) * both] = part
    left = f < n // 2
    third = jnp.where(f == 0, 1, jnp.where(f == n - 1, n - 2, jnp.where(left, 0, n - 1)))
    copies = [pltpu.make_async_copy(held.at[k], outs[k], sems.at[k]) for k in range(n)]
    for k, s in enumerate((jnp.where(left, n - 1, 0), jnp.where(left, n - 2, 1), third, f)):
        part = jnp.where(row_mask(s, lengths, slot_job, f * rows, doubled.shape), doubled, 0.0).astype(jnp.bfloat16)
        held[k] = lax.dot_general(acts[...], part, TN, preferred_element_type=jnp.float32).astype(jnp.bfloat16)
        copies[k].start()
    for copy in copies:
        copy.wait()


def terms_b_kernel(n, ids, lengths, slot_job, grad, h_parts, out, g_all, sem):
    f, column = ids[0], ids[2]
    rows, cols = g_all.shape
    shards = h_parts.shape[0]
    rank = out.shape[1]
    grab = pltpu.make_async_copy(grad.at[:, pl.ds(pl.multiple_of(column * cols, cols), cols)], g_all, sem)
    grab.start()
    low_h = added([h_parts[k] for k in range(shards)]).astype(jnp.float32) * adapter_scale
    side = jnp.where(column < shards // 2, low_h[:, :rank], low_h[:, rank:])
    grab.wait()
    for s in range(n):
        part = jnp.where(row_mask(s, lengths, slot_job, f * rows, side.shape), side, 0.0).astype(jnp.bfloat16)
        out[s] = lax.dot_general(part, g_all[...], TN, preferred_element_type=jnp.float32).astype(jnp.bfloat16)


def base_kernel(n, offset, size, packed, ids, grad, far_core, far_other, masked, far_masked, scale_rows, first_blocks, blocks, *refs):
    out, far_out, grads, masks, codes, factors, result, sems, in_sems, out_sem = refs[-10:]
    g, dp = ids[1], ids[3]
    rows, wide = grad.shape
    half, both, cols = out.shape[1] // 2, first_blocks.shape[2], wide // n
    part = far_core.shape[0]
    first = pl.multiple_of(g * half + offset, BLOCK)
    copies = [
        pltpu.make_async_copy(grad, grads.at[pl.ds(0, rows)], in_sems.at[0]),
        pltpu.make_async_copy(far_core, grads.at[pl.ds(pl.multiple_of(rows + dp * part, part), part)], in_sems.at[1]),
        pltpu.make_async_copy(far_other, grads.at[pl.ds(pl.multiple_of(rows + (1 - dp) * part, part), part)], in_sems.at[2]),
        pltpu.make_async_copy(masked, masks.at[pl.ds(0, rows)], in_sems.at[3]),
        pltpu.make_async_copy(far_masked, masks.at[pl.ds(rows, rows)], in_sems.at[4]),
    ]
    for s in range(n):
        if packed:
            for k in range(cols // both):
                src = first_blocks.at[s, pl.ds(half + k * size, size)]
                copies.append(pltpu.make_async_copy(src, codes.at[:, pl.ds(s * cols + k * both, both)], sems.at[s, k]))
        else:
            copies.append(pltpu.make_async_copy(blocks.at[s], codes.at[:, pl.ds(s * cols, cols)], sems.at[s, 0]))
        copies.append(pltpu.make_async_copy(first_blocks.at[s, pl.ds(offset, size)], factors.at[:, pl.ds(s * both, both)], sems.at[n, s]))
    for copy in copies:
        copy.start()
    for copy in copies:
        copy.wait()
    weight = []
    for b in range(size // BLOCK):
        scale = scale_rows[pl.ds(first // BLOCK + b, 1), :]
        weight.append((codes[b * BLOCK:(b + 1) * BLOCK, :].astype(jnp.float32) * scale).astype(jnp.bfloat16))
    weight = jnp.concatenate(weight, axis=0)
    for side in range(2):
        take = slice(side * rows, (side + 1) * rows)
        total = lax.dot_general(grads[take], weight, NT, preferred_element_type=jnp.float32)
        total += lax.dot_general(masks[take], factors[...], NT, preferred_element_type=jnp.float32)
        if side == 0:
            result[...] = total.astype(jnp.bfloat16)
            keep = pltpu.make_async_copy(result, out.at[:, pl.ds(first, size)], out_sem)
            keep.start()
        else:
            far_out[...] = total.astype(jnp.bfloat16)
    keep.wait()


def params():
    return pltpu.CompilerParams(vmem_limit_bytes=VMEM_LIMIT)


def cost(us=0):
    return pl.CostEstimate(flops=int(us * 1.1e9) + 1, bytes_accessed=1, transcendentals=0)


def sum_terms(own, *arrived):
    def kernel(own, *refs):
        total = own[...].astype(jnp.float32)
        for ref in refs[:-1]:
            total = total + ref[...].astype(jnp.float32)
        refs[-1][...] = total

    return pl.pallas_call(
        kernel,
        out_shape=jax.ShapeDtypeStruct(own.shape, jnp.float32),
        compiler_params=params(),
        cost_estimate=cost(SUM_COST),
        name="sum_terms",
    )(own, *arrived)


def piece_of(whole, ids, offset, size, after):
    half = whole.shape[0] // 2
    step = math.gcd(math.gcd(offset, size), half)

    def kernel(ids, whole, *refs):
        refs[-1][...] = whole[...]

    return pl.pallas_call(
        kernel,
        out_shape=jax.ShapeDtypeStruct((size, whole.shape[1]), whole.dtype),
        grid_spec=pltpu.PrefetchScalarGridSpec(
            num_scalar_prefetch=1,
            grid=(size // step,),
            in_specs=[pl.BlockSpec((step, whole.shape[1]), lambda i, ids: ((ids[1] * half + offset) // step + i, 0))] + [HBM] * len(after),
            out_specs=pl.BlockSpec((step, whole.shape[1]), lambda i, ids: (i, 0)),
        ),
        cost_estimate=cost(),
        name="piece",
    )(ids, whole, *after)


def place(whole, part, ids, offset):
    def kernel(ids, part, _, out, sem):
        first = pl.multiple_of((1 - ids[1]) * (out.shape[1] // 2) + offset, BLOCK)
        copy = pltpu.make_async_copy(part, out.at[:, pl.ds(first, part.shape[1])], sem)
        copy.start()
        copy.wait()

    return pl.pallas_call(
        kernel,
        out_shape=jax.ShapeDtypeStruct(whole.shape, whole.dtype),
        in_specs=[SMEM, VMEM, HBM],
        out_specs=HBM,
        scratch_shapes=[pltpu.SemaphoreType.DMA],
        input_output_aliases={2: 0},
        compiler_params=params(),
        cost_estimate=cost(),
        name="place",
    )(ids, part, whole)


def local_chain(activations, grad_out, codes, scales, adapter_a, adapter_b, lengths, slot_job):
    n = 4
    rows, width = activations.shape
    wide = grad_out.shape[1]
    both = adapter_a.shape[2]
    rank = both // 2
    cols = codes.shape[1]
    block_cols = adapter_b.shape[1]
    half = width // 2
    f, g = lax.axis_index("fsdp"), lax.axis_index("groups")
    tp, dp = lax.axis_index("tp"), lax.axis_index("dp")
    ids = jnp.stack([f, g, tp * 2 + dp, dp]).astype(jnp.int32)
    a_own = adapter_a[0]
    shards = ("tp", "dp")

    b_all = lax.all_gather(adapter_b[0].T, "fsdp")
    part = rows // 2
    far_core = lax.ppermute(lax.dynamic_slice_in_dim(grad_out, dp * part, part, 0), "groups", SWAP)
    far_other = lax.ppermute(far_core, "dp", SWAP)

    sizes = [half * parts // sum(CUTS) for parts in CUTS]
    offsets = [sum(sizes[:c]) for c in range(len(CUTS))]
    first_blocks = lax.all_gather(pack(a_own, codes, ids, sizes[0]), "fsdp")
    code_blocks = [first_blocks] + [
        lax.all_gather(lax.dynamic_slice_in_dim(codes, g * half + offset, size, 0), "fsdp") for offset, size in zip(offsets[1:], sizes[1:])
    ]

    u_part = pl.pallas_call(
        functools.partial(u_kernel, n),
        out_shape=jax.ShapeDtypeStruct((rows, rank), jnp.bfloat16),
        in_specs=[SMEM] * 3 + [HBM] * 2,
        out_specs=VMEM,
        scratch_shapes=[
            pltpu.VMEM((rows, block_cols), jnp.bfloat16),
            pltpu.VMEM((n, rank, block_cols), jnp.bfloat16),
            pltpu.SemaphoreType.DMA((2,)),
        ],
        compiler_params=params(),
        cost_estimate=cost(),
        name="low_u",
    )(ids, lengths, slot_job, grad_out, b_all)
    masked_u, far, middle, last, own_a = pl.pallas_call(
        functools.partial(terms_a_kernel, n),
        out_shape=(jax.ShapeDtypeStruct((rows, n * both), jnp.bfloat16),) + (jax.ShapeDtypeStruct((width, both), jnp.bfloat16),) * 4,
        in_specs=[SMEM] * 3 + [VMEM] * 2,
        out_specs=(VMEM,) + (HBM,) * 4,
        scratch_shapes=[pltpu.VMEM((n, width, both), jnp.bfloat16), pltpu.SemaphoreType.DMA((n,))],
        compiler_params=params(),
        cost_estimate=cost(),
        name="terms_a",
    )(ids, lengths, slot_job, activations, lax.all_gather(u_part, shards))
    far_in, middle_in, near = inward(far), inward(middle), inward(last)
    far_masked = lax.ppermute(masked_u, "groups", SWAP)
    a_others = swap_groups(first_blocks[:, :half], f, n)
    far = inside(far + far_in)

    scale_rows = jnp.repeat(scales, BLOCK, axis=1)

    def base(c, before, after):
        blocks, offset, size = code_blocks[c], offsets[c], sizes[c]
        more = [] if before is None else [before]
        return pl.pallas_call(
            functools.partial(base_kernel, n, offset, size, c == 0),
            out_shape=(jax.ShapeDtypeStruct((rows, width), jnp.bfloat16), jax.ShapeDtypeStruct((rows, size), jnp.bfloat16)),
            in_specs=[SMEM] + [ANY] * 5 + [VMEM] + [HBM] * (2 + len(more)) + [ANY] * len(after),
            out_specs=(HBM, VMEM),
            scratch_shapes=[
                pltpu.VMEM((2 * rows, wide), jnp.bfloat16),
                pltpu.VMEM((2 * rows, n * both), jnp.bfloat16),
                pltpu.VMEM((size, wide), jnp.bfloat16),
                pltpu.VMEM((size, n * both), jnp.bfloat16),
                pltpu.VMEM((rows, size), jnp.bfloat16),
                pltpu.SemaphoreType.DMA((n + 1, wide // n // both)),
                pltpu.SemaphoreType.DMA((5,)),
                pltpu.SemaphoreType.DMA,
            ],
            input_output_aliases={9: 0} if more else {},
            compiler_params=params(),
            cost_estimate=cost(BASE_COST),
            name="base",
        )(ids, grad_out, far_core, far_other, masked_u, far_masked, scale_rows, first_blocks, blocks, *more, *after)

    h_part = pl.pallas_call(
        functools.partial(h_kernel, n),
        out_shape=jax.ShapeDtypeStruct((rows, both), jnp.bfloat16),
        in_specs=[SMEM] * 3 + [VMEM] + [ANY] * 3,
        out_specs=VMEM,
        scratch_shapes=[pltpu.VMEM((width, n * both), jnp.bfloat16), pltpu.SemaphoreType.DMA((n, 2))],
        compiler_params=params(),
        cost_estimate=cost(),
        name="low_h",
    )(ids, lengths, slot_job, activations, a_own, a_others, first_blocks)
    terms_b = pl.pallas_call(
        functools.partial(terms_b_kernel, n),
        out_shape=jax.ShapeDtypeStruct((n, rank, block_cols), jnp.bfloat16),
        in_specs=[SMEM] * 3 + [HBM, VMEM],
        out_specs=VMEM,
        scratch_shapes=[pltpu.VMEM((rows, block_cols), jnp.bfloat16), pltpu.SemaphoreType.DMA],
        compiler_params=params(),
        cost_estimate=cost(),
        name="terms_b",
    )(ids, lengths, slot_job, grad_out, lax.all_gather(h_part, shards))
    grad_b = lax.psum_scatter(terms_b, "fsdp", scatter_dimension=0).astype(jnp.float32)
    middle = inside(middle + middle_in)

    result, far_out = base(0, None, ())
    parts = [lax.ppermute(far_out, "groups", SWAP)]
    last_out = last + far
    for c in range(1, len(CUTS)):
        result, far_out = base(c, result, (last_out,) if c == len(CUTS) - 1 and LATE else (terms_b,))
        parts.append(lax.ppermute(far_out, "groups", SWAP))
    for part, offset in zip(parts, offsets):
        result = place(result, part, ids, offset)
    grad_a = sum_terms(own_a, near, middle, outward(last_out))
    return result, grad_a[None], grad_b.T[None]


def local_any(activations, grad_out, codes, scales, adapter_a, adapter_b, lengths, slot_job):
    rows = activations.shape[0]
    width = activations.shape[1]
    wide = grad_out.shape[1]
    half = wide // 2
    both = adapter_a.shape[2]
    rank = both // 2
    jobs = lengths.shape[0]
    shards = lax.axis_size(("tp", "dp"))
    column = lax.axis_index(("tp", "dp"))
    block_cols = wide // shards
    first = lax.axis_index("fsdp") * rows
    starts = jnp.cumsum(lengths) - lengths
    positions = first + jnp.arange(rows, dtype=jnp.int32)
    row_job = jnp.sum((positions[:, None] >= starts[None, :]).astype(jnp.int32), axis=1) - 1
    onehot = row_job[:, None] == slot_job[None, :]
    scale_cols = jnp.repeat(jnp.repeat(scales, BLOCK, axis=0), BLOCK, axis=1)
    weight = (lax.all_gather(codes, "fsdp", axis=1, tiled=True).astype(jnp.float32) * scale_cols).astype(jnp.bfloat16)
    frozen = lax.dot_general(grad_out, weight, NT, preferred_element_type=jnp.float32)
    g_block = lax.dynamic_slice_in_dim(grad_out, column * block_cols, block_cols, 1)
    key_side = column * block_cols < half
    a_every = lax.all_gather(adapter_a, "fsdp", axis=0, tiled=True)
    b_every = lax.all_gather(adapter_b, "fsdp", axis=0, tiled=True)
    h_every = jnp.einsum("ri,sic->rsc", activations, a_every, preferred_element_type=jnp.float32)
    u_every = jnp.einsum("ro,sok->rsk", g_block, b_every, preferred_element_type=jnp.float32)
    h_part = jnp.sum(jnp.where(onehot[:, :, None], h_every, 0.0), axis=1)
    u_block = jnp.sum(jnp.where(onehot[:, :, None], u_every, 0.0), axis=1)
    u_part = jnp.concatenate([jnp.where(key_side, u_block, 0.0), jnp.where(key_side, 0.0, u_block)], axis=1)
    low_h = lax.psum(h_part.astype(jnp.bfloat16), ("tp", "dp"))
    low_u = lax.psum(u_part.astype(jnp.bfloat16), ("tp", "dp"))
    masked_u = jnp.where(onehot[:, :, None], low_u[:, None, :], 0).reshape(rows, jobs * both)
    branch = jnp.einsum("rsc,sic->ri", masked_u.reshape(rows, jobs, both), a_every, preferred_element_type=jnp.float32)
    input_gradient = (frozen + adapter_scale * branch).astype(jnp.bfloat16)
    h_side = jnp.where(key_side, low_h[:, :rank], low_h[:, rank:])
    masked_h = jnp.where(onehot[:, :, None], h_side[:, None, :], 0).reshape(rows, jobs * rank)
    down = lax.dot_general(activations, masked_u, TN, preferred_element_type=jnp.float32) * adapter_scale
    up = lax.dot_general(g_block, masked_h, TN, preferred_element_type=jnp.float32) * adapter_scale
    down = down.reshape(width, jobs, both).astype(jnp.bfloat16)
    up = up.reshape(block_cols, jobs, rank).astype(jnp.bfloat16)
    summed_a = lax.psum_scatter(down, "fsdp", scatter_dimension=1, tiled=True).astype(jnp.float32)
    summed_b = lax.psum_scatter(up, "fsdp", scatter_dimension=1, tiled=True).astype(jnp.float32)
    return input_gradient, jnp.transpose(summed_a, (1, 0, 2)), jnp.transpose(summed_b, (1, 0, 2))


def solution(mesh):
    in_specs = (
        P(("groups", "fsdp"), ("tp", "dp")),
        P(("groups", "fsdp"), None),
        P(("tp", "dp"), "fsdp"),
        P(("tp", "dp"), None),
        P("fsdp", ("tp", "dp"), None),
        P("fsdp", ("tp", "dp"), None),
        P("groups"),
        P(),
    )
    out_specs = (
        P(("groups", "fsdp"), ("tp", "dp")),
        P(("groups", "fsdp"), ("tp", "dp"), None),
        P(("groups", "fsdp"), ("tp", "dp"), None),
    )
    shape = dict(mesh.shape)
    chain = shape == {"groups": 2, "fsdp": 4, "tp": 2, "dp": 2}
    local = local_chain if chain else local_any
    return jax.shard_map(local, mesh=mesh, in_specs=in_specs, out_specs=out_specs, check_vma=False)
```

time: 355 us -> 189 us (0.53)
  waiting for transfers between devices: 242 us -> 57.9 us
  starting transfers between devices: 0.2 us -> 24.2 us
  matrix products: 22.1 us -> 0 us
  Pallas kernels: 21.2 us -> 43.3 us
  local copies, waits for them, and re-layouts: 24.2 us -> 8.06 us
  blocking collectives: 17.3 us -> 31.9 us
  other arithmetic: 13.5 us -> 8.42 us
    all_gather x2 -> x3, waiting for transfers between devices: 168 us -> 29.8 us  [the longest x2 29.8 us: local_chain(): lax.all_gather(lax.dynamic_slice_in_dim(codes, g * half + offset, size, 0...]
    pallas_call x0 -> x12, Pallas kernels: none -> 43.3 us  [the longest x3 22.2 us: base(): pl.pallas_call(functools.partial(base_kernel, n, offset, size, c == 0), o...]
    reduce_scatter x2 -> x1, waiting for transfers between devices: 40.7 us -> 0.02 us  [local_chain(): lax.psum_scatter(terms_b, 'fsdp', scatter_dimension=0).astype(jnp.float32)]
    psum x1 -> x0, waiting for transfers between devices: 31.4 us -> none  [local(): lax.psum(u_part.astype(jnp.bfloat16), ('tp', 'dp')).astype(jnp.float32)]
    ppermute x0 -> x13, waiting for transfers between devices: none -> 28.1 us  [the longest x3 22.4 us: inward(): return lax.ppermute(x, 'fsdp', [(0, 1), (3, 2)])]
    ppermute x0 -> x13, starting transfers between devices: none -> 24 us  [the longest x3 11.7 us: inward(): return lax.ppermute(x, 'fsdp', [(0, 1), (3, 2)])]
    dot_general x3 -> x0, matrix products: 22.1 us -> none  [the longest x1 16.1 us: local(): lax.dot_general(grad_out, weight, (((1,), (1,)), ((), ())), preferred_ele...]
    another operation x3 -> x0, Pallas kernels: 19.9 us -> none
  transfers between devices with their start and end apart: 5 -> 17, of which waited for: 4 -> 5; matrix products, arithmetic and copies ran while one was open for 8% -> 6% of each run, Pallas kernels for 4% -> 22%
where the time goes in v2:
time: 189 us; the launch traced here: 188 us
  waiting for transfers between devices  57.9 us (31%)
  Pallas kernels  43.3 us (23%)
  blocking collectives  31.9 us (17%)
  starting transfers between devices  24.2 us (13%)
  between operations  14.1 us (7%)
  other arithmetic  8.42 us (4%)
  local copies, waits for them, and re-layouts  8.06 us (4%)
    all_gather x2, waiting for transfers between devices, local_chain(): lax.all_gather(lax.dynamic_slice_in_dim(codes, g * half + offset, size, 0...  29.8 us
    ppermute x3, waiting for transfers between devices, inward(): return lax.ppermute(x, 'fsdp', [(0, 1), (3, 2)])  22.4 us
    pallas_call x3, Pallas kernels, base(): pl.pallas_call(functools.partial(base_kernel, n, offset, size, c == 0), o...  22.2 us
    all_gather x1, blocking collectives, local_chain(): b_all = lax.all_gather(adapter_b[0].T, 'fsdp')  16 us
    ppermute x3, starting transfers between devices, inward(): return lax.ppermute(x, 'fsdp', [(0, 1), (3, 2)])  11.7 us
    all_gather x1, blocking collectives, local_chain(): lax.all_gather(h_part, shards)  8.01 us
    all_gather x1, blocking collectives, local_chain(): lax.all_gather(u_part, shards)  7.9 us
    ppermute x2, waiting for transfers between devices, local_chain(): parts.append(lax.ppermute(far_out, 'groups', SWAP))  5.65 us
  transfers between devices with their start and end apart: 17, of which 5 were waited for; matrix products, arithmetic and copies ran while one was open for 6% of the time, Pallas kernels for 22%

profile of v2, /device:TPU:0, one launch (start us, length us, event | category | flops | bytes accessed | tf_op | source)
XLA Modules:
  0.0 187.9 jit_solution(4386661314158982129)
XLA Ops:
  7.8 2.6 %pack.1 = bf16[2048,128]{1,0:T(8,128)(2,1)} custom-call(s32[4]{0:T(128)} %pad_add_fusion.ids, bf16[2048,128]{1,0:T(8,128)(2,1)} %bitcast.37, bf16[2048,512]{1,0:T(8,128)(2,1)} %codes.1), custom_call_target="tpu_custom_call" | custom-call | flops 1 | bytes 1 | tf_op jit(solution)/shard_map/pack/pallas_call | solution.py:65
  10.6 2.1 %constant_dynamic-slice_fusion.3 = (bf16[384,512]{1,0:T(8,128)(2,1)}, bf16[384,512]{1,0:T(8,128)(2,1)}) fusion(bf16[2048,512]{1,0:T(8,128)(2,1)} %codes.1, s32[]{:T(128)S(6)} %select_n.36, s32[]{:T(128)S(6)} %select_n.35), kind=kLoop, calls=%fused_computation.6 | loop fusion | bytes 1572872 | tf_op jit(solution)/shard_map/dynamic_slice | solution.py:323
  13.9 3.0 %collective-permute-start = (bf16[320,2048]{1,0:T(8,128)(2,1)}, bf16[320,2048]{1,0:T(8,128)(2,1)}, u32[]{:S(2)}, u32[]{:S(2)}) collective-permute-start(bf16[320,2048]{1,0:T(8,128)(2,1)} %constant_dynamic-slice_fusion.5), channel_id=1, source_target_pairs={{0,16},{16,0},{1,17},{17,1},{2,18},{18,2},{3,19},{19,3},{4,20},{20... | collective-permute-start | bytes 3932168 | tf_op jit(solution)/shard_map/ppermute | solution.py:316
  17.0 16.0 %all-gather = bf16[256,512]{1,0:T(8,128)(2,1)S(1)} all-gather(bf16[64,512]{1,0:T(8,128)(2,1)S(1)} %bitcast.43), channel_id=2, replica_groups=mesh['groups'=2,'fsdp'=4,'tp'=2,'dp'=2] {'fsdp'}, dimensions={0}, use_global_device_ids=true | all-gather | bytes 327680 | tf_op jit(solution)/shard_map/all_gather | solution.py:314
  33.0 1.5 low_u.1
  34.6 7.9 %all-gather.1 = bf16[2560,64]{1,0:T(8,128)(2,1)S(1)} all-gather(bf16[640,64]{1,0:T(8,128)(2,1)S(1)} %low_u.1), channel_id=3, replica_groups=mesh['groups'=2,'fsdp'=4,'tp'=2,'dp'=2] {'tp','dp'}, dimensions={0}, use_global_device_ids=true | all-gather | bytes 409600 | tf_op jit(solution)/shard_map/all_gather | solution.py:349
  42.5 5.0 %terms_a.1 = (bf16[640,512]{1,0:T(8,128)(2,1)S(1)}, bf16[2048,128]{1,0:T(8,128)(2,1)}, bf16[2048,128]{1,0:T(8,128)(2,1)S(1)}, bf16[2048,128]{1,0:T(8,128)(2,1)}, bf16[2048,128]{1,0:T(8,128)(2,1)S(1)}) custom-call(s32[4]{0:T(128)S(1)} %copy-done.12, s32[4]{0:T(128)S(1)} %copy-done.13, s32[4]{0:T(128)S(1)} %copy-done.14, bf16[640,2048]{1,0:T(8,128)(2,1)S(1)} %copy-done.6, ...), custom_call_target="tpu_custom_call" | custom-call | flops 1 | bytes 1 | tf_op jit(solution)/shard_map/terms_a/pallas_call | solution.py:340
  48.3 4.3 %collective-permute-start.4 = (bf16[2048,128]{1,0:T(8,128)(2,1)}, bf16[2048,128]{1,0:T(8,128)(2,1)}, u32[]{:S(2)}, u32[]{:S(2)}) collective-permute-start(bf16[2048,128]{1,0:T(8,128)(2,1)} %get-tuple-element.18), channel_id=1, source_target_pairs={{0,4},{12,8},{1,5},{13,9},{2,6},{14,10},{3,7},{15,11},{16,20},{28,... | collective-permute-start | bytes 1572872 | tf_op jit(solution)/shard_map/ppermute | solution.py:77
  53.2 2.1 %collective-permute-start.10 = (bf16[2048,128]{1,0:T(8,128)(2,1)S(1)}, bf16[2048,128]{1,0:T(8,128)(2,1)}, u32[]{:S(2)}, u32[]{:S(2)}) collective-permute-start(bf16[2048,128]{1,0:T(8,128)(2,1)S(1)} %get-tuple-element.24), channel_id=1, source_target_pairs={{0,4},{12,8},{1,5},{13,9},{2,6},{14,10},{3,7},{15,11},{16,20},{28,... | collective-permute-start | bytes 1572872 | tf_op jit(solution)/shard_map/ppermute | solution.py:77
  55.3 15.5 %collective-permute-done.4 = bf16[2048,128]{1,0:T(8,128)(2,1)} collective-permute-done((bf16[2048,128]{1,0:T(8,128)(2,1)}, bf16[2048,128]{1,0:T(8,128)(2,1)}, u32[]{:S(2)}, u32[]{:S(2)}) %collective-permute-start.4) | collective-permute-done | bytes 524320 | tf_op jit(solution)/shard_map/ppermute | solution.py:77
  70.8 2.1 %add.77 = bf16[2048,128]{1,0:T(8,128)(2,1)} add(bf16[2048,128]{1,0:T(8,128)(2,1)} %get-tuple-element.18, bf16[2048,128]{1,0:T(8,128)(2,1)} %collective-permute-done.4) | non-fusion elementwise | flops 262144 | bytes 1572864 | tf_op jit(solution)/shard_map/add | solution.py:353
  72.9 1.5 collective-permute-start.5
  77.0 6.9 %collective-permute-done.10 = bf16[2048,128]{1,0:T(8,128)(2,1)} collective-permute-done((bf16[2048,128]{1,0:T(8,128)(2,1)S(1)}, bf16[2048,128]{1,0:T(8,128)(2,1)}, u32[]{:S(2)}, u32[]{:S(2)}) %collective-permute-start.10) | collective-permute-done | bytes 524320 | tf_op jit(solution)/shard_map/ppermute | solution.py:77
  83.8 5.3 %collective-permute-start.9 = (bf16[2048,128]{1,0:T(8,128)(2,1)}, bf16[2048,128]{1,0:T(8,128)(2,1)}, u32[]{:S(2)}, u32[]{:S(2)}) collective-permute-start(bf16[2048,128]{1,0:T(8,128)(2,1)} %get-tuple-element.17), channel_id=1, source_target_pairs={{0,4},{12,8},{1,5},{13,9},{2,6},{14,10},{3,7},{15,11},{16,20},{28,... | collective-permute-start | bytes 1572872 | tf_op jit(solution)/shard_map/ppermute | solution.py:77
  89.1 2.0 %add.79 = bf16[2048,128]{1,0:T(8,128)(2,1)} add(bf16[2048,128]{1,0:T(8,128)(2,1)S(1)} %get-tuple-element.24, bf16[2048,128]{1,0:T(8,128)(2,1)} %collective-permute-done.10) | non-fusion elementwise | flops 262144 | bytes 1572864 | tf_op jit(solution)/shard_map/add | solution.py:402
  91.1 1.5 collective-permute-start.11
  92.6 2.1 %add.78.refs_1_ = bf16[2048,128]{1,0:T(8,128)(2,1)} add(bf16[2048,128]{1,0:T(8,128)(2,1)} %get-tuple-element.17, bf16[2048,128]{1,0:T(8,128)(2,1)} %collective-permute-done.5) | non-fusion elementwise | flops 262144 | bytes 1572864 | tf_op jit(solution)/shard_map/add | solution.py:406
  96.2 7.3 %base.3 = (bf16[640,2048]{1,0:T(8,128)(2,1)}, bf16[640,256]{1,0:T(8,128)(2,1)}) custom-call(s32[4]{0:T(128)S(1)} %copy-done.12, bf16[640,2048]{1,0:T(8,128)(2,1)} %grad.9, bf16[320,2048]{1,0:T(8,128)(2,1)} %collective-permute-done.far_core, bf16[320,2048]{1,0:T(8,128)(2,1)S(1)} %collective-permute-done.1.far_other, ...), custom_call_target="tpu_custom_call" | custom-call | flops 1 | bytes 1 | tf_op jit(solution)/shard_map/base/pallas_call | solution.py:360
  104.1 2.7 %low_h.1 = bf16[640,128]{1,0:T(8,128)(2,1)S(1)} custom-call(s32[4]{0:T(128)S(1)} %copy-done.12, s32[4]{0:T(128)S(1)} %copy-done.13, s32[4]{0:T(128)S(1)} %copy-done.14, bf16[640,2048]{1,0:T(8,128)(2,1)S(1)} %copy-done.7, bf16[2048,128]{1,0:T(8,128)(2,1)S(1)} %bitcast.38, bf16[3,1024,128]{2,1,0:T(8,128)(2,1)S(1)} %collective-permute-done.3.others, ...), custom_call_target="tpu_custom_call" | custom-call | flops 1 | bytes 1 | tf_op jit(solution)/shard_map/low_h/pallas_call | solution.py:381
  106.7 8.0 %all-gather.5 = bf16[2560,128]{1,0:T(8,128)(2,1)S(1)} all-gather(bf16[640,128]{1,0:T(8,128)(2,1)S(1)} %low_h.1), channel_id=7, replica_groups=mesh['groups'=2,'fsdp'=4,'tp'=2,'dp'=2] {'tp','dp'}, dimensions={0}, use_global_device_ids=true | all-gather | bytes 819200 | tf_op jit(solution)/shard_map/all_gather | solution.py:400
  114.7 2.2 %terms_b.1.refs_1_ = bf16[4,64,512]{2,1,0:T(8,128)(2,1)} custom-call(s32[4]{0:T(128)S(1)} %copy-done.12, s32[4]{0:T(128)S(1)} %copy-done.13, s32[4]{0:T(128)S(1)} %copy-done.14, bf16[640,2048]{1,0:T(8,128)(2,1)S(1)} %copy-done.1, bf16[4,640,128]{2,1,0:T(8,128)(2,1)S(1)} %bitcast.33), custom_call_target="tpu_custom_call" | custom-call | flops 1 | bytes 1 | tf_op jit(solution)/shard_map/terms_b/pallas_call | solution.py:391
  116.9 2.1 %all-gather.14.cloned.1.call-done = bf16[1536,512]{1,0:T(8,128)(2,1)} async-done(((bf16[384,512]{1,0:T(8,128)(2,1)}), bf16[1536,512]{1,0:T(8,128)(2,1)}) %all-gather.14.cloned.1.call-update) | async-done | bytes 1572880 | tf_op jit(solution)/shard_map/all_gather | solution.py:323
  121.4 7.9 %base.4 = (bf16[640,2048]{1,0:T(8,128)(2,1)}, bf16[640,384]{1,0:T(8,128)(2,1)}) custom-call(s32[4]{0:T(128)S(1)} %copy-done.12, bf16[640,2048]{1,0:T(8,128)(2,1)} %grad.9, bf16[320,2048]{1,0:T(8,128)(2,1)} %collective-permute-done.far_core, bf16[320,2048]{1,0:T(8,128)(2,1)S(1)} %copy-done.4, ...), custom_call_target="tpu_custom_call", output_to_operand_aliasing={{0}: (9, {})} | custom-call | flops 1 | bytes 1 | tf_op jit(solution)/shard_map/base/pallas_call | solution.py:360
  129.3 1.5 collective-permute-start.7
  130.8 27.7 %all-gather.12.cloned.1.call-done = bf16[1536,512]{1,0:T(8,128)(2,1)} async-done(((bf16[384,512]{1,0:T(8,128)(2,1)}), bf16[1536,512]{1,0:T(8,128)(2,1)}) %all-gather.12.cloned.1.call-update) | async-done | bytes 1572880 | tf_op jit(solution)/shard_map/all_gather | solution.py:323
  158.5 7.1 %base.5 = (bf16[640,2048]{1,0:T(8,128)(2,1)}, bf16[640,384]{1,0:T(8,128)(2,1)S(1)}) custom-call(s32[4]{0:T(128)S(1)} %copy-done.12, bf16[640,2048]{1,0:T(8,128)(2,1)} %grad.9, bf16[320,2048]{1,0:T(8,128)(2,1)} %collective-permute-done.far_core, bf16[320,2048]{1,0:T(8,128)(2,1)S(1)} %copy-done.5, ...), custom_call_target="tpu_custom_call", output_to_operand_aliasing={{0}: (9, {})} | custom-call | flops 1 | bytes 1 | tf_op jit(solution)/shard_map/base/pallas_call | solution.py:360
  165.6 1.5 collective-permute-start.6
  167.2 2.6 %sum_terms.1 = f32[2048,128]{1,0:T(8,128)} custom-call(bf16[2048,128]{1,0:T(8,128)(2,1)S(1)} %copy-done.16, bf16[2048,128]{1,0:T(8,128)(2,1)} %collective-permute-done.9.refs_0_, bf16[2048,128]{1,0:T(8,128)(2,1)} %collective-permute-done.11.refs_1_, bf16[2048,128]{1,0:T(8,128)(2,1)} %collective-permute-done.12.refs_2_), custom_call_target="tpu_custom_call" | custom-call | flops 22000001024 | bytes 1 | tf_op jit(solution)/shard_map/sum_terms/pallas_call | solution.py:249
  169.8 1.7 place.3._
  171.5 1.3 place.4._
  172.9 5.6 %collective-permute-done.6.part = bf16[640,384]{1,0:T(8,128)(2,1)S(1)} collective-permute-done((bf16[640,384]{1,0:T(8,128)(2,1)S(1)}, bf16[640,384]{1,0:T(8,128)(2,1)S(1)}, u32[]{:S(2)}, u32[]{:S(2)}) %collective-permute-start.6) | collective-permute-done | bytes 491552 | tf_op jit(solution)/shard_map/ppermute | solution.py:409
  179.9 1.5 convert_bitcast_fusion
  (71 shorter events, 11.5 us)
Async XLA Ops:
  7.2 67.2 %all-gather.10.cloned.1.call-start = ((), (), s32[]{:S(2)}) async-start(), calls=%async_computation.2 | async-start | bytes 2621440 | tf_op jit(solution)/shard_map/all_gather | solution.py:321
  10.5 6.5 %copy-start.17 = (bf16[1,512,64]{1,2,0:T(8,128)(2,1)S(1)}, bf16[1,512,64]{1,2,0:T(8,128)(2,1)}, u32[]{:S(2)}) copy-start(bf16[1,512,64]{1,2,0:T(8,128)(2,1)} %param.13) | copy-start | bytes 196612
  10.5 108.6 %all-gather.14.cloned.1.call-start = ((), (), s32[]{:S(2)}) async-start(), calls=%async_computation.4 | async-start | bytes 1966080 | tf_op jit(solution)/shard_map/all_gather | solution.py:323
  10.5 22.5 %copy-start.12 = (s32[4]{0:T(128)S(1)}, s32[4]{0:T(128)}, u32[]{:S(2)}) copy-start(s32[4]{0:T(128)} %pad_add_fusion.ids) | copy-start | bytes 52
  10.5 22.5 %copy-start.13 = (s32[4]{0:T(128)S(1)}, s32[4]{0:T(128)}, u32[]{:S(2)}) copy-start(s32[4]{0:T(128)} %lengths.7) | copy-start | bytes 52
  10.5 22.5 %copy-start.14 = (s32[4]{0:T(128)S(1)}, s32[4]{0:T(128)}, u32[]{:S(2)}) copy-start(s32[4]{0:T(128)} %slot_job.7) | copy-start | bytes 52
  12.7 145.8 %all-gather.12.cloned.1.call-start = ((), (), s32[]{:S(2)}) async-start(), calls=%async_computation.3 | async-start | bytes 1966080 | tf_op jit(solution)/shard_map/all_gather | solution.py:323
  13.9 38.8 %collective-permute-start = (bf16[320,2048]{1,0:T(8,128)(2,1)}, bf16[320,2048]{1,0:T(8,128)(2,1)}, u32[]{:S(2)}, u32[]{:S(2)}) collective-permute-start(bf16[320,2048]{1,0:T(8,128)(2,1)} %constant_dynamic-slice_fusion.5), channel_id=1, source_target_pairs={{0,16},{16,0},{1,17},{17,1},{2,18},{18,2},{3,19},{19,3},{4,20},{20... | collective-permute-start | bytes 3932168 | tf_op jit(solution)/shard_map/ppermute | solution.py:316
  16.9 163.0 %reduce-scatter.2.cloned.1.call-start = ((), (), s32[]{:S(2)}) async-start(), calls=%async_computation.1 | async-start | bytes 327680 | tf_op jit(solution)/shard_map/reduce_scatter | solution.py:401
  16.9 25.5 %copy-start.6 = (bf16[640,2048]{1,0:T(8,128)(2,1)S(1)}, bf16[640,2048]{1,0:T(8,128)(2,1)}, u32[]{:S(2)}) copy-start(bf16[640,2048]{1,0:T(8,128)(2,1)} %acts.3) | copy-start | bytes 7864324
  48.3 22.4 %collective-permute-start.4 = (bf16[2048,128]{1,0:T(8,128)(2,1)}, bf16[2048,128]{1,0:T(8,128)(2,1)}, u32[]{:S(2)}, u32[]{:S(2)}) collective-permute-start(bf16[2048,128]{1,0:T(8,128)(2,1)} %get-tuple-element.18), channel_id=1, source_target_pairs={{0,4},{12,8},{1,5},{13,9},{2,6},{14,10},{3,7},{15,11},{16,20},{28,... | collective-permute-start | bytes 1572872 | tf_op jit(solution)/shard_map/ppermute | solution.py:77
  52.7 43.5 %collective-permute-start.1 = (bf16[320,2048]{1,0:T(8,128)(2,1)}, bf16[320,2048]{1,0:T(8,128)(2,1)S(1)}, u32[]{:S(2)}, u32[]{:S(2)}) collective-permute-start(bf16[320,2048]{1,0:T(8,128)(2,1)} %collective-permute-done.far_core), channel_id=1, source_target_pairs={{0,1},{1,0},{2,3},{3,2},{4,5},{5,4},{6,7},{7,6},{8,9},{9,8},{10,11... | collective-permute-start | bytes 3932168 | tf_op jit(solution)/shard_map/ppermute | solution.py:317
  52.7 42.0 %collective-permute-start.2 = (bf16[640,512]{1,0:T(8,128)(2,1)S(1)}, bf16[640,512]{1,0:T(8,128)(2,1)S(1)}, u32[]{:S(2)}, u32[]{:S(2)}) collective-permute-start(bf16[640,512]{1,0:T(8,128)(2,1)S(1)} %get-tuple-element.14.masked), channel_id=1, source_target_pairs={{0,16},{16,0},{1,17},{17,1},{2,18},{18,2},{3,19},{19,3},{4,20},{20... | collective-permute-start | bytes 1966088 | tf_op jit(solution)/shard_map/ppermute | solution.py:351
  53.2 30.7 %collective-permute-start.10 = (bf16[2048,128]{1,0:T(8,128)(2,1)S(1)}, bf16[2048,128]{1,0:T(8,128)(2,1)}, u32[]{:S(2)}, u32[]{:S(2)}) collective-permute-start(bf16[2048,128]{1,0:T(8,128)(2,1)S(1)} %get-tuple-element.24), channel_id=1, source_target_pairs={{0,4},{12,8},{1,5},{13,9},{2,6},{14,10},{3,7},{15,11},{16,20},{28,... | collective-permute-start | bytes 1572872 | tf_op jit(solution)/shard_map/ppermute | solution.py:77
  72.9 18.2 %collective-permute-start.5 = (bf16[2048,128]{1,0:T(8,128)(2,1)}, bf16[2048,128]{1,0:T(8,128)(2,1)}, u32[]{:S(2)}, u32[]{:S(2)}) collective-permute-start(bf16[2048,128]{1,0:T(8,128)(2,1)} %add.77), channel_id=1, source_target_pairs={{4,8},{8,4},{5,9},{9,5},{6,10},{10,6},{7,11},{11,7},{20,24},{24,20... | collective-permute-start | bytes 1572872 | tf_op jit(solution)/shard_map/ppermute | solution.py:81
  75.7 20.3 %copy-start.18 = (f32[16,16]{1,0:T(8,128)S(1)}, f32[16,16]{1,0:T(8,128)}, u32[]{:S(2)}) copy-start(f32[16,16]{1,0:T(8,128)} %param.11) | copy-start | bytes 3076
  75.8 28.2 %collective-permute-start.3 = (bf16[3,1024,128]{2,1,0:T(8,128)(2,1)S(1)}, bf16[3,1024,128]{2,1,0:T(8,128)(2,1)S(1)}, u32[]{:S(2)}, u32[]{:S(2)}) collective-permute-start(bf16[3,1024,128]{2,1,0:T(8,128)(2,1)S(1)} %pad_maximum_fusion), channel_id=1, source_target_pairs={{0,16},{16,0},{1,17},{17,1},{2,18},{18,2},{3,19},{19,3},{4,20},{20... | collective-permute-start | bytes 2359304 | tf_op jit(solution)/shard_map/ppermute | solution.py:31
  83.8 81.8 %collective-permute-start.9 = (bf16[2048,128]{1,0:T(8,128)(2,1)}, bf16[2048,128]{1,0:T(8,128)(2,1)}, u32[]{:S(2)}, u32[]{:S(2)}) collective-permute-start(bf16[2048,128]{1,0:T(8,128)(2,1)} %get-tuple-element.17), channel_id=1, source_target_pairs={{0,4},{12,8},{1,5},{13,9},{2,6},{14,10},{3,7},{15,11},{16,20},{28,... | collective-permute-start | bytes 1572872 | tf_op jit(solution)/shard_map/ppermute | solution.py:77
  91.1 76.0 %collective-permute-start.11 = (bf16[2048,128]{1,0:T(8,128)(2,1)}, bf16[2048,128]{1,0:T(8,128)(2,1)}, u32[]{:S(2)}, u32[]{:S(2)}) collective-permute-start(bf16[2048,128]{1,0:T(8,128)(2,1)} %add.79), channel_id=1, source_target_pairs={{4,8},{8,4},{5,9},{9,5},{6,10},{10,6},{7,11},{11,7},{20,24},{24,20... | collective-permute-start | bytes 1572872 | tf_op jit(solution)/shard_map/ppermute | solution.py:81
  94.7 8.8 %copy-start.8 = (bf16[640,512]{1,0:T(8,128)(2,1)}, bf16[640,512]{1,0:T(8,128)(2,1)S(1)}, u32[]{:S(2)}) copy-start(bf16[640,512]{1,0:T(8,128)(2,1)S(1)} %collective-permute-done.2.far_masked) | copy-start | bytes 1966084
  94.7 72.4 %collective-permute-start.12 = (bf16[2048,128]{1,0:T(8,128)(2,1)}, bf16[2048,128]{1,0:T(8,128)(2,1)}, u32[]{:S(2)}, u32[]{:S(2)}) collective-permute-start(bf16[2048,128]{1,0:T(8,128)(2,1)} %add.78.refs_1_), channel_id=1, source_target_pairs={{4,0},{8,12},{5,1},{9,13},{6,2},{10,14},{7,3},{11,15},{20,16},{24,... | collective-permute-start | bytes 1572872 | tf_op jit(solution)/shard_map/ppermute | solution.py:85
  96.2 7.4 %copy-start.3 = (bf16[320,2048]{1,0:T(8,128)(2,1)}, bf16[320,2048]{1,0:T(8,128)(2,1)S(1)}, u32[]{:S(2)}) copy-start(bf16[320,2048]{1,0:T(8,128)(2,1)S(1)} %collective-permute-done.1.far_other) | copy-start | bytes 3932164
  96.2 7.8 %copy-start.2 = (bf16[8192,128]{1,0:T(8,128)(2,1)S(1)}, bf16[8192,128]{1,0:T(8,128)(2,1)}, u32[]{:S(2)}) copy-start(bf16[8192,128]{1,0:T(8,128)(2,1)} %all-gather.10.cloned.1.call-done) | copy-start | bytes 6291460
  96.2 7.8 %copy-start.7 = (bf16[640,2048]{1,0:T(8,128)(2,1)S(1)}, bf16[640,2048]{1,0:T(8,128)(2,1)}, u32[]{:S(2)}) copy-start(bf16[640,2048]{1,0:T(8,128)(2,1)} %acts.3) | copy-start | bytes 7864324
  96.2 7.8 %copy-start.11 = (bf16[1,2048,128]{2,1,0:T(8,128)(2,1)S(1)}, bf16[1,2048,128]{2,1,0:T(8,128)(2,1)}, u32[]{:S(2)}) copy-start(bf16[1,2048,128]{2,1,0:T(8,128)(2,1)} %param.12) | copy-start | bytes 1572868
  103.6 11.2 %copy-start.1 = (bf16[640,2048]{1,0:T(8,128)(2,1)S(1)}, bf16[640,2048]{1,0:T(8,128)(2,1)}, u32[]{:S(2)}) copy-start(bf16[640,2048]{1,0:T(8,128)(2,1)} %grad.9) | copy-start | bytes 7864324
  103.6 66.2 %collective-permute-start.8 = (bf16[640,256]{1,0:T(8,128)(2,1)}, bf16[640,256]{1,0:T(8,128)(2,1)}, u32[]{:S(2)}, u32[]{:S(2)}) collective-permute-start(bf16[640,256]{1,0:T(8,128)(2,1)} %get-tuple-element.21), channel_id=1, source_target_pairs={{0,16},{16,0},{1,17},{17,1},{2,18},{18,2},{3,19},{19,3},{4,20},{20... | collective-permute-start | bytes 983048 | tf_op jit(solution)/shard_map/ppermute | solution.py:405
  121.4 37.1 %copy-start.5 = (bf16[320,2048]{1,0:T(8,128)(2,1)S(1)}, bf16[320,2048]{1,0:T(8,128)(2,1)}, u32[]{:S(2)}) copy-start(bf16[320,2048]{1,0:T(8,128)(2,1)} %copy-done.3) | copy-start | bytes 3932164
  121.4 37.1 %copy-start.10 = (bf16[640,512]{1,0:T(8,128)(2,1)S(1)}, bf16[640,512]{1,0:T(8,128)(2,1)}, u32[]{:S(2)}) copy-start(bf16[640,512]{1,0:T(8,128)(2,1)} %copy-done.8) | copy-start | bytes 1966084
  129.3 42.2 %collective-permute-start.7 = (bf16[640,384]{1,0:T(8,128)(2,1)}, bf16[640,384]{1,0:T(8,128)(2,1)S(1)}, u32[]{:S(2)}, u32[]{:S(2)}) collective-permute-start(bf16[640,384]{1,0:T(8,128)(2,1)} %get-tuple-element.20), channel_id=1, source_target_pairs={{0,16},{16,0},{1,17},{17,1},{2,18},{18,2},{3,19},{19,3},{4,20},{20... | collective-permute-start | bytes 1474568 | tf_op jit(solution)/shard_map/ppermute | solution.py:409
  158.5 8.6 %copy-start.16 = (bf16[2048,128]{1,0:T(8,128)(2,1)S(1)}, bf16[2048,128]{1,0:T(8,128)(2,1)}, u32[]{:S(2)}) copy-start(bf16[2048,128]{1,0:T(8,128)(2,1)} %copy-done.15) | copy-start | bytes 1572868
  165.6 12.9 %collective-permute-start.6 = (bf16[640,384]{1,0:T(8,128)(2,1)S(1)}, bf16[640,384]{1,0:T(8,128)(2,1)S(1)}, u32[]{:S(2)}, u32[]{:S(2)}) collective-permute-start(bf16[640,384]{1,0:T(8,128)(2,1)S(1)} %get-tuple-element.19), channel_id=1, source_target_pairs={{0,16},{16,0},{1,17},{17,1},{2,18},{18,2},{3,19},{19,3},{4,20},{20... | collective-permute-start | bytes 1474568 | tf_op jit(solution)/shard_map/ppermute | solution.py:409
  (4 other events, 8.2 us)
Sparse Core Ops, SparseCore 0:
  10.6 55.2 all-gather.9
  67.5 51.5 all-gather.13
  120.6 37.8 all-gather.11
  160.6 18.4 reduce-scatter.1

commit v3 on v2

--- a/solution.py
+++ b/solution.py
@@ -47,19 +47,22 @@
     half, both = a_own.shape[0] // 2, a_own.shape[1]
     parts = codes.shape[1] // both
 
-    def kernel(ids, a_own, codes, out, held, sems):
+    def kernel(ids, a_own, codes, out, held, sems, out_sems):
         first = pl.multiple_of(ids[1] * half, half)
         copies = [pltpu.make_async_copy(a_own.at[pl.ds(first, half)], held.at[pl.ds(0, half)], sems.at[parts])]
         for k in range(parts):
             src = codes.at[pl.ds(first, size), pl.ds(k * both, both)]
             copies.append(pltpu.make_async_copy(src, held.at[pl.ds(half + k * size, size)], sems.at[k]))
+        places = [pl.ds(half + k * size, size) for k in range(parts)]
+        places = [pl.ds(0, half)] + places
+        stores = [pltpu.make_async_copy(held.at[place], out.at[place], out_sems.at[k]) for k, place in enumerate(places)]
         for copy in copies:
             copy.start()
-        for copy in copies:
+        for copy, store in zip(copies, stores):
             copy.wait()
-        copy = pltpu.make_async_copy(held, out, sems.at[0])
-        copy.start()
-        copy.wait()
+            store.start()
+        for store in stores:
+            store.wait()
 
     shape = (half + parts * size, both)
     return pl.pallas_call(
@@ -67,7 +70,7 @@
         out_shape=jax.ShapeDtypeStruct(shape, a_own.dtype),
         in_specs=[SMEM, HBM, HBM],
         out_specs=HBM,
-        scratch_shapes=[pltpu.VMEM(shape, a_own.dtype), pltpu.SemaphoreType.DMA((parts + 1,))],
+        scratch_shapes=[pltpu.VMEM(shape, a_own.dtype), pltpu.SemaphoreType.DMA((parts + 1,)), pltpu.SemaphoreType.DMA((parts + 1,))],
         cost_estimate=cost(),
         name="pack",
     )(ids, a_own, codes)
@@ -194,40 +197,47 @@
     half, both, cols = out.shape[1] // 2, first_blocks.shape[2], wide // n
     part = far_core.shape[0]
     first = pl.multiple_of(g * half + offset, BLOCK)
-    copies = [
+    near = [
         pltpu.make_async_copy(grad, grads.at[pl.ds(0, rows)], in_sems.at[0]),
+        pltpu.make_async_copy(masked, masks.at[pl.ds(0, rows)], in_sems.at[3]),
+    ]
+    far = [
         pltpu.make_async_copy(far_core, grads.at[pl.ds(pl.multiple_of(rows + dp * part, part), part)], in_sems.at[1]),
         pltpu.make_async_copy(far_other, grads.at[pl.ds(pl.multiple_of(rows + (1 - dp) * part, part), part)], in_sems.at[2]),
-        pltpu.make_async_copy(masked, masks.at[pl.ds(0, rows)], in_sems.at[3]),
         pltpu.make_async_copy(far_masked, masks.at[pl.ds(rows, rows)], in_sems.at[4]),
     ]
+    arriving = []
     for s in range(n):
         if packed:
             for k in range(cols // both):
                 src = first_blocks.at[s, pl.ds(half + k * size, size)]
-                copies.append(pltpu.make_async_copy(src, codes.at[:, pl.ds(s * cols + k * both, both)], sems.at[s, k]))
+                arriving.append(pltpu.make_async_copy(src, codes.at[:, pl.ds(s * cols + k * both, both)], sems.at[s, k]))
         else:
-            copies.append(pltpu.make_async_copy(blocks.at[s], codes.at[:, pl.ds(s * cols, cols)], sems.at[s, 0]))
-        copies.append(pltpu.make_async_copy(first_blocks.at[s, pl.ds(offset, size)], factors.at[:, pl.ds(s * both, both)], sems.at[n, s]))
-    for copy in copies:
+            arriving.append(pltpu.make_async_copy(blocks.at[s], codes.at[:, pl.ds(s * cols, cols)], sems.at[s, 0]))
+        near.append(pltpu.make_async_copy(first_blocks.at[s, pl.ds(offset, size)], factors.at[:, pl.ds(s * both, both)], sems.at[n, s]))
+    for copy in arriving + near + far:
         copy.start()
-    for copy in copies:
+    for copy in arriving:
         copy.wait()
     weight = []
     for b in range(size // BLOCK):
         scale = scale_rows[pl.ds(first // BLOCK + b, 1), :]
         weight.append((codes[b * BLOCK:(b + 1) * BLOCK, :].astype(jnp.float32) * scale).astype(jnp.bfloat16))
     weight = jnp.concatenate(weight, axis=0)
-    for side in range(2):
-        take = slice(side * rows, (side + 1) * rows)
+
+    def product(take):
         total = lax.dot_general(grads[take], weight, NT, preferred_element_type=jnp.float32)
         total += lax.dot_general(masks[take], factors[...], NT, preferred_element_type=jnp.float32)
-        if side == 0:
-            result[...] = total.astype(jnp.bfloat16)
-            keep = pltpu.make_async_copy(result, out.at[:, pl.ds(first, size)], out_sem)
-            keep.start()
-        else:
-            far_out[...] = total.astype(jnp.bfloat16)
+        return total.astype(jnp.bfloat16)
+
+    for copy in near:
+        copy.wait()
+    result[...] = product(slice(0, rows))
+    keep = pltpu.make_async_copy(result, out.at[:, pl.ds(first, size)], out_sem)
+    keep.start()
+    for copy in far:
+        copy.wait()
+    far_out[...] = product(slice(rows, 2 * rows))
     keep.wait()
 
 

time: 189 us -> 188 us (level)
  no operation moved by 1% of the time
where the time goes in v3:
time: 188 us
  waiting for transfers between devices  57.2 us (30%)
  Pallas kernels  43.7 us (23%)
  blocking collectives  31.9 us (17%)
  starting transfers between devices  24.2 us (13%)
  between operations  14.1 us (8%)
  other arithmetic  8.42 us (4%)
  local copies, waits for them, and re-layouts  8.06 us (4%)
    all_gather x2, waiting for transfers between devices, local_chain(): lax.all_gather(lax.dynamic_slice_in_dim(codes, g * half + offset, size, 0...  29.1 us
    pallas_call x3, Pallas kernels, base(): pl.pallas_call(functools.partial(base_kernel, n, offset, size, c == 0), o...  22.7 us
    ppermute x3, waiting for transfers between devices, inward(): return lax.ppermute(x, 'fsdp', [(0, 1), (3, 2)])  22.4 us
    all_gather x1, blocking collectives, local_chain(): b_all = lax.all_gather(adapter_b[0].T, 'fsdp')  16 us
    ppermute x3, starting transfers between devices, inward(): return lax.ppermute(x, 'fsdp', [(0, 1), (3, 2)])  11.7 us
    all_gather x1, blocking collectives, local_chain(): lax.all_gather(h_part, shards)  8 us
    all_gather x1, blocking collectives, local_chain(): lax.all_gather(u_part, shards)  7.9 us
    ppermute x2, waiting for transfers between devices, local_chain(): parts.append(lax.ppermute(far_out, 'groups', SWAP))  5.64 us
  transfers between devices with their start and end apart: 17, of which 5 were waited for; matrix products, arithmetic and copies ran while one was open for 6% of the time, Pallas kernels for 22%

profile of v3, /device:TPU:0, one launch (start us, length us, event | category | flops | bytes accessed | tf_op | source)
XLA Modules:
  0.0 187.7 jit_solution(14802714178585088212)
XLA Ops:
  7.8 2.6 %pack.1 = bf16[2048,128]{1,0:T(8,128)(2,1)} custom-call(s32[4]{0:T(128)} %pad_add_fusion.ids, bf16[2048,128]{1,0:T(8,128)(2,1)} %bitcast.37, bf16[2048,512]{1,0:T(8,128)(2,1)} %codes.1), custom_call_target="tpu_custom_call" | custom-call | flops 1 | bytes 1 | tf_op jit(solution)/shard_map/pack/pallas_call | solution.py:68
  10.5 2.1 %constant_dynamic-slice_fusion.3 = (bf16[384,512]{1,0:T(8,128)(2,1)}, bf16[384,512]{1,0:T(8,128)(2,1)}) fusion(bf16[2048,512]{1,0:T(8,128)(2,1)} %codes.1, s32[]{:T(128)S(6)} %select_n.36, s32[]{:T(128)S(6)} %select_n.35), kind=kLoop, calls=%fused_computation.6 | loop fusion | bytes 1572872 | tf_op jit(solution)/shard_map/dynamic_slice | solution.py:333
  13.9 3.0 %collective-permute-start = (bf16[320,2048]{1,0:T(8,128)(2,1)}, bf16[320,2048]{1,0:T(8,128)(2,1)}, u32[]{:S(2)}, u32[]{:S(2)}) collective-permute-start(bf16[320,2048]{1,0:T(8,128)(2,1)} %constant_dynamic-slice_fusion.5), channel_id=1, source_target_pairs={{0,16},{16,0},{1,17},{17,1},{2,18},{18,2},{3,19},{19,3},{4,20},{20... | collective-permute-start | bytes 3932168 | tf_op jit(solution)/shard_map/ppermute | solution.py:326
  16.9 16.0 %all-gather = bf16[256,512]{1,0:T(8,128)(2,1)S(1)} all-gather(bf16[64,512]{1,0:T(8,128)(2,1)S(1)} %bitcast.43), channel_id=2, replica_groups=mesh['groups'=2,'fsdp'=4,'tp'=2,'dp'=2] {'fsdp'}, dimensions={0}, use_global_device_ids=true | all-gather | bytes 327680 | tf_op jit(solution)/shard_map/all_gather | solution.py:324
  33.0 1.5 low_u.1
  34.5 7.9 %all-gather.1 = bf16[2560,64]{1,0:T(8,128)(2,1)S(1)} all-gather(bf16[640,64]{1,0:T(8,128)(2,1)S(1)} %low_u.1), channel_id=3, replica_groups=mesh['groups'=2,'fsdp'=4,'tp'=2,'dp'=2] {'tp','dp'}, dimensions={0}, use_global_device_ids=true | all-gather | bytes 409600 | tf_op jit(solution)/shard_map/all_gather | solution.py:359
  42.4 5.0 %terms_a.1 = (bf16[640,512]{1,0:T(8,128)(2,1)S(1)}, bf16[2048,128]{1,0:T(8,128)(2,1)}, bf16[2048,128]{1,0:T(8,128)(2,1)S(1)}, bf16[2048,128]{1,0:T(8,128)(2,1)}, bf16[2048,128]{1,0:T(8,128)(2,1)S(1)}) custom-call(s32[4]{0:T(128)S(1)} %copy-done.12, s32[4]{0:T(128)S(1)} %copy-done.13, s32[4]{0:T(128)S(1)} %copy-done.14, bf16[640,2048]{1,0:T(8,128)(2,1)S(1)} %copy-done.6, ...), custom_call_target="tpu_custom_call" | custom-call | flops 1 | bytes 1 | tf_op jit(solution)/shard_map/terms_a/pallas_call | solution.py:350
  48.3 4.3 %collective-permute-start.4 = (bf16[2048,128]{1,0:T(8,128)(2,1)}, bf16[2048,128]{1,0:T(8,128)(2,1)}, u32[]{:S(2)}, u32[]{:S(2)}) collective-permute-start(bf16[2048,128]{1,0:T(8,128)(2,1)} %get-tuple-element.18), channel_id=1, source_target_pairs={{0,4},{12,8},{1,5},{13,9},{2,6},{14,10},{3,7},{15,11},{16,20},{28,... | collective-permute-start | bytes 1572872 | tf_op jit(solution)/shard_map/ppermute | solution.py:80
  53.1 2.1 %collective-permute-start.10 = (bf16[2048,128]{1,0:T(8,128)(2,1)S(1)}, bf16[2048,128]{1,0:T(8,128)(2,1)}, u32[]{:S(2)}, u32[]{:S(2)}) collective-permute-start(bf16[2048,128]{1,0:T(8,128)(2,1)S(1)} %get-tuple-element.24), channel_id=1, source_target_pairs={{0,4},{12,8},{1,5},{13,9},{2,6},{14,10},{3,7},{15,11},{16,20},{28,... | collective-permute-start | bytes 1572872 | tf_op jit(solution)/shard_map/ppermute | solution.py:80
  55.2 15.5 %collective-permute-done.4 = bf16[2048,128]{1,0:T(8,128)(2,1)} collective-permute-done((bf16[2048,128]{1,0:T(8,128)(2,1)}, bf16[2048,128]{1,0:T(8,128)(2,1)}, u32[]{:S(2)}, u32[]{:S(2)}) %collective-permute-start.4) | collective-permute-done | bytes 524320 | tf_op jit(solution)/shard_map/ppermute | solution.py:80
  70.8 2.1 %add.77 = bf16[2048,128]{1,0:T(8,128)(2,1)} add(bf16[2048,128]{1,0:T(8,128)(2,1)} %get-tuple-element.18, bf16[2048,128]{1,0:T(8,128)(2,1)} %collective-permute-done.4) | non-fusion elementwise | flops 262144 | bytes 1572864 | tf_op jit(solution)/shard_map/add | solution.py:363
  72.9 1.5 collective-permute-start.5
  76.9 6.9 %collective-permute-done.10 = bf16[2048,128]{1,0:T(8,128)(2,1)} collective-permute-done((bf16[2048,128]{1,0:T(8,128)(2,1)S(1)}, bf16[2048,128]{1,0:T(8,128)(2,1)}, u32[]{:S(2)}, u32[]{:S(2)}) %collective-permute-start.10) | collective-permute-done | bytes 524320 | tf_op jit(solution)/shard_map/ppermute | solution.py:80
  83.8 5.3 %collective-permute-start.9 = (bf16[2048,128]{1,0:T(8,128)(2,1)}, bf16[2048,128]{1,0:T(8,128)(2,1)}, u32[]{:S(2)}, u32[]{:S(2)}) collective-permute-start(bf16[2048,128]{1,0:T(8,128)(2,1)} %get-tuple-element.17), channel_id=1, source_target_pairs={{0,4},{12,8},{1,5},{13,9},{2,6},{14,10},{3,7},{15,11},{16,20},{28,... | collective-permute-start | bytes 1572872 | tf_op jit(solution)/shard_map/ppermute | solution.py:80
  89.1 2.0 %add.79 = bf16[2048,128]{1,0:T(8,128)(2,1)} add(bf16[2048,128]{1,0:T(8,128)(2,1)S(1)} %get-tuple-element.24, bf16[2048,128]{1,0:T(8,128)(2,1)} %collective-permute-done.10) | non-fusion elementwise | flops 262144 | bytes 1572864 | tf_op jit(solution)/shard_map/add | solution.py:412
  91.1 1.5 collective-permute-start.11
  92.6 2.1 %add.78.refs_1_ = bf16[2048,128]{1,0:T(8,128)(2,1)} add(bf16[2048,128]{1,0:T(8,128)(2,1)} %get-tuple-element.17, bf16[2048,128]{1,0:T(8,128)(2,1)} %collective-permute-done.5) | non-fusion elementwise | flops 262144 | bytes 1572864 | tf_op jit(solution)/shard_map/add | solution.py:416
  96.2 8.2 %base.3 = (bf16[640,2048]{1,0:T(8,128)(2,1)}, bf16[640,256]{1,0:T(8,128)(2,1)}) custom-call(s32[4]{0:T(128)S(1)} %copy-done.12, bf16[640,2048]{1,0:T(8,128)(2,1)} %grad.9, bf16[320,2048]{1,0:T(8,128)(2,1)} %collective-permute-done.far_core, bf16[320,2048]{1,0:T(8,128)(2,1)S(1)} %collective-permute-done.1.far_other, ...), custom_call_target="tpu_custom_call" | custom-call | flops 1 | bytes 1 | tf_op jit(solution)/shard_map/base/pallas_call | solution.py:370
  104.9 2.7 %low_h.1 = bf16[640,128]{1,0:T(8,128)(2,1)S(1)} custom-call(s32[4]{0:T(128)S(1)} %copy-done.12, s32[4]{0:T(128)S(1)} %copy-done.13, s32[4]{0:T(128)S(1)} %copy-done.14, bf16[640,2048]{1,0:T(8,128)(2,1)S(1)} %copy-done.7, bf16[2048,128]{1,0:T(8,128)(2,1)S(1)} %bitcast.38, bf16[3,1024,128]{2,1,0:T(8,128)(2,1)S(1)} %collective-permute-done.3.others, ...), custom_call_target="tpu_custom_call" | custom-call | flops 1 | bytes 1 | tf_op jit(solution)/shard_map/low_h/pallas_call | solution.py:391
  107.6 8.0 %all-gather.5 = bf16[2560,128]{1,0:T(8,128)(2,1)S(1)} all-gather(bf16[640,128]{1,0:T(8,128)(2,1)S(1)} %low_h.1), channel_id=7, replica_groups=mesh['groups'=2,'fsdp'=4,'tp'=2,'dp'=2] {'tp','dp'}, dimensions={0}, use_global_device_ids=true | all-gather | bytes 819200 | tf_op jit(solution)/shard_map/all_gather | solution.py:410
  115.6 2.2 %terms_b.1.refs_1_ = bf16[4,64,512]{2,1,0:T(8,128)(2,1)} custom-call(s32[4]{0:T(128)S(1)} %copy-done.12, s32[4]{0:T(128)S(1)} %copy-done.13, s32[4]{0:T(128)S(1)} %copy-done.14, bf16[640,2048]{1,0:T(8,128)(2,1)S(1)} %copy-done.1, bf16[4,640,128]{2,1,0:T(8,128)(2,1)S(1)} %bitcast.33), custom_call_target="tpu_custom_call" | custom-call | flops 1 | bytes 1 | tf_op jit(solution)/shard_map/terms_b/pallas_call | solution.py:401
  121.4 7.7 %base.4 = (bf16[640,2048]{1,0:T(8,128)(2,1)}, bf16[640,384]{1,0:T(8,128)(2,1)}) custom-call(s32[4]{0:T(128)S(1)} %copy-done.12, bf16[640,2048]{1,0:T(8,128)(2,1)} %grad.9, bf16[320,2048]{1,0:T(8,128)(2,1)} %collective-permute-done.far_core, bf16[320,2048]{1,0:T(8,128)(2,1)S(1)} %copy-done.4, ...), custom_call_target="tpu_custom_call", output_to_operand_aliasing={{0}: (9, {})} | custom-call | flops 1 | bytes 1 | tf_op jit(solution)/shard_map/base/pallas_call | solution.py:370
  129.1 1.5 collective-permute-start.7
  130.6 27.9 %all-gather.12.cloned.1.call-done = bf16[1536,512]{1,0:T(8,128)(2,1)} async-done(((bf16[384,512]{1,0:T(8,128)(2,1)}), bf16[1536,512]{1,0:T(8,128)(2,1)}) %all-gather.12.cloned.1.call-update) | async-done | bytes 1572880 | tf_op jit(solution)/shard_map/all_gather | solution.py:333
  158.5 6.8 %base.5 = (bf16[640,2048]{1,0:T(8,128)(2,1)}, bf16[640,384]{1,0:T(8,128)(2,1)S(1)}) custom-call(s32[4]{0:T(128)S(1)} %copy-done.12, bf16[640,2048]{1,0:T(8,128)(2,1)} %grad.9, bf16[320,2048]{1,0:T(8,128)(2,1)} %collective-permute-done.far_core, bf16[320,2048]{1,0:T(8,128)(2,1)S(1)} %copy-done.5, ...), custom_call_target="tpu_custom_call", output_to_operand_aliasing={{0}: (9, {})} | custom-call | flops 1 | bytes 1 | tf_op jit(solution)/shard_map/base/pallas_call | solution.py:370
  165.4 1.5 collective-permute-start.6
  166.9 2.6 %sum_terms.1 = f32[2048,128]{1,0:T(8,128)} custom-call(bf16[2048,128]{1,0:T(8,128)(2,1)S(1)} %copy-done.16, bf16[2048,128]{1,0:T(8,128)(2,1)} %collective-permute-done.9.refs_0_, bf16[2048,128]{1,0:T(8,128)(2,1)} %collective-permute-done.11.refs_1_, bf16[2048,128]{1,0:T(8,128)(2,1)} %collective-permute-done.12.refs_2_), custom_call_target="tpu_custom_call" | custom-call | flops 22000001024 | bytes 1 | tf_op jit(solution)/shard_map/sum_terms/pallas_call | solution.py:259
  169.6 1.7 place.3._
  171.3 1.3 place.4._
  172.6 5.6 %collective-permute-done.6.part = bf16[640,384]{1,0:T(8,128)(2,1)S(1)} collective-permute-done((bf16[640,384]{1,0:T(8,128)(2,1)S(1)}, bf16[640,384]{1,0:T(8,128)(2,1)S(1)}, u32[]{:S(2)}, u32[]{:S(2)}) %collective-permute-start.6) | collective-permute-done | bytes 491552 | tf_op jit(solution)/shard_map/ppermute | solution.py:419
  178.3 1.3 place.5
  179.7 1.5 convert_bitcast_fusion
  (71 shorter events, 11.4 us)
Async XLA Ops:
  7.2 67.2 %all-gather.10.cloned.1.call-start = ((), (), s32[]{:S(2)}) async-start(), calls=%async_computation.2 | async-start | bytes 2621440 | tf_op jit(solution)/shard_map/all_gather | solution.py:331
  10.4 6.5 %copy-start.17 = (bf16[1,512,64]{1,2,0:T(8,128)(2,1)S(1)}, bf16[1,512,64]{1,2,0:T(8,128)(2,1)}, u32[]{:S(2)}) copy-start(bf16[1,512,64]{1,2,0:T(8,128)(2,1)} %param.13) | copy-start | bytes 196612
  10.4 108.6 %all-gather.14.cloned.1.call-start = ((), (), s32[]{:S(2)}) async-start(), calls=%async_computation.4 | async-start | bytes 1966080 | tf_op jit(solution)/shard_map/all_gather | solution.py:333
  10.5 22.5 %copy-start.12 = (s32[4]{0:T(128)S(1)}, s32[4]{0:T(128)}, u32[]{:S(2)}) copy-start(s32[4]{0:T(128)} %pad_add_fusion.ids) | copy-start | bytes 52
  10.5 22.5 %copy-start.13 = (s32[4]{0:T(128)S(1)}, s32[4]{0:T(128)}, u32[]{:S(2)}) copy-start(s32[4]{0:T(128)} %lengths.7) | copy-start | bytes 52
  10.5 22.5 %copy-start.14 = (s32[4]{0:T(128)S(1)}, s32[4]{0:T(128)}, u32[]{:S(2)}) copy-start(s32[4]{0:T(128)} %slot_job.7) | copy-start | bytes 52
  12.7 145.8 %all-gather.12.cloned.1.call-start = ((), (), s32[]{:S(2)}) async-start(), calls=%async_computation.3 | async-start | bytes 1966080 | tf_op jit(solution)/shard_map/all_gather | solution.py:333
  13.9 38.8 %collective-permute-start = (bf16[320,2048]{1,0:T(8,128)(2,1)}, bf16[320,2048]{1,0:T(8,128)(2,1)}, u32[]{:S(2)}, u32[]{:S(2)}) collective-permute-start(bf16[320,2048]{1,0:T(8,128)(2,1)} %constant_dynamic-slice_fusion.5), channel_id=1, source_target_pairs={{0,16},{16,0},{1,17},{17,1},{2,18},{18,2},{3,19},{19,3},{4,20},{20... | collective-permute-start | bytes 3932168 | tf_op jit(solution)/shard_map/ppermute | solution.py:326
  16.9 162.8 %reduce-scatter.2.cloned.1.call-start = ((), (), s32[]{:S(2)}) async-start(), calls=%async_computation.1 | async-start | bytes 327680 | tf_op jit(solution)/shard_map/reduce_scatter | solution.py:411
  16.9 25.5 %copy-start.6 = (bf16[640,2048]{1,0:T(8,128)(2,1)S(1)}, bf16[640,2048]{1,0:T(8,128)(2,1)}, u32[]{:S(2)}) copy-start(bf16[640,2048]{1,0:T(8,128)(2,1)} %acts.3) | copy-start | bytes 7864324
  48.3 22.4 %collective-permute-start.4 = (bf16[2048,128]{1,0:T(8,128)(2,1)}, bf16[2048,128]{1,0:T(8,128)(2,1)}, u32[]{:S(2)}, u32[]{:S(2)}) collective-permute-start(bf16[2048,128]{1,0:T(8,128)(2,1)} %get-tuple-element.18), channel_id=1, source_target_pairs={{0,4},{12,8},{1,5},{13,9},{2,6},{14,10},{3,7},{15,11},{16,20},{28,... | collective-permute-start | bytes 1572872 | tf_op jit(solution)/shard_map/ppermute | solution.py:80
  52.7 43.5 %collective-permute-start.1 = (bf16[320,2048]{1,0:T(8,128)(2,1)}, bf16[320,2048]{1,0:T(8,128)(2,1)S(1)}, u32[]{:S(2)}, u32[]{:S(2)}) collective-permute-start(bf16[320,2048]{1,0:T(8,128)(2,1)} %collective-permute-done.far_core), channel_id=1, source_target_pairs={{0,1},{1,0},{2,3},{3,2},{4,5},{5,4},{6,7},{7,6},{8,9},{9,8},{10,11... | collective-permute-start | bytes 3932168 | tf_op jit(solution)/shard_map/ppermute | solution.py:327
  52.7 42.0 %collective-permute-start.2 = (bf16[640,512]{1,0:T(8,128)(2,1)S(1)}, bf16[640,512]{1,0:T(8,128)(2,1)S(1)}, u32[]{:S(2)}, u32[]{:S(2)}) collective-permute-start(bf16[640,512]{1,0:T(8,128)(2,1)S(1)} %get-tuple-element.14.masked), channel_id=1, source_target_pairs={{0,16},{16,0},{1,17},{17,1},{2,18},{18,2},{3,19},{19,3},{4,20},{20... | collective-permute-start | bytes 1966088 | tf_op jit(solution)/shard_map/ppermute | solution.py:361
  53.1 30.7 %collective-permute-start.10 = (bf16[2048,128]{1,0:T(8,128)(2,1)S(1)}, bf16[2048,128]{1,0:T(8,128)(2,1)}, u32[]{:S(2)}, u32[]{:S(2)}) collective-permute-start(bf16[2048,128]{1,0:T(8,128)(2,1)S(1)} %get-tuple-element.24), channel_id=1, source_target_pairs={{0,4},{12,8},{1,5},{13,9},{2,6},{14,10},{3,7},{15,11},{16,20},{28,... | collective-permute-start | bytes 1572872 | tf_op jit(solution)/shard_map/ppermute | solution.py:80
  72.9 18.2 %collective-permute-start.5 = (bf16[2048,128]{1,0:T(8,128)(2,1)}, bf16[2048,128]{1,0:T(8,128)(2,1)}, u32[]{:S(2)}, u32[]{:S(2)}) collective-permute-start(bf16[2048,128]{1,0:T(8,128)(2,1)} %add.77), channel_id=1, source_target_pairs={{4,8},{8,4},{5,9},{9,5},{6,10},{10,6},{7,11},{11,7},{20,24},{24,20... | collective-permute-start | bytes 1572872 | tf_op jit(solution)/shard_map/ppermute | solution.py:84
  75.7 20.3 %copy-start.18 = (f32[16,16]{1,0:T(8,128)S(1)}, f32[16,16]{1,0:T(8,128)}, u32[]{:S(2)}) copy-start(f32[16,16]{1,0:T(8,128)} %param.11) | copy-start | bytes 3076
  75.8 29.1 %collective-permute-start.3 = (bf16[3,1024,128]{2,1,0:T(8,128)(2,1)S(1)}, bf16[3,1024,128]{2,1,0:T(8,128)(2,1)S(1)}, u32[]{:S(2)}, u32[]{:S(2)}) collective-permute-start(bf16[3,1024,128]{2,1,0:T(8,128)(2,1)S(1)} %pad_maximum_fusion), channel_id=1, source_target_pairs={{0,16},{16,0},{1,17},{17,1},{2,18},{18,2},{3,19},{19,3},{4,20},{20... | collective-permute-start | bytes 2359304 | tf_op jit(solution)/shard_map/ppermute | solution.py:31
  83.8 81.6 %collective-permute-start.9 = (bf16[2048,128]{1,0:T(8,128)(2,1)}, bf16[2048,128]{1,0:T(8,128)(2,1)}, u32[]{:S(2)}, u32[]{:S(2)}) collective-permute-start(bf16[2048,128]{1,0:T(8,128)(2,1)} %get-tuple-element.17), channel_id=1, source_target_pairs={{0,4},{12,8},{1,5},{13,9},{2,6},{14,10},{3,7},{15,11},{16,20},{28,... | collective-permute-start | bytes 1572872 | tf_op jit(solution)/shard_map/ppermute | solution.py:80
  91.1 75.8 %collective-permute-start.11 = (bf16[2048,128]{1,0:T(8,128)(2,1)}, bf16[2048,128]{1,0:T(8,128)(2,1)}, u32[]{:S(2)}, u32[]{:S(2)}) collective-permute-start(bf16[2048,128]{1,0:T(8,128)(2,1)} %add.79), channel_id=1, source_target_pairs={{4,8},{8,4},{5,9},{9,5},{6,10},{10,6},{7,11},{11,7},{20,24},{24,20... | collective-permute-start | bytes 1572872 | tf_op jit(solution)/shard_map/ppermute | solution.py:84
  94.7 9.7 %copy-start.8 = (bf16[640,512]{1,0:T(8,128)(2,1)}, bf16[640,512]{1,0:T(8,128)(2,1)S(1)}, u32[]{:S(2)}) copy-start(bf16[640,512]{1,0:T(8,128)(2,1)S(1)} %collective-permute-done.2.far_masked) | copy-start | bytes 1966084
  94.7 72.2 %collective-permute-start.12 = (bf16[2048,128]{1,0:T(8,128)(2,1)}, bf16[2048,128]{1,0:T(8,128)(2,1)}, u32[]{:S(2)}, u32[]{:S(2)}) collective-permute-start(bf16[2048,128]{1,0:T(8,128)(2,1)} %add.78.refs_1_), channel_id=1, source_target_pairs={{4,0},{8,12},{5,1},{9,13},{6,2},{10,14},{7,3},{11,15},{20,16},{24,... | collective-permute-start | bytes 1572872 | tf_op jit(solution)/shard_map/ppermute | solution.py:88
  96.2 8.3 %copy-start.3 = (bf16[320,2048]{1,0:T(8,128)(2,1)}, bf16[320,2048]{1,0:T(8,128)(2,1)S(1)}, u32[]{:S(2)}) copy-start(bf16[320,2048]{1,0:T(8,128)(2,1)S(1)} %collective-permute-done.1.far_other) | copy-start | bytes 3932164
  96.2 8.7 %copy-start.2 = (bf16[8192,128]{1,0:T(8,128)(2,1)S(1)}, bf16[8192,128]{1,0:T(8,128)(2,1)}, u32[]{:S(2)}) copy-start(bf16[8192,128]{1,0:T(8,128)(2,1)} %all-gather.10.cloned.1.call-done) | copy-start | bytes 6291460
  96.2 8.7 %copy-start.7 = (bf16[640,2048]{1,0:T(8,128)(2,1)S(1)}, bf16[640,2048]{1,0:T(8,128)(2,1)}, u32[]{:S(2)}) copy-start(bf16[640,2048]{1,0:T(8,128)(2,1)} %acts.3) | copy-start | bytes 7864324
  96.2 8.7 %copy-start.11 = (bf16[1,2048,128]{2,1,0:T(8,128)(2,1)S(1)}, bf16[1,2048,128]{2,1,0:T(8,128)(2,1)}, u32[]{:S(2)}) copy-start(bf16[1,2048,128]{2,1,0:T(8,128)(2,1)} %param.12) | copy-start | bytes 1572868
  104.4 11.2 %copy-start.1 = (bf16[640,2048]{1,0:T(8,128)(2,1)S(1)}, bf16[640,2048]{1,0:T(8,128)(2,1)}, u32[]{:S(2)}) copy-start(bf16[640,2048]{1,0:T(8,128)(2,1)} %grad.9) | copy-start | bytes 7864324
  104.4 65.1 %collective-permute-start.8 = (bf16[640,256]{1,0:T(8,128)(2,1)}, bf16[640,256]{1,0:T(8,128)(2,1)}, u32[]{:S(2)}, u32[]{:S(2)}) collective-permute-start(bf16[640,256]{1,0:T(8,128)(2,1)} %get-tuple-element.21), channel_id=1, source_target_pairs={{0,16},{16,0},{1,17},{17,1},{2,18},{18,2},{3,19},{19,3},{4,20},{20... | collective-permute-start | bytes 983048 | tf_op jit(solution)/shard_map/ppermute | solution.py:415
  121.4 37.1 %copy-start.5 = (bf16[320,2048]{1,0:T(8,128)(2,1)S(1)}, bf16[320,2048]{1,0:T(8,128)(2,1)}, u32[]{:S(2)}) copy-start(bf16[320,2048]{1,0:T(8,128)(2,1)} %copy-done.3) | copy-start | bytes 3932164
  121.4 37.1 %copy-start.10 = (bf16[640,512]{1,0:T(8,128)(2,1)S(1)}, bf16[640,512]{1,0:T(8,128)(2,1)}, u32[]{:S(2)}) copy-start(bf16[640,512]{1,0:T(8,128)(2,1)} %copy-done.8) | copy-start | bytes 1966084
  129.1 42.2 %collective-permute-start.7 = (bf16[640,384]{1,0:T(8,128)(2,1)}, bf16[640,384]{1,0:T(8,128)(2,1)S(1)}, u32[]{:S(2)}, u32[]{:S(2)}) collective-permute-start(bf16[640,384]{1,0:T(8,128)(2,1)} %get-tuple-element.20), channel_id=1, source_target_pairs={{0,16},{16,0},{1,17},{17,1},{2,18},{18,2},{3,19},{19,3},{4,20},{20... | collective-permute-start | bytes 1474568 | tf_op jit(solution)/shard_map/ppermute | solution.py:419
  158.5 8.4 %copy-start.16 = (bf16[2048,128]{1,0:T(8,128)(2,1)S(1)}, bf16[2048,128]{1,0:T(8,128)(2,1)}, u32[]{:S(2)}) copy-start(bf16[2048,128]{1,0:T(8,128)(2,1)} %copy-done.15) | copy-start | bytes 1572868
  165.4 12.9 %collective-permute-start.6 = (bf16[640,384]{1,0:T(8,128)(2,1)S(1)}, bf16[640,384]{1,0:T(8,128)(2,1)S(1)}, u32[]{:S(2)}, u32[]{:S(2)}) collective-permute-start(bf16[640,384]{1,0:T(8,128)(2,1)S(1)} %get-tuple-element.19), channel_id=1, source_target_pairs={{0,16},{16,0},{1,17},{17,1},{2,18},{18,2},{3,19},{19,3},{4,20},{20... | collective-permute-start | bytes 1474568 | tf_op jit(solution)/shard_map/ppermute | solution.py:419
  (4 other events, 8.2 us)
Sparse Core Ops, SparseCore 0:
  10.6 55.2 all-gather.9
  67.4 51.5 all-gather.13
  120.6 37.8 all-gather.11
  160.6 18.4 reduce-scatter.1

commit v4 on v3

--- a/solution.py
+++ b/solution.py
@@ -330,7 +330,7 @@
     offsets = [sum(sizes[:c]) for c in range(len(CUTS))]
     first_blocks = lax.all_gather(pack(a_own, codes, ids, sizes[0]), "fsdp")
     code_blocks = [first_blocks] + [
-        lax.all_gather(lax.dynamic_slice_in_dim(codes, g * half + offset, size, 0), "fsdp") for offset, size in zip(offsets[1:], sizes[1:])
+        lax.all_gather(piece_of(codes, ids, offset, size, (b_all,)), "fsdp") for offset, size in zip(offsets[1:], sizes[1:])
     ]
 
     u_part = pl.pallas_call(

time: 188 us -> 186 us (0.989)
  waiting for transfers between devices: 57.2 us -> 48.2 us
  Pallas kernels: 43.7 us -> 50.5 us
  local copies, waits for them, and re-layouts: 8.06 us -> 5.95 us
    pallas_call x0 -> x2, Pallas kernels: none -> 6.57 us  [piece_of(): pl.pallas_call(kernel, out_shape=jax.ShapeDtypeStruct((size, whole.shape[...]
    all_gather x2, waiting for transfers between devices: 29.1 us -> 22.6 us  [local_chain(): lax.all_gather(piece_of(codes, ids, offset, size, (b_all,)), 'fsdp')]
    ppermute x3, waiting for transfers between devices: 22.4 us -> 16.4 us  [inward(): return lax.ppermute(x, 'fsdp', [(0, 1), (3, 2)])]
    ppermute x1, waiting for transfers between devices: 0.01 us -> 3.42 us  [local_chain(): lax.ppermute(lax.dynamic_slice_in_dim(grad_out, dp * part, part, 0), 'gro...]
    ppermute x3, starting transfers between devices: 11.7 us -> 14 us  [inward(): return lax.ppermute(x, 'fsdp', [(0, 1), (3, 2)])]
    dynamic_slice x1 -> x0, local copies, waits for them, and re-layouts: 2.11 us -> none  [local_chain(): lax.dynamic_slice_in_dim(codes, g * half + offset, size, 0)]
  transfers between devices with their start and end apart: 17 -> 17, of which waited for: 5 -> 5; matrix products, arithmetic and copies ran while one was open for 6% -> 5% of each run, Pallas kernels for 22% -> 26%
where the time goes in v4:
time: 186 us; the launch traced here: 185 us
  Pallas kernels  50.5 us (27%)
  waiting for transfers between devices  48.2 us (26%)
  blocking collectives  32.9 us (18%)
  starting transfers between devices  25.2 us (14%)
  between operations  14.2 us (8%)
  other arithmetic  8.48 us (5%)
  local copies, waits for them, and re-layouts  5.95 us (3%)
    pallas_call x3, Pallas kernels, base(): pl.pallas_call(functools.partial(base_kernel, n, offset, size, c == 0), o...  23 us
    all_gather x2, waiting for transfers between devices, local_chain(): lax.all_gather(piece_of(codes, ids, offset, size, (b_all,)), 'fsdp')  22.6 us
    all_gather x1, blocking collectives, local_chain(): b_all = lax.all_gather(adapter_b[0].T, 'fsdp')  17 us
    ppermute x3, waiting for transfers between devices, inward(): return lax.ppermute(x, 'fsdp', [(0, 1), (3, 2)])  16.4 us
    ppermute x3, starting transfers between devices, inward(): return lax.ppermute(x, 'fsdp', [(0, 1), (3, 2)])  14 us
    all_gather x1, blocking collectives, local_chain(): lax.all_gather(h_part, shards)  8.04 us
    all_gather x1, blocking collectives, local_chain(): lax.all_gather(u_part, shards)  7.89 us
    pallas_call x2, Pallas kernels, piece_of(): pl.pallas_call(kernel, out_shape=jax.ShapeDtypeStruct((size, whole.shape[...  6.57 us
  transfers between devices with their start and end apart: 17, of which 5 were waited for; matrix products, arithmetic and copies ran while one was open for 5% of the time, Pallas kernels for 26%

profile of v4, /device:TPU:0, one launch (start us, length us, event | category | flops | bytes accessed | tf_op | source)
XLA Modules:
  0.0 185.4 jit_solution(8574984992892300912)
XLA Ops:
  7.8 2.5 %pack.1 = bf16[2048,128]{1,0:T(8,128)(2,1)} custom-call(s32[4]{0:T(128)} %pad_add_fusion.ids, bf16[2048,128]{1,0:T(8,128)(2,1)} %bitcast.40, bf16[2048,512]{1,0:T(8,128)(2,1)} %whole.3), custom_call_target="tpu_custom_call" | custom-call | flops 1 | bytes 1 | tf_op jit(solution)/shard_map/pack/pallas_call | solution.py:68
  10.4 17.0 %all-gather = bf16[256,512]{1,0:T(8,128)(2,1)} all-gather(bf16[64,512]{1,0:T(8,128)(2,1)S(1)} %bitcast.45), channel_id=2, replica_groups=mesh['groups'=2,'fsdp'=4,'tp'=2,'dp'=2] {'fsdp'}, dimensions={0}, use_global_device_ids=true | all-gather | bytes 327680 | tf_op jit(solution)/shard_map/all_gather | solution.py:324
  27.3 3.3 %piece.3 = bf16[384,512]{1,0:T(8,128)(2,1)} custom-call(s32[4]{0:T(128)} %pad_add_fusion.ids, bf16[2048,512]{1,0:T(8,128)(2,1)} %whole.3, bf16[4,64,512]{2,1,0:T(8,128)(2,1)} %bitcast.32), custom_call_target="tpu_custom_call" | custom-call | flops 1 | bytes 1 | tf_op jit(solution)/shard_map/piece/pallas_call | solution.py:275
  31.9 1.5 collective-permute-start
  33.4 3.3 %piece.2 = bf16[384,512]{1,0:T(8,128)(2,1)} custom-call(s32[4]{0:T(128)} %pad_add_fusion.ids, bf16[2048,512]{1,0:T(8,128)(2,1)} %whole.3, bf16[4,64,512]{2,1,0:T(8,128)(2,1)} %bitcast.33), custom_call_target="tpu_custom_call" | custom-call | flops 1 | bytes 1 | tf_op jit(solution)/shard_map/piece/pallas_call | solution.py:275
  36.9 1.5 low_u.1
  38.4 7.9 %all-gather.1 = bf16[2560,64]{1,0:T(8,128)(2,1)S(1)} all-gather(bf16[640,64]{1,0:T(8,128)(2,1)S(1)} %low_u.1), channel_id=3, replica_groups=mesh['groups'=2,'fsdp'=4,'tp'=2,'dp'=2] {'tp','dp'}, dimensions={0}, use_global_device_ids=true | all-gather | bytes 409600 | tf_op jit(solution)/shard_map/all_gather | solution.py:359
  46.3 5.0 %terms_a.1 = (bf16[640,512]{1,0:T(8,128)(2,1)S(1)}, bf16[2048,128]{1,0:T(8,128)(2,1)}, bf16[2048,128]{1,0:T(8,128)(2,1)S(1)}, bf16[2048,128]{1,0:T(8,128)(2,1)}, bf16[2048,128]{1,0:T(8,128)(2,1)S(1)}) custom-call(s32[4]{0:T(128)S(1)} %copy-done.13, s32[4]{0:T(128)S(1)} %copy-done.14, s32[4]{0:T(128)S(1)} %copy-done.15, bf16[640,2048]{1,0:T(8,128)(2,1)S(1)} %copy-done.6, ...), custom_call_target="tpu_custom_call" | custom-call | flops 1 | bytes 1 | tf_op jit(solution)/shard_map/terms_a/pallas_call | solution.py:350
  52.2 4.9 %collective-permute-start.4 = (bf16[2048,128]{1,0:T(8,128)(2,1)}, bf16[2048,128]{1,0:T(8,128)(2,1)}, u32[]{:S(2)}, u32[]{:S(2)}) collective-permute-start(bf16[2048,128]{1,0:T(8,128)(2,1)} %get-tuple-element.18), channel_id=1, source_target_pairs={{0,4},{12,8},{1,5},{13,9},{2,6},{14,10},{3,7},{15,11},{16,20},{28,... | collective-permute-start | bytes 1572872 | tf_op jit(solution)/shard_map/ppermute | solution.py:80
  57.1 3.4 %collective-permute-done.far_core = bf16[320,2048]{1,0:T(8,128)(2,1)} collective-permute-done((bf16[320,2048]{1,0:T(8,128)(2,1)}, bf16[320,2048]{1,0:T(8,128)(2,1)}, u32[]{:S(2)}, u32[]{:S(2)}) %collective-permute-start) | collective-permute-done | bytes 1310752 | tf_op jit(solution)/shard_map/ppermute | solution.py:326
  60.5 1.5 collective-permute-start.2
  62.0 3.9 %collective-permute-start.10 = (bf16[2048,128]{1,0:T(8,128)(2,1)S(1)}, bf16[2048,128]{1,0:T(8,128)(2,1)}, u32[]{:S(2)}, u32[]{:S(2)}) collective-permute-start(bf16[2048,128]{1,0:T(8,128)(2,1)S(1)} %get-tuple-element.24), channel_id=1, source_target_pairs={{0,4},{12,8},{1,5},{13,9},{2,6},{14,10},{3,7},{15,11},{16,20},{28,... | collective-permute-start | bytes 1572872 | tf_op jit(solution)/shard_map/ppermute | solution.py:80
  65.9 3.0 %collective-permute-done.4 = bf16[2048,128]{1,0:T(8,128)(2,1)} collective-permute-done((bf16[2048,128]{1,0:T(8,128)(2,1)}, bf16[2048,128]{1,0:T(8,128)(2,1)}, u32[]{:S(2)}, u32[]{:S(2)}) %collective-permute-start.4) | collective-permute-done | bytes 524320 | tf_op jit(solution)/shard_map/ppermute | solution.py:80
  68.8 2.2 %add.57 = bf16[2048,128]{1,0:T(8,128)(2,1)} add(bf16[2048,128]{1,0:T(8,128)(2,1)} %get-tuple-element.18, bf16[2048,128]{1,0:T(8,128)(2,1)} %collective-permute-done.4) | non-fusion elementwise | flops 262144 | bytes 1572864 | tf_op jit(solution)/shard_map/add | solution.py:363
  71.0 1.5 collective-permute-start.5
  75.0 13.5 %collective-permute-done.10 = bf16[2048,128]{1,0:T(8,128)(2,1)} collective-permute-done((bf16[2048,128]{1,0:T(8,128)(2,1)S(1)}, bf16[2048,128]{1,0:T(8,128)(2,1)}, u32[]{:S(2)}, u32[]{:S(2)}) %collective-permute-start.10) | collective-permute-done | bytes 524320 | tf_op jit(solution)/shard_map/ppermute | solution.py:80
  88.4 5.3 %collective-permute-start.9 = (bf16[2048,128]{1,0:T(8,128)(2,1)}, bf16[2048,128]{1,0:T(8,128)(2,1)}, u32[]{:S(2)}, u32[]{:S(2)}) collective-permute-start(bf16[2048,128]{1,0:T(8,128)(2,1)} %get-tuple-element.17), channel_id=1, source_target_pairs={{0,4},{12,8},{1,5},{13,9},{2,6},{14,10},{3,7},{15,11},{16,20},{28,... | collective-permute-start | bytes 1572872 | tf_op jit(solution)/shard_map/ppermute | solution.py:80
  93.7 2.0 %add.59 = bf16[2048,128]{1,0:T(8,128)(2,1)} add(bf16[2048,128]{1,0:T(8,128)(2,1)S(1)} %get-tuple-element.24, bf16[2048,128]{1,0:T(8,128)(2,1)} %collective-permute-done.10) | non-fusion elementwise | flops 262144 | bytes 1572864 | tf_op jit(solution)/shard_map/add | solution.py:412
  95.7 1.5 collective-permute-start.11
  97.2 2.1 %add.58.refs_1_ = bf16[2048,128]{1,0:T(8,128)(2,1)} add(bf16[2048,128]{1,0:T(8,128)(2,1)} %get-tuple-element.17, bf16[2048,128]{1,0:T(8,128)(2,1)} %collective-permute-done.5) | non-fusion elementwise | flops 262144 | bytes 1572864 | tf_op jit(solution)/shard_map/add | solution.py:416
  100.9 8.2 %base.3 = (bf16[640,2048]{1,0:T(8,128)(2,1)}, bf16[640,256]{1,0:T(8,128)(2,1)}) custom-call(s32[4]{0:T(128)S(1)} %copy-done.13, bf16[640,2048]{1,0:T(8,128)(2,1)} %grad.9, bf16[320,2048]{1,0:T(8,128)(2,1)} %collective-permute-done.far_core, bf16[320,2048]{1,0:T(8,128)(2,1)S(1)} %collective-permute-done.1.far_other, ...), custom_call_target="tpu_custom_call" | custom-call | flops 1 | bytes 1 | tf_op jit(solution)/shard_map/base/pallas_call | solution.py:370
  109.7 2.7 %low_h.1 = bf16[640,128]{1,0:T(8,128)(2,1)S(1)} custom-call(s32[4]{0:T(128)S(1)} %copy-done.13, s32[4]{0:T(128)S(1)} %copy-done.14, s32[4]{0:T(128)S(1)} %copy-done.15, bf16[640,2048]{1,0:T(8,128)(2,1)S(1)} %copy-done.7, bf16[2048,128]{1,0:T(8,128)(2,1)S(1)} %bitcast.41, bf16[3,1024,128]{2,1,0:T(8,128)(2,1)S(1)} %collective-permute-done.3.others, ...), custom_call_target="tpu_custom_call" | custom-call | flops 1 | bytes 1 | tf_op jit(solution)/shard_map/low_h/pallas_call | solution.py:391
  112.4 8.0 %all-gather.5 = bf16[2560,128]{1,0:T(8,128)(2,1)S(1)} all-gather(bf16[640,128]{1,0:T(8,128)(2,1)S(1)} %low_h.1), channel_id=7, replica_groups=mesh['groups'=2,'fsdp'=4,'tp'=2,'dp'=2] {'tp','dp'}, dimensions={0}, use_global_device_ids=true | all-gather | bytes 819200 | tf_op jit(solution)/shard_map/all_gather | solution.py:410
  120.4 2.2 %terms_b.1.refs_1_ = bf16[4,64,512]{2,1,0:T(8,128)(2,1)} custom-call(s32[4]{0:T(128)S(1)} %copy-done.13, s32[4]{0:T(128)S(1)} %copy-done.14, s32[4]{0:T(128)S(1)} %copy-done.15, bf16[640,2048]{1,0:T(8,128)(2,1)S(1)} %copy-done.1, bf16[4,640,128]{2,1,0:T(8,128)(2,1)S(1)} %bitcast.36), custom_call_target="tpu_custom_call" | custom-call | flops 1 | bytes 1 | tf_op jit(solution)/shard_map/terms_b/pallas_call | solution.py:401
  125.1 8.0 %base.4 = (bf16[640,2048]{1,0:T(8,128)(2,1)}, bf16[640,384]{1,0:T(8,128)(2,1)}) custom-call(s32[4]{0:T(128)S(1)} %copy-done.13, bf16[640,2048]{1,0:T(8,128)(2,1)} %grad.9, bf16[320,2048]{1,0:T(8,128)(2,1)} %collective-permute-done.far_core, bf16[320,2048]{1,0:T(8,128)(2,1)S(1)} %copy-done.4, ...), custom_call_target="tpu_custom_call", output_to_operand_aliasing={{0}: (9, {})} | custom-call | flops 1 | bytes 1 | tf_op jit(solution)/shard_map/base/pallas_call | solution.py:370
  133.6 22.5 %all-gather.12.cloned.1.call-done = bf16[1536,512]{1,0:T(8,128)(2,1)} async-done(((bf16[384,512]{1,0:T(8,128)(2,1)}), bf16[1536,512]{1,0:T(8,128)(2,1)}) %all-gather.12.cloned.1.call-update) | async-done | bytes 1572880 | tf_op jit(solution)/shard_map/all_gather | solution.py:333
  156.2 6.8 %base.5 = (bf16[640,2048]{1,0:T(8,128)(2,1)}, bf16[640,384]{1,0:T(8,128)(2,1)S(1)}) custom-call(s32[4]{0:T(128)S(1)} %copy-done.13, bf16[640,2048]{1,0:T(8,128)(2,1)} %grad.9, bf16[320,2048]{1,0:T(8,128)(2,1)} %collective-permute-done.far_core, bf16[320,2048]{1,0:T(8,128)(2,1)S(1)} %copy-done.5, ...), custom_call_target="tpu_custom_call", output_to_operand_aliasing={{0}: (9, {})} | custom-call | flops 1 | bytes 1 | tf_op jit(solution)/shard_map/base/pallas_call | solution.py:370
  163.0 1.5 collective-permute-start.6
  164.6 2.6 %sum_terms.1 = f32[2048,128]{1,0:T(8,128)} custom-call(bf16[2048,128]{1,0:T(8,128)(2,1)S(1)} %copy-done.17, bf16[2048,128]{1,0:T(8,128)(2,1)} %collective-permute-done.9.refs_0_, bf16[2048,128]{1,0:T(8,128)(2,1)} %collective-permute-done.11.refs_1_, bf16[2048,128]{1,0:T(8,128)(2,1)} %collective-permute-done.12.refs_2_), custom_call_target="tpu_custom_call" | custom-call | flops 22000001024 | bytes 1 | tf_op jit(solution)/shard_map/sum_terms/pallas_call | solution.py:259
  167.2 1.7 place.3._
  170.3 5.7 %collective-permute-done.6.part = bf16[640,384]{1,0:T(8,128)(2,1)S(1)} collective-permute-done((bf16[640,384]{1,0:T(8,128)(2,1)S(1)}, bf16[640,384]{1,0:T(8,128)(2,1)S(1)}, u32[]{:S(2)}, u32[]{:S(2)}) %collective-permute-start.6) | collective-permute-done | bytes 491552 | tf_op jit(solution)/shard_map/ppermute | solution.py:419
  177.3 1.5 convert_bitcast_fusion
  (74 shorter events, 13.1 us)
Async XLA Ops:
  7.2 65.3 %all-gather.10.cloned.1.call-start = ((), (), s32[]{:S(2)}) async-start(), calls=%async_computation.2 | async-start | bytes 2621440 | tf_op jit(solution)/shard_map/all_gather | solution.py:331
  10.3 20.4 %copy-start = (bf16[640,2048]{1,0:T(8,128)(2,1)S(1)}, bf16[640,2048]{1,0:T(8,128)(2,1)}, u32[]{:S(2)}) copy-start(bf16[640,2048]{1,0:T(8,128)(2,1)} %grad.9) | copy-start | bytes 7864324
  10.3 112.3 %all-gather.14.cloned.1.call-start = ((), (), s32[]{:S(2)}) async-start(), calls=%async_computation.4 | async-start | bytes 1966080 | tf_op jit(solution)/shard_map/all_gather | solution.py:333
  30.7 125.5 %all-gather.12.cloned.1.call-start = ((), (), s32[]{:S(2)}) async-start(), calls=%async_computation.3 | async-start | bytes 1966080 | tf_op jit(solution)/shard_map/all_gather | solution.py:333
  30.7 6.1 %copy-start.11 = (bf16[256,512]{1,0:T(8,128)(2,1)S(1)}, bf16[256,512]{1,0:T(8,128)(2,1)}, u32[]{:S(2)}) copy-start(bf16[256,512]{1,0:T(8,128)(2,1)} %all-gather) | copy-start | bytes 786436
  30.7 6.1 %copy-start.13 = (s32[4]{0:T(128)S(1)}, s32[4]{0:T(128)}, u32[]{:S(2)}) copy-start(s32[4]{0:T(128)} %pad_add_fusion.ids) | copy-start | bytes 52
  30.7 6.1 %copy-start.14 = (s32[4]{0:T(128)S(1)}, s32[4]{0:T(128)}, u32[]{:S(2)}) copy-start(s32[4]{0:T(128)} %lengths.7) | copy-start | bytes 52
  31.9 28.6 %collective-permute-start = (bf16[320,2048]{1,0:T(8,128)(2,1)}, bf16[320,2048]{1,0:T(8,128)(2,1)}, u32[]{:S(2)}, u32[]{:S(2)}) collective-permute-start(bf16[320,2048]{1,0:T(8,128)(2,1)} %constant_dynamic-slice_fusion.3), channel_id=1, source_target_pairs={{0,16},{16,0},{1,17},{17,1},{2,18},{18,2},{3,19},{19,3},{4,20},{20... | collective-permute-start | bytes 3932168 | tf_op jit(solution)/shard_map/ppermute | solution.py:326
  36.8 140.6 %reduce-scatter.2.cloned.1.call-start = ((), (), s32[]{:S(2)}) async-start(), calls=%async_computation.1 | async-start | bytes 327680 | tf_op jit(solution)/shard_map/reduce_scatter | solution.py:411
  36.8 9.4 %copy-start.6 = (bf16[640,2048]{1,0:T(8,128)(2,1)S(1)}, bf16[640,2048]{1,0:T(8,128)(2,1)}, u32[]{:S(2)}) copy-start(bf16[640,2048]{1,0:T(8,128)(2,1)} %acts.3) | copy-start | bytes 7864324
  52.2 16.6 %collective-permute-start.4 = (bf16[2048,128]{1,0:T(8,128)(2,1)}, bf16[2048,128]{1,0:T(8,128)(2,1)}, u32[]{:S(2)}, u32[]{:S(2)}) collective-permute-start(bf16[2048,128]{1,0:T(8,128)(2,1)} %get-tuple-element.18), channel_id=1, source_target_pairs={{0,4},{12,8},{1,5},{13,9},{2,6},{14,10},{3,7},{15,11},{16,20},{28,... | collective-permute-start | bytes 1572872 | tf_op jit(solution)/shard_map/ppermute | solution.py:80
  60.5 40.3 %collective-permute-start.1 = (bf16[320,2048]{1,0:T(8,128)(2,1)}, bf16[320,2048]{1,0:T(8,128)(2,1)S(1)}, u32[]{:S(2)}, u32[]{:S(2)}) collective-permute-start(bf16[320,2048]{1,0:T(8,128)(2,1)} %collective-permute-done.far_core), channel_id=1, source_target_pairs={{0,1},{1,0},{2,3},{3,2},{4,5},{5,4},{6,7},{7,6},{8,9},{9,8},{10,11... | collective-permute-start | bytes 3932168 | tf_op jit(solution)/shard_map/ppermute | solution.py:327
  60.5 38.9 %collective-permute-start.2 = (bf16[640,512]{1,0:T(8,128)(2,1)S(1)}, bf16[640,512]{1,0:T(8,128)(2,1)S(1)}, u32[]{:S(2)}, u32[]{:S(2)}) collective-permute-start(bf16[640,512]{1,0:T(8,128)(2,1)S(1)} %get-tuple-element.14.masked), channel_id=1, source_target_pairs={{0,16},{16,0},{1,17},{17,1},{2,18},{18,2},{3,19},{19,3},{4,20},{20... | collective-permute-start | bytes 1966088 | tf_op jit(solution)/shard_map/ppermute | solution.py:361
  62.0 26.4 %collective-permute-start.10 = (bf16[2048,128]{1,0:T(8,128)(2,1)S(1)}, bf16[2048,128]{1,0:T(8,128)(2,1)}, u32[]{:S(2)}, u32[]{:S(2)}) collective-permute-start(bf16[2048,128]{1,0:T(8,128)(2,1)S(1)} %get-tuple-element.24), channel_id=1, source_target_pairs={{0,4},{12,8},{1,5},{13,9},{2,6},{14,10},{3,7},{15,11},{16,20},{28,... | collective-permute-start | bytes 1572872 | tf_op jit(solution)/shard_map/ppermute | solution.py:80
  71.0 24.7 %collective-permute-start.5 = (bf16[2048,128]{1,0:T(8,128)(2,1)}, bf16[2048,128]{1,0:T(8,128)(2,1)}, u32[]{:S(2)}, u32[]{:S(2)}) collective-permute-start(bf16[2048,128]{1,0:T(8,128)(2,1)} %add.57), channel_id=1, source_target_pairs={{4,8},{8,4},{5,9},{9,5},{6,10},{10,6},{7,11},{11,7},{20,24},{24,20... | collective-permute-start | bytes 1572872 | tf_op jit(solution)/shard_map/ppermute | solution.py:84
  73.8 26.8 %copy-start.19 = (f32[16,16]{1,0:T(8,128)S(1)}, f32[16,16]{1,0:T(8,128)}, u32[]{:S(2)}) copy-start(f32[16,16]{1,0:T(8,128)} %param.11) | copy-start | bytes 3076
  73.9 35.8 %collective-permute-start.3 = (bf16[3,1024,128]{2,1,0:T(8,128)(2,1)S(1)}, bf16[3,1024,128]{2,1,0:T(8,128)(2,1)S(1)}, u32[]{:S(2)}, u32[]{:S(2)}) collective-permute-start(bf16[3,1024,128]{2,1,0:T(8,128)(2,1)S(1)} %pad_maximum_fusion), channel_id=1, source_target_pairs={{0,16},{16,0},{1,17},{17,1},{2,18},{18,2},{3,19},{19,3},{4,20},{20... | collective-permute-start | bytes 2359304 | tf_op jit(solution)/shard_map/ppermute | solution.py:31
  88.4 74.6 %collective-permute-start.9 = (bf16[2048,128]{1,0:T(8,128)(2,1)}, bf16[2048,128]{1,0:T(8,128)(2,1)}, u32[]{:S(2)}, u32[]{:S(2)}) collective-permute-start(bf16[2048,128]{1,0:T(8,128)(2,1)} %get-tuple-element.17), channel_id=1, source_target_pairs={{0,4},{12,8},{1,5},{13,9},{2,6},{14,10},{3,7},{15,11},{16,20},{28,... | collective-permute-start | bytes 1572872 | tf_op jit(solution)/shard_map/ppermute | solution.py:80
  95.7 68.8 %collective-permute-start.11 = (bf16[2048,128]{1,0:T(8,128)(2,1)}, bf16[2048,128]{1,0:T(8,128)(2,1)}, u32[]{:S(2)}, u32[]{:S(2)}) collective-permute-start(bf16[2048,128]{1,0:T(8,128)(2,1)} %add.59), channel_id=1, source_target_pairs={{4,8},{8,4},{5,9},{9,5},{6,10},{10,6},{7,11},{11,7},{20,24},{24,20... | collective-permute-start | bytes 1572872 | tf_op jit(solution)/shard_map/ppermute | solution.py:84
  99.4 9.7 %copy-start.8 = (bf16[640,512]{1,0:T(8,128)(2,1)}, bf16[640,512]{1,0:T(8,128)(2,1)S(1)}, u32[]{:S(2)}) copy-start(bf16[640,512]{1,0:T(8,128)(2,1)S(1)} %collective-permute-done.2.far_masked) | copy-start | bytes 1966084
  99.4 65.2 %collective-permute-start.12 = (bf16[2048,128]{1,0:T(8,128)(2,1)}, bf16[2048,128]{1,0:T(8,128)(2,1)}, u32[]{:S(2)}, u32[]{:S(2)}) collective-permute-start(bf16[2048,128]{1,0:T(8,128)(2,1)} %add.58.refs_1_), channel_id=1, source_target_pairs={{4,0},{8,12},{5,1},{9,13},{6,2},{10,14},{7,3},{11,15},{20,16},{24,... | collective-permute-start | bytes 1572872 | tf_op jit(solution)/shard_map/ppermute | solution.py:88
  100.8 8.2 %copy-start.3 = (bf16[320,2048]{1,0:T(8,128)(2,1)}, bf16[320,2048]{1,0:T(8,128)(2,1)S(1)}, u32[]{:S(2)}) copy-start(bf16[320,2048]{1,0:T(8,128)(2,1)S(1)} %collective-permute-done.1.far_other) | copy-start | bytes 3932164
  100.8 8.9 %copy-start.2 = (bf16[8192,128]{1,0:T(8,128)(2,1)S(1)}, bf16[8192,128]{1,0:T(8,128)(2,1)}, u32[]{:S(2)}) copy-start(bf16[8192,128]{1,0:T(8,128)(2,1)} %all-gather.10.cloned.1.call-done) | copy-start | bytes 6291460
  100.8 8.9 %copy-start.7 = (bf16[640,2048]{1,0:T(8,128)(2,1)S(1)}, bf16[640,2048]{1,0:T(8,128)(2,1)}, u32[]{:S(2)}) copy-start(bf16[640,2048]{1,0:T(8,128)(2,1)} %acts.3) | copy-start | bytes 7864324
  100.8 8.9 %copy-start.12 = (bf16[1,2048,128]{2,1,0:T(8,128)(2,1)S(1)}, bf16[1,2048,128]{2,1,0:T(8,128)(2,1)}, u32[]{:S(2)}) copy-start(bf16[1,2048,128]{2,1,0:T(8,128)(2,1)} %param.12) | copy-start | bytes 1572868
  109.1 11.4 %copy-start.1 = (bf16[640,2048]{1,0:T(8,128)(2,1)S(1)}, bf16[640,2048]{1,0:T(8,128)(2,1)}, u32[]{:S(2)}) copy-start(bf16[640,2048]{1,0:T(8,128)(2,1)} %grad.9) | copy-start | bytes 7864324
  109.1 58.1 %collective-permute-start.8 = (bf16[640,256]{1,0:T(8,128)(2,1)}, bf16[640,256]{1,0:T(8,128)(2,1)}, u32[]{:S(2)}, u32[]{:S(2)}) collective-permute-start(bf16[640,256]{1,0:T(8,128)(2,1)} %get-tuple-element.21), channel_id=1, source_target_pairs={{0,16},{16,0},{1,17},{17,1},{2,18},{18,2},{3,19},{19,3},{4,20},{20... | collective-permute-start | bytes 983048 | tf_op jit(solution)/shard_map/ppermute | solution.py:415
  125.1 31.1 %copy-start.5 = (bf16[320,2048]{1,0:T(8,128)(2,1)S(1)}, bf16[320,2048]{1,0:T(8,128)(2,1)}, u32[]{:S(2)}) copy-start(bf16[320,2048]{1,0:T(8,128)(2,1)} %copy-done.3) | copy-start | bytes 3932164
  125.1 31.1 %copy-start.10 = (bf16[640,512]{1,0:T(8,128)(2,1)S(1)}, bf16[640,512]{1,0:T(8,128)(2,1)}, u32[]{:S(2)}) copy-start(bf16[640,512]{1,0:T(8,128)(2,1)} %copy-done.8) | copy-start | bytes 1966084
  133.0 35.9 %collective-permute-start.7 = (bf16[640,384]{1,0:T(8,128)(2,1)}, bf16[640,384]{1,0:T(8,128)(2,1)S(1)}, u32[]{:S(2)}, u32[]{:S(2)}) collective-permute-start(bf16[640,384]{1,0:T(8,128)(2,1)} %get-tuple-element.20), channel_id=1, source_target_pairs={{0,16},{16,0},{1,17},{17,1},{2,18},{18,2},{3,19},{19,3},{4,20},{20... | collective-permute-start | bytes 1474568 | tf_op jit(solution)/shard_map/ppermute | solution.py:419
  156.2 8.4 %copy-start.17 = (bf16[2048,128]{1,0:T(8,128)(2,1)S(1)}, bf16[2048,128]{1,0:T(8,128)(2,1)}, u32[]{:S(2)}) copy-start(bf16[2048,128]{1,0:T(8,128)(2,1)} %copy-done.16) | copy-start | bytes 1572868
  163.0 12.9 %collective-permute-start.6 = (bf16[640,384]{1,0:T(8,128)(2,1)S(1)}, bf16[640,384]{1,0:T(8,128)(2,1)S(1)}, u32[]{:S(2)}, u32[]{:S(2)}) collective-permute-start(bf16[640,384]{1,0:T(8,128)(2,1)S(1)} %get-tuple-element.19), channel_id=1, source_target_pairs={{0,16},{16,0},{1,17},{17,1},{2,18},{18,2},{3,19},{19,3},{4,20},{20... | collective-permute-start | bytes 1474568 | tf_op jit(solution)/shard_map/ppermute | solution.py:419
  (5 other events, 12.5 us)
Sparse Core Ops, SparseCore 0:
  10.4 49.3 all-gather.9
  61.4 54.6 all-gather.13
  117.7 38.4 all-gather.11
  158.3 18.5 reduce-scatter.1
